TPU v7x, 32 devices: a whole 2x2x4 slice. The times are simulated.
32 devices in a mesh: seq: 8 (over z, x), tensor: 4 (over y, core).
Axes of the slice: x: 2, y: 2, z: 4, core: 2. Of those that a mesh axis runs over, the one named last changes fastest.
Arguments:
- inputs: bfloat16 [4096, 1024], P(('seq', 'tensor')), may hold values from -6 to 6
- cotangent: bfloat16 [4096, 1024], P(('seq', 'tensor')), may hold values from -6 to 6
- seq_lengths: int32 [8], replicated, may hold values from 1 to 3584, as said below
- norm_gains: float32 [4, 1024], replicated, may hold values from 0.5 to 1.5
- query_one: bfloat16 [1024, 256], P(None, 'tensor'), may hold values from -0.1875 to 0.1875
- key_one: bfloat16 [1024, 256], P(None, 'tensor'), may hold values from -0.1875 to 0.1875
- value_one: bfloat16 [1024, 1024], P(None, 'tensor'), may hold values from -0.1875 to 0.1875
- out_one: bfloat16 [1024, 1024], P('tensor'), may hold values from -1.5 to 1.5
- gate_one: bfloat16 [1024, 2752], P(None, 'tensor'), may hold values from -0.1875 to 0.1875
- up_one: bfloat16 [1024, 2752], P(None, 'tensor'), may hold values from -0.1875 to 0.1875
- down_one: bfloat16 [2752, 1024], P('tensor'), may hold values from -0.109375 to 0.109375
- query_two: bfloat16 [1024, 1024], P(None, 'tensor'), may hold values from -0.1875 to 0.1875
- key_two: bfloat16 [1024, 1024], P(None, 'tensor'), may hold values from -0.1875 to 0.1875
- value_two: bfloat16 [1024, 1024], P(None, 'tensor'), may hold values from -0.1875 to 0.1875
- out_two: bfloat16 [1024, 1024], P('tensor'), may hold values from -0.5 to 0.5
- gate_two: bfloat16 [1024, 2752], P(None, 'tensor'), may hold values from -0.1875 to 0.1875
- up_two: bfloat16 [1024, 2752], P(None, 'tensor'), may hold values from -0.1875 to 0.1875
- down_two: bfloat16 [2752, 1024], P('tensor'), may hold values from -0.109375 to 0.109375
Outputs:
- block_output: bfloat16 [4096, 1024], P(('seq', 'tensor'))
- input_grad: float32 [4096, 1024], P(('seq', 'tensor'))
- gain_grads: float32 [4, 1024], P(None, ('seq', 'tensor'))
- query_one_grad: float32 [1024, 256], P('seq', 'tensor')
- key_one_grad: float32 [1024, 256], P('seq', 'tensor')
- value_one_grad: float32 [1024, 1024], P('seq', 'tensor')
- out_one_grad: float32 [1024, 1024], P('tensor', 'seq')
- gate_one_grad: float32 [1024, 2752], P('seq', 'tensor')
- up_one_grad: float32 [1024, 2752], P('seq', 'tensor')
- down_one_grad: float32 [2752, 1024], P('tensor', 'seq')
- query_two_grad: float32 [1024, 1024], P('seq', 'tensor')
- key_two_grad: float32 [1024, 1024], P('seq', 'tensor')
- value_two_grad: float32 [1024, 1024], P('seq', 'tensor')
- out_two_grad: float32 [1024, 1024], P('tensor', 'seq')
- gate_two_grad: float32 [1024, 2752], P('seq', 'tensor')
- up_two_grad: float32 [1024, 2752], P('seq', 'tensor')
- down_two_grad: float32 [2752, 1024], P('tensor', 'seq')
Inputs may be any that keep to these rules, and one draw needn't show every extreme that they name: `seq_lengths`: 8 sequences fill all 4096 tokens in order; the longest, never the first or the last, holds 3584 tokens and the others together 512.
All inputs are finite; a program needn't handle non-finite values.
Results may differ from a plain program's by a relative error of at most 0.035.
Values may be sent and summed in bfloat16 or wider, within the bound.
A program may use at most 192 MiB of HBM per device.

v0:
```python
import math

import jax
import jax.numpy as jnp
from jax import lax
from jax.sharding import PartitionSpec as P

FEAT = 16
HEAD = 64
WINDOW = 64


EPS = 1e-05
HIGH = lax.Precision.HIGHEST
ROOT_HALF = 0.5**0.5
FLOOR_SCORE = -1e30
SAME_DIMS = (((0,), (0,)), ((), ()))
BACK_DIMS = (((1,), (1,)), ((), ()))


def shortened(array):
    return jax.tree.map(lambda a: a.astype(jnp.bfloat16) if a.dtype == jnp.float32 else a, array)


def from_behind(block, axis, distance):
    devices = range(lax.axis_size(axis))
    route = [(i - distance, i) for i in devices if i - distance in devices]
    return lax.ppermute(block, axis, route)


def plain(left, right):
    return jnp.dot(left, right, preferred_element_type=jnp.float32)


def inner(left, right):
    return lax.dot_general(left, right, SAME_DIMS, preferred_element_type=jnp.float32)


def through(left, right):
    return lax.dot_general(left, right, BACK_DIMS, preferred_element_type=jnp.float32)


def features(values):
    outer = (values[..., :, None] * values[..., None, :]).reshape(
        values.shape[:-1] + (values.shape[-1] * values.shape[-1],)
    )
    ones = jnp.ones(values.shape[:-1] + (1,), jnp.float32)
    return jnp.concatenate([ones, values, outer * ROOT_HALF], axis=-1)


def segment_ids(seq_lengths, first, count):
    ends = jnp.cumsum(seq_lengths)
    positions = first + lax.iota(jnp.int32, count)
    return jnp.sum((positions[:, None] >= ends[None, :]).astype(jnp.int32), axis=1)


def start_flags(seq_lengths, stretch, n_seq):
    ends = jnp.cumsum(seq_lengths)
    owners = (ends - seq_lengths) // stretch
    devices = lax.iota(jnp.int32, n_seq)
    return jnp.max((owners[None, :] == devices[:, None]).astype(jnp.float32), axis=1)


def reach(flags, position, n_seq, forward):
    before = jnp.concatenate([jnp.zeros((1,), jnp.float32), jnp.cumsum(flags)])
    others = lax.iota(jnp.int32, n_seq)
    if forward:
        mine = lax.dynamic_index_in_dim(before, position, keepdims=False)
        clear = mine - before[1:] == 0.0
        return ((others < position) & clear).astype(jnp.float32)
    mine = lax.dynamic_index_in_dim(before, position + 1, keepdims=False)
    clear = before[:-1] - mine == 0.0
    return ((others > position) & clear).astype(jnp.float32)


def spread(part):
    return lax.all_gather(part, "tensor", axis=0, tiled=True)


def collect(product, rows):
    return lax.psum_scatter(
        product(jnp.int32(0), rows * lax.axis_size("tensor")).astype(jnp.bfloat16),
        "tensor",
        scatter_dimension=0,
        tiled=True,
    ).astype(jnp.float32)


def pass_states(state, norm_sum, place, backward):
    seq_lengths, stretch_start, stretch, position, n_seq, flags = place
    weights = reach(flags, position, n_seq, not backward)
    feats = state.shape[0]

    def absorb(carry, pieces):
        count = pieces[0].shape[0] // feats
        return (
            carry[0]
            + jnp.einsum("k,kfx->fx", weights, pieces[0].reshape(count, feats, -1), precision=HIGH),
            carry[1]
            + jnp.einsum("k,kfx->fx", weights, pieces[1].reshape(count, feats, -1), precision=HIGH),
        )

    empty = (jnp.zeros_like(state), jnp.zeros_like(norm_sum))
    if backward:
        return absorb(
            empty,
            (
                lax.all_gather(shortened(state), "seq", axis=0, tiled=True),
                lax.all_gather(shortened(norm_sum), "seq", axis=0, tiled=True),
            ),
        )
    return absorb(
        empty,
        (
            lax.all_gather(state.astype(jnp.bfloat16), "seq", axis=0, tiled=True).astype(
                jnp.float32
            ),
            lax.all_gather(norm_sum.astype(jnp.bfloat16), "seq", axis=0, tiled=True).astype(
                jnp.float32
            ),
        ),
    )


def taylor_pieces(query, key, value, place):
    seq_lengths, stretch_start, stretch, position, n_seq, flags = place
    heads = query.shape[1] // FEAT
    query_half = query.astype(jnp.float32).reshape(stretch, heads, FEAT) * 0.5
    key_half = key.astype(jnp.float32).reshape(stretch, heads, FEAT) * 0.5
    value_full = value.astype(jnp.float32).reshape(stretch, heads, HEAD)
    segs = segment_ids(seq_lengths, stretch_start, stretch)
    order = lax.iota(jnp.int32, stretch)
    allowed = (order[:, None] >= order[None, :]) & (segs[:, None] == segs[None, :])
    inner_qk = jnp.einsum("ihf,jhf->hij", query_half, key_half, precision=HIGH)
    score = jnp.where(allowed[None], 1.0 + inner_qk + 0.5 * inner_qk * inner_qk, 0.0)
    return (heads, query_half, key_half, value_full, segs, allowed, inner_qk, score)


def taylor_forward(query, key, value, place):
    seq_lengths, stretch_start, stretch, position, n_seq, flags = place
    heads, query_half, key_half, value_full, segs, allowed, inner_qk, score = taylor_pieces(
        query, key, value, place
    )
    previous = segment_ids(seq_lengths, stretch_start - 1, 1)[0]
    carried = (segs == previous).astype(jnp.float32)
    tail = (segs == segs[-1]).astype(jnp.float32)
    query_feat = features(query_half)
    key_feat = features(key_half)
    feats = key_feat.shape[-1]
    local_state = jnp.einsum(
        "jhf,jhe->fhe", key_feat * tail[:, None, None], value_full, precision=HIGH
    ).reshape(feats, heads * HEAD)
    local_norm = jnp.einsum("jhf,j->fh", key_feat, tail, precision=HIGH)
    numerator = jnp.einsum("hij,jhe->ihe", score, value_full, precision=HIGH)
    totals = jnp.sum(score, axis=2).T
    state_in, norm_in = pass_states(local_state, local_norm, place, False)
    state_three = state_in.reshape(feats, heads, HEAD)
    numerator = numerator + carried[:, None, None] * jnp.einsum(
        "ihf,fhe->ihe", query_feat, state_three, precision=HIGH
    )
    totals = totals + carried[:, None] * jnp.einsum(
        "ihf,fh->ih", query_feat, norm_in, precision=HIGH
    )
    mixed = numerator / totals[:, :, None]
    saved = (totals, mixed, query_feat, key_feat, state_in, norm_in, carried, tail)
    return (mixed.reshape(stretch, heads * HEAD), saved)


def taylor_backward(d_mixed, query, key, value, saved, place):
    seq_lengths, stretch_start, stretch, position, n_seq, flags = place
    totals, mixed, query_feat, key_feat, state_in, norm_in, carried, tail = saved
    heads, query_half, key_half, value_full, segs, allowed, inner_qk, score = taylor_pieces(
        query, key, value, place
    )
    feats = key_feat.shape[-1]
    d_out = d_mixed.astype(jnp.float32).reshape(stretch, heads, HEAD)
    d_numer = d_out / totals[:, :, None]
    d_total = -jnp.sum(d_out * mixed, axis=2) / totals
    d_score = (
        jnp.einsum("ihe,jhe->hij", d_numer, value_full, precision=HIGH) + d_total.T[:, :, None]
    )
    d_score = jnp.where(allowed[None], d_score, 0.0)
    d_value = jnp.einsum("hij,ihe->jhe", score, d_numer, precision=HIGH)
    d_inner = d_score * (1.0 + inner_qk)
    d_query = jnp.einsum("hij,jhf->ihf", d_inner, key_half, precision=HIGH)
    d_key = jnp.einsum("hij,ihf->jhf", d_inner, query_half, precision=HIGH)
    state_three = state_in.reshape(feats, heads, HEAD)
    carried_feat = query_feat * carried[:, None, None]
    d_qfeat = carried[:, None, None] * (
        jnp.einsum("ihe,fhe->ihf", d_numer, state_three, precision=HIGH)
        + d_total[:, :, None] * norm_in.T[None]
    )
    d_state = jnp.einsum("ihf,ihe->fhe", carried_feat, d_numer, precision=HIGH).reshape(
        feats, heads * HEAD
    )
    d_norm = jnp.einsum("ihf,ih->fh", carried_feat, d_total, precision=HIGH)
    grad_state, grad_norm = pass_states(d_state, d_norm, place, True)
    grad_three = grad_state.reshape(feats, heads, HEAD)
    d_kfeat = tail[:, None, None] * (
        jnp.einsum("fhe,jhe->jhf", grad_three, value_full, precision=HIGH) + grad_norm.T[None]
    )
    d_value = d_value + tail[:, None, None] * jnp.einsum(
        "jhf,fhe->jhe", key_feat, grad_three, precision=HIGH
    )
    d_query = d_query + jax.vjp(features, query_half)[1](d_qfeat)[0]
    d_key = d_key + jax.vjp(features, key_half)[1](d_kfeat)[0]
    return (
        (0.5 * d_query).reshape(stretch, heads * FEAT).astype(jnp.bfloat16),
        (0.5 * d_key).reshape(stretch, heads * FEAT).astype(jnp.bfloat16),
        d_value.reshape(stretch, heads * HEAD).astype(jnp.bfloat16),
    )


def window_allowed(key_segs, stretch_start, first, block, span):
    query_row = first + lax.iota(jnp.int32, block)[:, None] + span
    key_col = first + lax.iota(jnp.int32, block + span)[None, :]
    query_seg = key_segs[first + span : first + span + block]
    return (
        (key_col <= query_row)
        & (key_col > query_row - WINDOW)
        & (key_segs[None, :] == query_seg[:, None])
        & (stretch_start - span + key_col >= 0)
    )


def window_forward(query, key, value, place):
    seq_lengths, stretch_start, stretch, position, n_seq, flags = place
    span = WINDOW - 1
    heads = query.shape[1] // HEAD
    prev_key, prev_value = from_behind((key[stretch - span :], value[stretch - span :]), "seq", 1)
    keys = jnp.concatenate([prev_key, key]).reshape(stretch + span, heads, HEAD)
    values = jnp.concatenate([prev_value, value]).reshape(stretch + span, heads, HEAD)
    queries = query.reshape(stretch, heads, HEAD)
    key_segs = segment_ids(seq_lengths, stretch_start - span, stretch + span)
    block = math.gcd(stretch, 512)
    allowed = window_allowed(key_segs, stretch_start, 0, block, span)
    score = jnp.einsum(
        "ihe,jhe->hij", queries, keys, preferred_element_type=jnp.float32
    ) * HEAD ** (-0.5)
    score = jnp.where(allowed[None], score, FLOOR_SCORE)
    top = jnp.max(score, axis=2, keepdims=True)
    weight = jnp.exp(score - top)
    total = jnp.sum(weight, axis=2, keepdims=True)
    prob = (weight / total).astype(jnp.bfloat16)
    outputs = jnp.einsum("hij,jhe->ihe", prob, values, preferred_element_type=jnp.float32)
    log_totals = top + jnp.log(total)
    mixed = outputs.reshape(stretch, heads * HEAD)
    return (mixed, (keys, values, key_segs, log_totals))


def window_backward(d_mixed, query, key, value, saved, place):
    seq_lengths, stretch_start, stretch, position, n_seq, flags = place
    keys, values, key_segs, log_totals = saved
    span = WINDOW - 1
    heads = query.shape[1] // HEAD
    queries = query.reshape(stretch, heads, HEAD)
    d_out = d_mixed.reshape(stretch, heads, HEAD)
    block = math.gcd(stretch, 512)
    d_keys = jnp.zeros((stretch + span, heads, HEAD), jnp.float32)
    d_values = jnp.zeros((stretch + span, heads, HEAD), jnp.float32)
    allowed = window_allowed(key_segs, stretch_start, 0, block, span)
    score = jnp.einsum(
        "ihe,jhe->hij", queries, keys, preferred_element_type=jnp.float32
    ) * HEAD ** (-0.5)
    score = jnp.where(allowed[None], score, FLOOR_SCORE)
    prob = jnp.exp(score - log_totals)
    d_prob = jnp.einsum("ihe,jhe->hij", d_out, values, preferred_element_type=jnp.float32)
    d_score = prob * (d_prob - jnp.sum(prob * d_prob, axis=2, keepdims=True)) * HEAD ** (-0.5)
    d_queries = jnp.einsum("hij,jhe->ihe", d_score, keys.astype(jnp.float32), precision=HIGH)
    d_keys = d_keys.at[0 : block + span].add(
        jnp.einsum("hij,ihe->jhe", d_score, queries.astype(jnp.float32), precision=HIGH)
    )
    d_values = d_values.at[0 : block + span].add(
        jnp.einsum(
            "hij,ihe->jhe", prob.astype(jnp.bfloat16), d_out, preferred_element_type=jnp.float32
        )
    )
    back_key, back_value = (
        from_behind(d_keys[:span].astype(jnp.bfloat16), "seq", -1).astype(jnp.float32),
        from_behind(d_values[:span].astype(jnp.bfloat16), "seq", -1).astype(jnp.float32),
    )
    own_keys = d_keys[span:].at[stretch - span :].add(back_key)
    own_values = d_values[span:].at[stretch - span :].add(back_value)
    return (
        d_queries.reshape(stretch, heads * HEAD).astype(jnp.bfloat16),
        own_keys.reshape(stretch, heads * HEAD).astype(jnp.bfloat16),
        own_values.reshape(stretch, heads * HEAD).astype(jnp.bfloat16),
    )


def norm_forward(values, gain):
    inverse = lax.rsqrt(jnp.mean(values * values, axis=-1, keepdims=True) + EPS)
    scaled = values * inverse
    return ((scaled * gain).astype(jnp.bfloat16), scaled, inverse)


def norm_backward(grad, scaled, inverse, gain):
    d_scaled = grad * gain
    d_values = inverse * (d_scaled - scaled * jnp.mean(d_scaled * scaled, axis=-1, keepdims=True))
    return (d_values, jnp.sum(grad * scaled, axis=0))


def attention_forward(inputs, gain, weights, core, place, rows):
    w_query, w_key, w_value, w_out = weights
    normed, scaled, inverse = norm_forward(inputs, gain)
    gathered = spread(normed)
    query = plain(gathered, w_query).astype(jnp.bfloat16)
    key = plain(gathered, w_key).astype(jnp.bfloat16)
    value = plain(gathered, w_value).astype(jnp.bfloat16)
    mixed, saved = core(query, key, value, place)
    mixed_low = mixed.astype(jnp.bfloat16)

    def attention_project(start, count):
        return plain(mixed_low, w_out)

    branch = collect(attention_project, rows)
    return (inputs + branch, (scaled, inverse, gathered, query, key, value, mixed_low, saved))


def attention_backward(grad, kept, gain, weights, core_back, place, rows):
    w_query, w_key, w_value, w_out = weights
    scaled, inverse, gathered, query, key, value, mixed_low, saved = kept
    grad_full = spread(grad.astype(jnp.bfloat16))
    d_out_w = inner(mixed_low, grad_full)
    d_mixed = through(grad_full, w_out).astype(jnp.bfloat16)
    d_query, d_key, d_value = core_back(d_mixed, query, key, value, saved, place)
    d_query_w = inner(gathered, d_query)
    d_key_w = inner(gathered, d_key)
    d_value_w = inner(gathered, d_value)

    def attention_back_rows(start, count):
        return through(d_query, w_query) + through(d_key, w_key) + through(d_value, w_value)

    d_normed = collect(attention_back_rows, rows)
    d_inputs, d_gain = norm_backward(d_normed, scaled, inverse, gain)
    return (grad + d_inputs, d_gain, (d_query_w, d_key_w, d_value_w, d_out_w))


def mlp_forward(inputs, gain, w_gate, w_up, w_down, rows):
    normed, scaled, inverse = norm_forward(inputs, gain)
    gathered = spread(normed)
    gate = plain(gathered, w_gate)
    up_val = plain(gathered, w_up)
    hidden = (jax.nn.silu(gate) * up_val).astype(jnp.bfloat16)

    def mlp_project(start, count):
        return plain(hidden, w_down)

    branch = collect(mlp_project, rows)
    return (inputs + branch, (scaled, inverse, gathered, gate, up_val, hidden))


def mlp_backward(grad, kept, gain, w_gate, w_up, w_down, rows):
    scaled, inverse, gathered, gate, up_val, hidden = kept
    grad_full = spread(grad.astype(jnp.bfloat16))
    d_hidden = through(grad_full, w_down)
    d_down_w = inner(hidden, grad_full)
    sigma = jax.nn.sigmoid(gate)
    d_gate = (d_hidden * up_val * sigma * (1.0 + gate * (1.0 - sigma))).astype(jnp.bfloat16)
    d_up = (d_hidden * gate * sigma).astype(jnp.bfloat16)
    d_gate_w = inner(gathered, d_gate)
    d_up_w = inner(gathered, d_up)

    def mlp_back_rows(start, count):
        return through(d_gate, w_gate) + through(d_up, w_up)

    d_normed = collect(mlp_back_rows, rows)
    d_inputs, d_gain = norm_backward(d_normed, scaled, inverse, gain)
    return (grad + d_inputs, d_gain, (d_gate_w, d_up_w, d_down_w))


def on_device(
    inputs,
    cotangent,
    seq_lengths,
    norm_gains,
    query_one,
    key_one,
    value_one,
    out_one,
    gate_one,
    up_one,
    down_one,
    query_two,
    key_two,
    value_two,
    out_two,
    gate_two,
    up_two,
    down_two,
):
    rows = inputs.shape[0]
    stretch = rows * lax.axis_size("tensor")
    n_seq = lax.axis_size("seq")
    position = lax.axis_index("seq")
    stretch_start = position * stretch
    flags = start_flags(seq_lengths, stretch, n_seq)
    place = (seq_lengths, stretch_start, stretch, position, n_seq, flags)
    first_attn = (query_one, key_one, value_one, out_one)
    second_attn = (query_two, key_two, value_two, out_two)
    start = inputs.astype(jnp.float32)
    middle_one, kept_one = attention_forward(
        start, norm_gains[0], first_attn, taylor_forward, place, rows
    )
    layer_out, kept_two = mlp_forward(middle_one, norm_gains[1], gate_one, up_one, down_one, rows)
    middle_two, kept_three = attention_forward(
        layer_out, norm_gains[2], second_attn, window_forward, place, rows
    )
    result, kept_four = mlp_forward(middle_two, norm_gains[3], gate_two, up_two, down_two, rows)
    grad = cotangent.astype(jnp.float32)
    grad, gain_four, feed_two = mlp_backward(
        grad, kept_four, norm_gains[3], gate_two, up_two, down_two, rows
    )
    grad, gain_three, attn_two = attention_backward(
        grad, kept_three, norm_gains[2], second_attn, window_backward, place, rows
    )
    grad, gain_two, feed_one = mlp_backward(
        grad, kept_two, norm_gains[1], gate_one, up_one, down_one, rows
    )
    grad, gain_one, attn_one = attention_backward(
        grad, kept_one, norm_gains[0], first_attn, taylor_backward, place, rows
    )
    summed = (
        lax.psum_scatter(attn_one[0], "seq", scatter_dimension=0, tiled=True),
        lax.psum_scatter(attn_one[1], "seq", scatter_dimension=0, tiled=True),
        lax.psum_scatter(attn_one[2], "seq", scatter_dimension=0, tiled=True),
        lax.psum_scatter(attn_one[3], "seq", scatter_dimension=1, tiled=True),
        lax.psum_scatter(feed_one[0], "seq", scatter_dimension=0, tiled=True),
        lax.psum_scatter(feed_one[1], "seq", scatter_dimension=0, tiled=True),
        lax.psum_scatter(feed_one[2], "seq", scatter_dimension=1, tiled=True),
        lax.psum_scatter(attn_two[0], "seq", scatter_dimension=0, tiled=True),
        lax.psum_scatter(attn_two[1], "seq", scatter_dimension=0, tiled=True),
        lax.psum_scatter(attn_two[2], "seq", scatter_dimension=0, tiled=True),
        lax.psum_scatter(attn_two[3], "seq", scatter_dimension=1, tiled=True),
        lax.psum_scatter(feed_two[0], "seq", scatter_dimension=0, tiled=True),
        lax.psum_scatter(feed_two[1], "seq", scatter_dimension=0, tiled=True),
        lax.psum_scatter(feed_two[2], "seq", scatter_dimension=1, tiled=True),
    )
    sums_one = summed[:7]
    sums_two = summed[7:]
    gains = lax.psum_scatter(
        jnp.stack([gain_one, gain_two, gain_three, gain_four]),
        ("seq", "tensor"),
        scatter_dimension=1,
        tiled=True,
    )
    return (
        result.astype(jnp.bfloat16),
        grad,
        gains,
        sums_one[0],
        sums_one[1],
        sums_one[2],
        sums_one[3],
        sums_one[4],
        sums_one[5],
        sums_one[6],
        sums_two[0],
        sums_two[1],
        sums_two[2],
        sums_two[3],
        sums_two[4],
        sums_two[5],
        sums_two[6],
    )


def solution(mesh):
    return jax.shard_map(
        on_device,
        mesh=mesh,
        in_specs=(
            P(("seq", "tensor"), None),
            P(("seq", "tensor"), None),
            P(),
            P(),
            P(None, "tensor"),
            P(None, "tensor"),
            P(None, "tensor"),
            P("tensor", None),
            P(None, "tensor"),
            P(None, "tensor"),
            P("tensor", None),
            P(None, "tensor"),
            P(None, "tensor"),
            P(None, "tensor"),
            P("tensor", None),
            P(None, "tensor"),
            P(None, "tensor"),
            P("tensor", None),
        ),
        out_specs=(
            P(("seq", "tensor"), None),
            P(("seq", "tensor"), None),
            P(None, ("seq", "tensor")),
            P("seq", "tensor"),
            P("seq", "tensor"),
            P("seq", "tensor"),
            P("tensor", "seq"),
            P("seq", "tensor"),
            P("seq", "tensor"),
            P("tensor", "seq"),
            P("seq", "tensor"),
            P("seq", "tensor"),
            P("seq", "tensor"),
            P("tensor", "seq"),
            P("seq", "tensor"),
            P("seq", "tensor"),
            P("tensor", "seq"),
        ),
        check_vma=False,
    )
```

profile of v0, /device:TPU:0, one launch (start us, length us, event | category | flops | bytes accessed | tf_op | source)
XLA Modules:
  0.0 1763.4 jit_solution(18435338880967556840)
XLA Ops:
  18.5 12.9 all-gather.15.cloned.1.call-done
  34.9 30.4 %all-gather.1 = bf16[8,273,4]{1,2,0:T(4,128)(2,1)S(1)} all-gather(bf16[1,273,4]{1,2,0:T(4,128)(2,1)S(1)} %bitcast.357), channel_id=1, replica_groups=mesh['seq'=8,'tensor'=4] {'seq'}, dimensions={0}, use_global_device_ids=true | all-gather | bytes 19656 | tf_op jit(solution)/shard_map/all_gather | solution.py:118
  73.6 4.3 fusion.17
  82.5 26.6 %all-gather.31.cloned.1.call-done = bf16[8,273,256]{2,1,0:T(8,128)(2,1)} async-done(((bf16[1,273,256]{2,1,0:T(8,128)(2,1)}), bf16[8,273,256]{2,1,0:T(8,128)(2,1)}) %all-gather.31.cloned.1.call-update) | async-done | bytes 1118224 | tf_op jit(solution)/shard_map/all_gather | solution.py:115
  114.6 4.7 fusion.135
  121.9 23.4 %reduce-scatter.26.cloned.1.call-done = bf16[128,1024]{1,0:T(8,128)(2,1)} async-done(((bf16[512,1024]{1,0:T(8,128)(2,1)}), bf16[128,1024]{1,0:T(8,128)(2,1)}) %reduce-scatter.26.cloned.1.call-update) | async-done | bytes 262160 | tf_op jit(solution)/shard_map/reduce_scatter | solution.py:81
  148.3 16.8 all-gather.17.cloned.1.call-done
  173.0 25.0 %reduce-scatter.28.cloned.1.call-done = bf16[128,1024]{1,0:T(8,128)(2,1)} async-done(((bf16[512,1024]{1,0:T(8,128)(2,1)}), bf16[128,1024]{1,0:T(8,128)(2,1)}) %reduce-scatter.28.cloned.1.call-update) | async-done | bytes 262160 | tf_op jit(solution)/shard_map/reduce_scatter | solution.py:81
  201.5 15.4 all-gather.19.cloned.1.call-done
  225.4 4.0 collective-permute-start
  244.4 23.5 %reduce-scatter.30.cloned.1.call-done = bf16[128,1024]{1,0:T(8,128)(2,1)} async-done(((bf16[512,1024]{1,0:T(8,128)(2,1)}), bf16[128,1024]{1,0:T(8,128)(2,1)}) %reduce-scatter.30.cloned.1.call-update) | async-done | bytes 262160 | tf_op jit(solution)/shard_map/reduce_scatter | solution.py:81
  271.6 16.1 all-gather.21.cloned.1.call-done
  287.7 3.8 fusion.139
  293.6 12.5 all-gather.23.cloned.1.call-done
  306.1 4.5 multiply_convert_fusion.2
  314.5 25.0 %reduce-scatter.34.cloned.1.call-done = bf16[128,1024]{1,0:T(8,128)(2,1)} async-done(((bf16[512,1024]{1,0:T(8,128)(2,1)}), bf16[128,1024]{1,0:T(8,128)(2,1)}) %reduce-scatter.34.cloned.1.call-update) | async-done | bytes 262160 | tf_op jit(solution)/shard_map/reduce_scatter | solution.py:81
  344.5 15.9 all-gather.25.cloned.1.call-done
  365.6 3.6 multiply_reduce_fusion
  393.3 4.0 add_convert_fusion.2
  400.5 23.1 %reduce-scatter.36.cloned.1.call-done = bf16[128,1024]{1,0:T(8,128)(2,1)} async-done(((bf16[512,1024]{1,0:T(8,128)(2,1)}), bf16[128,1024]{1,0:T(8,128)(2,1)}) %reduce-scatter.36.cloned.1.call-update) | async-done | bytes 262160 | tf_op jit(solution)/shard_map/reduce_scatter | solution.py:81
  424.8 26.3 %reduce-scatter.32.cloned.1.call-done = bf16[128,1024]{1,0:T(8,128)(2,1)} async-done(((bf16[512,1024]{1,0:T(8,128)(2,1)}), bf16[128,1024]{1,0:T(8,128)(2,1)}) %reduce-scatter.32.cloned.1.call-update) | async-done | bytes 262160 | tf_op jit(solution)/shard_map/reduce_scatter | solution.py:81
  453.9 16.6 all-gather.27.cloned.1.call-done
  470.5 3.9 multiply_convert_fusion
  478.4 25.0 %reduce-scatter.38.cloned.1.call-done = bf16[128,1024]{1,0:T(8,128)(2,1)} async-done(((bf16[512,1024]{1,0:T(8,128)(2,1)}), bf16[128,1024]{1,0:T(8,128)(2,1)}) %reduce-scatter.38.cloned.1.call-update) | async-done | bytes 262160 | tf_op jit(solution)/shard_map/reduce_scatter | solution.py:81
  506.7 16.8 all-gather.29.cloned.1.call-done
  531.2 31.0 %all-gather.3 = bf16[8,273,4]{1,2,0:T(4,128)(2,1)S(1)} all-gather(bf16[1,273,4]{1,2,0:T(4,128)(2,1)S(1)} %bitcast.356), channel_id=1, replica_groups=mesh['seq'=8,'tensor'=4] {'seq'}, dimensions={0}, use_global_device_ids=true | all-gather | bytes 19656 | tf_op jit(solution)/shard_map/all_gather | solution.py:109
  567.8 3.7 multiply_reduce_fusion.4
  579.4 5.6 fusion.15
  590.7 3.7 fusion.30
  598.2 3.6 fusion.56
  605.0 24.7 %reduce-scatter.40.cloned.1.call-done = bf16[128,1024]{1,0:T(8,128)(2,1)} async-done(((bf16[512,1024]{1,0:T(8,128)(2,1)}), bf16[128,1024]{1,0:T(8,128)(2,1)}) %reduce-scatter.40.cloned.1.call-update) | async-done | bytes 262160 | tf_op jit(solution)/shard_map/reduce_scatter | solution.py:81
  632.1 3.6 fusion.153
  640.9 3.6 fusion.158
  674.8 91.5 %reduce-scatter.70.cloned.1.call-done = f32[32,4]{1,0:T(8,128)} async-done(((f32[1024,4]{1,0:T(8,128)}), f32[32,4]{1,0:T(8,128)}) %reduce-scatter.70.cloned.1.call-update) | async-done | bytes 528
  767.6 73.2 %reduce-scatter.68.cloned.1.call-done = f32[688,128]{1,0:T(8,128)} async-done(((f32[688,1024]{1,0:T(8,128)}), f32[688,128]{1,0:T(8,128)}) %reduce-scatter.68.cloned.1.call-update) | async-done | bytes 352272 | tf_op jit(solution)/shard_map/reduce_scatter | solution.py:437
  840.8 77.5 %reduce-scatter.66.cloned.1.call-done = f32[128,688]{0,1:T(8,128)} async-done(((f32[1024,688]{0,1:T(8,128)}), f32[128,688]{0,1:T(8,128)}) %reduce-scatter.66.cloned.1.call-update) | async-done | bytes 352272 | tf_op jit(solution)/shard_map/reduce_scatter | solution.py:436
  918.3 77.4 %reduce-scatter.64.cloned.1.call-done = f32[128,688]{0,1:T(8,128)} async-done(((f32[1024,688]{0,1:T(8,128)}), f32[128,688]{0,1:T(8,128)}) %reduce-scatter.64.cloned.1.call-update) | async-done | bytes 352272 | tf_op jit(solution)/shard_map/reduce_scatter | solution.py:435
  995.7 66.8 %reduce-scatter.62.cloned.1.call-done = f32[256,128]{1,0:T(8,128)} async-done(((f32[256,1024]{1,0:T(8,128)}), f32[256,128]{1,0:T(8,128)}) %reduce-scatter.62.cloned.1.call-update) | async-done | bytes 131088 | tf_op jit(solution)/shard_map/reduce_scatter | solution.py:434
  1062.5 66.3 %reduce-scatter.56.cloned.1.call-done = f32[128,256]{1,0:T(8,128)} async-done(((f32[1024,256]{1,0:T(8,128)}), f32[128,256]{1,0:T(8,128)}) %reduce-scatter.56.cloned.1.call-update) | async-done | bytes 131088 | tf_op jit(solution)/shard_map/reduce_scatter | solution.py:431
  1128.8 66.7 %reduce-scatter.60.cloned.1.call-done = f32[128,256]{1,0:T(8,128)} async-done(((f32[1024,256]{1,0:T(8,128)}), f32[128,256]{1,0:T(8,128)}) %reduce-scatter.60.cloned.1.call-update) | async-done | bytes 131088 | tf_op jit(solution)/shard_map/reduce_scatter | solution.py:433
  1195.5 66.2 %reduce-scatter.58.cloned.1.call-done = f32[128,256]{1,0:T(8,128)} async-done(((f32[1024,256]{1,0:T(8,128)}), f32[128,256]{1,0:T(8,128)}) %reduce-scatter.58.cloned.1.call-update) | async-done | bytes 131088 | tf_op jit(solution)/shard_map/reduce_scatter | solution.py:432
  1261.7 64.9 %reduce-scatter.42.cloned.1.call-done = f32[128,64]{0,1:T(8,128)} async-done(((f32[1024,64]{0,1:T(8,128)}), f32[128,64]{0,1:T(8,128)}) %reduce-scatter.42.cloned.1.call-update) | async-done | bytes 32784 | tf_op jit(solution)/shard_map/reduce_scatter | solution.py:424
  1326.6 77.8 %reduce-scatter.54.cloned.1.call-done = f32[688,128]{1,0:T(8,128)} async-done(((f32[688,1024]{1,0:T(8,128)}), f32[688,128]{1,0:T(8,128)}) %reduce-scatter.54.cloned.1.call-update) | async-done | bytes 352272 | tf_op jit(solution)/shard_map/reduce_scatter | solution.py:430
  1404.4 77.4 %reduce-scatter.52.cloned.1.call-done = f32[128,688]{0,1:T(8,128)} async-done(((f32[1024,688]{0,1:T(8,128)}), f32[128,688]{0,1:T(8,128)}) %reduce-scatter.52.cloned.1.call-update) | async-done | bytes 352272 | tf_op jit(solution)/shard_map/reduce_scatter | solution.py:429
  1481.8 76.6 %reduce-scatter.50.cloned.1.call-done = f32[128,688]{0,1:T(8,128)} async-done(((f32[1024,688]{0,1:T(8,128)}), f32[128,688]{0,1:T(8,128)}) %reduce-scatter.50.cloned.1.call-update) | async-done | bytes 352272 | tf_op jit(solution)/shard_map/reduce_scatter | solution.py:428
  1558.4 66.9 %reduce-scatter.48.cloned.1.call-done = f32[256,128]{1,0:T(8,128)} async-done(((f32[256,1024]{1,0:T(8,128)}), f32[256,128]{1,0:T(8,128)}) %reduce-scatter.48.cloned.1.call-update) | async-done | bytes 131088 | tf_op jit(solution)/shard_map/reduce_scatter | solution.py:427
  1625.3 64.7 %reduce-scatter.44.cloned.1.call-done = f32[128,64]{0,1:T(8,128)} async-done(((f32[1024,64]{0,1:T(8,128)}), f32[128,64]{0,1:T(8,128)}) %reduce-scatter.44.cloned.1.call-update) | async-done | bytes 32784 | tf_op jit(solution)/shard_map/reduce_scatter | solution.py:425
  1689.9 66.4 %reduce-scatter.46.cloned.1.call-done = f32[128,256]{1,0:T(8,128)} async-done(((f32[1024,256]{1,0:T(8,128)}), f32[128,256]{1,0:T(8,128)}) %reduce-scatter.46.cloned.1.call-update) | async-done | bytes 131088 | tf_op jit(solution)/shard_map/reduce_scatter | solution.py:426
  (438 shorter events, 203.2 us)
Async XLA Ops:
  7.2 298.9 %copy-start = (bf16[688,1024]{1,0:T(8,128)(2,1)S(1)}, bf16[688,1024]{1,0:T(8,128)(2,1)}, u32[]{:S(2)}) copy-start(bf16[688,1024]{1,0:T(8,128)(2,1)} %param.47) | copy-start | bytes 4227076
  7.2 24.2 %all-gather.15.cloned.1.call-start = ((), (), s32[]{:S(2)}) async-start(), calls=%async_computation.23 | async-start | bytes 1310720 | tf_op jit(solution)/shard_map/all_gather | solution.py:77
  11.7 97.4 %all-gather.31.cloned.1.call-start = ((), (), s32[]{:S(2)}) async-start(), calls=%async_computation.53 | async-start | bytes 1290240 | tf_op jit(solution)/shard_map/all_gather | solution.py:115
  15.8 50.0 %copy-start.82 = (f32[512]{0:T(512)}, f32[512]{0:T(512)S(1)}, u32[]{:S(2)}) copy-start(f32[512]{0:T(512)S(1)} %get-tuple-element.97) | copy-start | bytes 6148
  16.8 51.7 %copy-start.102 = (f32[8,1]{0,1:T(1,128)}, f32[8,1]{0,1:T(1,128)S(1)}, u32[]{:S(2)}) copy-start(f32[8,1]{0,1:T(1,128)S(1)} %reduce-window.15) | copy-start | bytes 100
  16.8 49.0 %copy-start.76 = (f32[273]{0:T(512)}, f32[273]{0:T(512)S(1)}, u32[]{:S(2)}) copy-start(f32[273]{0:T(512)S(1)} %pad.21.clone) | copy-start | bytes 3280
  68.3 77.0 %reduce-scatter.26.cloned.1.call-start = ((), (), s32[]{:S(2)}) async-start(), calls=%async_computation.24 | async-start | bytes 1310720 | tf_op jit(solution)/shard_map/reduce_scatter | solution.py:81
  71.7 42.9 %copy-start.17 = (f32[512,64]{0,1:T(8,128)}, f32[512,64]{0,1:T(8,128)S(1)}, u32[]{:S(2)}) copy-start(f32[512,64]{0,1:T(8,128)S(1)} %fusion.52) | copy-start | bytes 393220
  121.5 43.7 %all-gather.17.cloned.1.call-start = ((), (), s32[]{:S(2)}) async-start(), calls=%async_computation.25 | async-start | bytes 1310720 | tf_op jit(solution)/shard_map/all_gather | solution.py:77
  148.3 49.8 %reduce-scatter.28.cloned.1.call-start = ((), (), s32[]{:S(2)}) async-start(), calls=%async_computation.26 | async-start | bytes 1310720 | tf_op jit(solution)/shard_map/reduce_scatter | solution.py:81
  173.0 44.0 %all-gather.19.cloned.1.call-start = ((), (), s32[]{:S(2)}) async-start(), calls=%async_computation.27 | async-start | bytes 1310720 | tf_op jit(solution)/shard_map/all_gather | solution.py:77
  200.1 67.8 %reduce-scatter.30.cloned.1.call-start = ((), (), s32[]{:S(2)}) async-start(), calls=%async_computation.28 | async-start | bytes 1310720 | tf_op jit(solution)/shard_map/reduce_scatter | solution.py:81
  218.9 11.7 collective-permute-start.1
  225.4 7.8 collective-permute-start
  244.3 43.3 %all-gather.21.cloned.1.call-start = ((), (), s32[]{:S(2)}) async-start(), calls=%async_computation.29 | async-start | bytes 1310720 | tf_op jit(solution)/shard_map/all_gather | solution.py:77
  269.0 72.5 %copy-start.85 = (f32[128]{0:T(128)}, f32[128]{0:T(128)S(1)}, u32[]{:S(2)}) copy-start(f32[128]{0:T(128)S(1)} %add_rsqrt_fusion) | copy-start | bytes 1540
  270.8 35.3 %all-gather.23.cloned.1.call-start = ((), (), s32[]{:S(2)}) async-start(), calls=%async_computation.31 | async-start | bytes 1310720 | tf_op jit(solution)/shard_map/all_gather | solution.py:77
  271.5 68.0 %reduce-scatter.34.cloned.1.call-start = ((), (), s32[]{:S(2)}) async-start(), calls=%async_computation.32 | async-start | bytes 1310720 | tf_op jit(solution)/shard_map/reduce_scatter | solution.py:81
  314.5 46.0 %all-gather.25.cloned.1.call-start = ((), (), s32[]{:S(2)}) async-start(), calls=%async_computation.33 | async-start | bytes 1310720 | tf_op jit(solution)/shard_map/all_gather | solution.py:77
  343.6 80.0 %reduce-scatter.36.cloned.1.call-start = ((), (), s32[]{:S(2)}) async-start(), calls=%async_computation.34 | async-start | bytes 1310720 | tf_op jit(solution)/shard_map/reduce_scatter | solution.py:81
  376.2 13.6 collective-permute-start.3
  377.5 6.8 collective-permute-start.2
  397.3 53.8 %reduce-scatter.32.cloned.1.call-start = ((), (), s32[]{:S(2)}) async-start(), calls=%async_computation.30 | async-start | bytes 1310720 | tf_op jit(solution)/shard_map/reduce_scatter | solution.py:81
  397.4 53.8 %copy-start.86 = (f32[128]{0:T(128)S(1)}, f32[128]{0:T(128)}, u32[]{:S(2)}) copy-start(f32[128]{0:T(128)} %copy-done.85) | copy-start | bytes 1540
  397.4 53.8 %copy-start.99 = (f32[128]{0:T(128)S(1)}, f32[128]{0:T(128)}, u32[]{:S(2)}) copy-start(f32[128]{0:T(128)} %copy-done.98) | copy-start | bytes 1540
  400.5 70.0 %all-gather.27.cloned.1.call-start = ((), (), s32[]{:S(2)}) async-start(), calls=%async_computation.35 | async-start | bytes 1310720 | tf_op jit(solution)/shard_map/all_gather | solution.py:77
  453.6 51.1 %copy-start.19 = (f32[128,1024]{1,0:T(8,128)}, f32[128,1024]{1,0:T(8,128)S(1)}, u32[]{:S(2)}) copy-start(f32[128,1024]{1,0:T(8,128)S(1)} %get-tuple-element.94) | copy-start | bytes 1572868
  453.6 49.8 %reduce-scatter.38.cloned.1.call-start = ((), (), s32[]{:S(2)}) async-start(), calls=%async_computation.36 | async-start | bytes 1310720 | tf_op jit(solution)/shard_map/reduce_scatter | solution.py:81
  478.4 45.2 %copy-start.48 = (bf16[256,1024]{1,0:T(8,128)(2,1)S(1)}, bf16[256,1024]{1,0:T(8,128)(2,1)}, u32[]{:S(2)}) copy-start(bf16[256,1024]{1,0:T(8,128)(2,1)} %param.37) | copy-start | bytes 1572868
  478.4 45.2 %all-gather.29.cloned.1.call-start = ((), (), s32[]{:S(2)}) async-start(), calls=%async_computation.37 | async-start | bytes 1310720 | tf_op jit(solution)/shard_map/all_gather | solution.py:77
  506.7 78.4 %all-gather.33.cloned.1.call-start = ((), (), s32[]{:S(2)}) async-start(), calls=%async_computation.54 | async-start | bytes 1290240 | tf_op jit(solution)/shard_map/all_gather | solution.py:108
  531.2 98.5 %reduce-scatter.40.cloned.1.call-start = ((), (), s32[]{:S(2)}) async-start(), calls=%async_computation.38 | async-start | bytes 1310720 | tf_op jit(solution)/shard_map/reduce_scatter | solution.py:81
  604.9 161.3 %reduce-scatter.70.cloned.1.call-start = ((), (), s32[]{:S(2)}) async-start(), calls=%async_computation.55 | async-start | bytes 540672
  632.1 208.8 %reduce-scatter.68.cloned.1.call-start = ((), (), s32[]{:S(2)}) async-start(), calls=%async_computation.52 | async-start | bytes 3170304 | tf_op jit(solution)/shard_map/reduce_scatter | solution.py:437
  635.8 282.5 %reduce-scatter.66.cloned.1.call-start = ((), (), s32[]{:S(2)}) async-start(), calls=%async_computation.51 | async-start | bytes 3170304 | tf_op jit(solution)/shard_map/reduce_scatter | solution.py:436
  640.6 355.1 %reduce-scatter.64.cloned.1.call-start = ((), (), s32[]{:S(2)}) async-start(), calls=%async_computation.50 | async-start | bytes 3170304 | tf_op jit(solution)/shard_map/reduce_scatter | solution.py:435
  644.5 418.0 %reduce-scatter.62.cloned.1.call-start = ((), (), s32[]{:S(2)}) async-start(), calls=%async_computation.49 | async-start | bytes 1179648 | tf_op jit(solution)/shard_map/reduce_scatter | solution.py:434
  648.1 480.7 %reduce-scatter.56.cloned.1.call-start = ((), (), s32[]{:S(2)}) async-start(), calls=%async_computation.46 | async-start | bytes 1179648 | tf_op jit(solution)/shard_map/reduce_scatter | solution.py:431
  649.7 545.8 %reduce-scatter.60.cloned.1.call-start = ((), (), s32[]{:S(2)}) async-start(), calls=%async_computation.48 | async-start | bytes 1179648 | tf_op jit(solution)/shard_map/reduce_scatter | solution.py:433
  651.3 610.4 %reduce-scatter.58.cloned.1.call-start = ((), (), s32[]{:S(2)}) async-start(), calls=%async_computation.47 | async-start | bytes 1179648 | tf_op jit(solution)/shard_map/reduce_scatter | solution.py:432
  652.9 673.7 %reduce-scatter.42.cloned.1.call-start = ((), (), s32[]{:S(2)}) async-start(), calls=%async_computation.39 | async-start | bytes 294912 | tf_op jit(solution)/shard_map/reduce_scatter | solution.py:424
  654.0 750.5 %reduce-scatter.54.cloned.1.call-start = ((), (), s32[]{:S(2)}) async-start(), calls=%async_computation.45 | async-start | bytes 3170304 | tf_op jit(solution)/shard_map/reduce_scatter | solution.py:430
  657.7 824.2 %reduce-scatter.52.cloned.1.call-start = ((), (), s32[]{:S(2)}) async-start(), calls=%async_computation.44 | async-start | bytes 3170304 | tf_op jit(solution)/shard_map/reduce_scatter | solution.py:429
  662.4 896.0 %reduce-scatter.50.cloned.1.call-start = ((), (), s32[]{:S(2)}) async-start(), calls=%async_computation.43 | async-start | bytes 3170304 | tf_op jit(solution)/shard_map/reduce_scatter | solution.py:428
  666.1 959.2 %reduce-scatter.48.cloned.1.call-start = ((), (), s32[]{:S(2)}) async-start(), calls=%async_computation.42 | async-start | bytes 1179648 | tf_op jit(solution)/shard_map/reduce_scatter | solution.py:427
  668.7 1021.2 %reduce-scatter.44.cloned.1.call-start = ((), (), s32[]{:S(2)}) async-start(), calls=%async_computation.40 | async-start | bytes 294912 | tf_op jit(solution)/shard_map/reduce_scatter | solution.py:425
  669.8 1086.5 %reduce-scatter.46.cloned.1.call-start = ((), (), s32[]{:S(2)}) async-start(), calls=%async_computation.41 | async-start | bytes 1179648 | tf_op jit(solution)/shard_map/reduce_scatter | solution.py:426
  669.9 1086.4 %copy-start.1 = (bf16[688,1024]{1,0:T(8,128)(2,1)S(1)}, bf16[688,1024]{1,0:T(8,128)(2,1)}, u32[]{:S(2)}) copy-start(bf16[688,1024]{1,0:T(8,128)(2,1)} %param.47) | copy-start | bytes 4227076
  (103 other events, 953.6 us)
Sparse Core Ops, SparseCore 0:
  11.9 19.4 all-gather.14
  68.4 40.6 all-gather.30
  121.6 23.7 reduce-scatter.25
  148.4 16.7 all-gather.16
  173.1 24.8 reduce-scatter.27
  200.2 16.6 all-gather.18
  244.5 23.3 reduce-scatter.29
  270.9 16.7 all-gather.20
  289.3 16.7 all-gather.22
  314.6 24.8 reduce-scatter.33
  343.7 16.7 all-gather.24
  397.4 26.1 reduce-scatter.35
  426.3 24.8 reduce-scatter.31
  453.7 16.7 all-gather.26
  478.5 24.8 reduce-scatter.37
  506.8 16.7 all-gather.28
  531.3 40.8 all-gather.32
  605.0 24.6 reduce-scatter.39
  632.2 134.0 reduce-scatter.69
  770.6 70.1 reduce-scatter.67
  845.3 72.9 reduce-scatter.65
  922.8 72.8 reduce-scatter.63
  1000.0 62.4 reduce-scatter.61
  1066.3 62.4 reduce-scatter.55
  1133.2 62.3 reduce-scatter.59
  1199.4 62.3 reduce-scatter.57
  1265.8 60.7 reduce-scatter.41
  1331.1 73.3 reduce-scatter.53
  1408.9 72.8 reduce-scatter.51
  1486.2 72.1 reduce-scatter.49
  1562.8 62.4 reduce-scatter.47
  1629.2 60.7 reduce-scatter.43
  1693.8 62.4 reduce-scatter.45
where the time goes:
time: 1770 us; the launch traced here: 1760 us
  waiting for transfers between devices  1430 us (81%)
  matrix products  159 us (9%)
  blocking collectives  61.4 us (3%)
  other arithmetic  45.4 us (3%)
  local copies, waits for them, and re-layouts  39.3 us (2%)
    reduce_scatter x8, waiting for transfers between devices, collect(): lax.psum_scatter(product(jnp.int32(0), rows * lax.axis_size('tensor')).as...  196 us
    all_gather x8, waiting for transfers between devices, spread(): return lax.all_gather(part, 'tensor', axis=0, tiled=True)  123 us
    unnamed x34, waiting for transfers between devices  92.7 us
    reduce_scatter x1, waiting for transfers between devices, on_device(): lax.psum_scatter(feed_one[2], 'seq', scatter_dimension=1, tiled=True)  77.8 us
    reduce_scatter x1, waiting for transfers between devices, on_device(): lax.psum_scatter(feed_two[1], 'seq', scatter_dimension=0, tiled=True)  77.5 us
    reduce_scatter x1, waiting for transfers between devices, on_device(): lax.psum_scatter(feed_one[1], 'seq', scatter_dimension=0, tiled=True)  77.4 us
    reduce_scatter x1, waiting for transfers between devices, on_device(): lax.psum_scatter(feed_two[0], 'seq', scatter_dimension=0, tiled=True)  77.4 us
    reduce_scatter x1, waiting for transfers between devices, on_device(): lax.psum_scatter(feed_one[0], 'seq', scatter_dimension=0, tiled=True)  76.6 us
  transfers between devices with their start and end apart: 37, of which 33 were waited for; matrix products, arithmetic and copies ran while one was open for 6% of the time, Pallas kernels for 0%

commit v1 on v0

--- a/solution.py
+++ b/solution.py
@@ -3,6 +3,8 @@
 import jax
 import jax.numpy as jnp
 from jax import lax
+from jax.experimental import pallas as pl
+from jax.experimental.pallas import tpu as pltpu
 from jax.sharding import PartitionSpec as P
 
 FEAT = 16
@@ -300,73 +302,487 @@
     return (d_values, jnp.sum(grad * scaled, axis=0))
 
 
-def attention_forward(inputs, gain, weights, core, place, rows):
-    w_query, w_key, w_value, w_out = weights
-    normed, scaled, inverse = norm_forward(inputs, gain)
-    gathered = spread(normed)
-    query = plain(gathered, w_query).astype(jnp.bfloat16)
-    key = plain(gathered, w_key).astype(jnp.bfloat16)
-    value = plain(gathered, w_value).astype(jnp.bfloat16)
-    mixed, saved = core(query, key, value, place)
-    mixed_low = mixed.astype(jnp.bfloat16)
-
-    def attention_project(start, count):
-        return plain(mixed_low, w_out)
-
-    branch = collect(attention_project, rows)
-    return (inputs + branch, (scaled, inverse, gathered, query, key, value, mixed_low, saved))
-
-
-def attention_backward(grad, kept, gain, weights, core_back, place, rows):
-    w_query, w_key, w_value, w_out = weights
-    scaled, inverse, gathered, query, key, value, mixed_low, saved = kept
-    grad_full = spread(grad.astype(jnp.bfloat16))
-    d_out_w = inner(mixed_low, grad_full)
-    d_mixed = through(grad_full, w_out).astype(jnp.bfloat16)
-    d_query, d_key, d_value = core_back(d_mixed, query, key, value, saved, place)
-    d_query_w = inner(gathered, d_query)
-    d_key_w = inner(gathered, d_key)
-    d_value_w = inner(gathered, d_value)
-
-    def attention_back_rows(start, count):
-        return through(d_query, w_query) + through(d_key, w_key) + through(d_value, w_value)
-
-    d_normed = collect(attention_back_rows, rows)
-    d_inputs, d_gain = norm_backward(d_normed, scaled, inverse, gain)
-    return (grad + d_inputs, d_gain, (d_query_w, d_key_w, d_value_w, d_out_w))
-
-
-def mlp_forward(inputs, gain, w_gate, w_up, w_down, rows):
-    normed, scaled, inverse = norm_forward(inputs, gain)
-    gathered = spread(normed)
-    gate = plain(gathered, w_gate)
-    up_val = plain(gathered, w_up)
-    hidden = (jax.nn.silu(gate) * up_val).astype(jnp.bfloat16)
-
-    def mlp_project(start, count):
-        return plain(hidden, w_down)
-
-    branch = collect(mlp_project, rows)
-    return (inputs + branch, (scaled, inverse, gathered, gate, up_val, hidden))
-
-
-def mlp_backward(grad, kept, gain, w_gate, w_up, w_down, rows):
-    scaled, inverse, gathered, gate, up_val, hidden = kept
-    grad_full = spread(grad.astype(jnp.bfloat16))
-    d_hidden = through(grad_full, w_down)
-    d_down_w = inner(hidden, grad_full)
-    sigma = jax.nn.sigmoid(gate)
-    d_gate = (d_hidden * up_val * sigma * (1.0 + gate * (1.0 - sigma))).astype(jnp.bfloat16)
-    d_up = (d_hidden * gate * sigma).astype(jnp.bfloat16)
-    d_gate_w = inner(gathered, d_gate)
-    d_up_w = inner(gathered, d_up)
-
-    def mlp_back_rows(start, count):
-        return through(d_gate, w_gate) + through(d_up, w_up)
-
-    d_normed = collect(mlp_back_rows, rows)
-    d_inputs, d_gain = norm_backward(d_normed, scaled, inverse, gain)
-    return (grad + d_inputs, d_gain, (d_gate_w, d_up_w, d_down_w))
+MESH = pl.DeviceIdType.MESH
+LOW = jnp.bfloat16
+FULL = jnp.float32
+VMEM = pl.BlockSpec(memory_space=pltpu.VMEM)
+VMEM_BYTES = 56 * 1024 * 1024
+
+
+class Group:
+    def __init__(self):
+        index = lax.axis_index("tensor")
+        self.index = index
+        self.low = lax.rem(index, 2)
+        self.high = index // 2
+        self.pair = {"tensor": index + 1 - 2 * self.low}
+        self.partner = {"tensor": lax.rem(index + 2, 4)}
+
+    def own(self, chunk):
+        return self.low + 2 * chunk
+
+    def other(self, chunk):
+        return 1 - self.low + 2 * chunk
+
+    def greet(self):
+        barrier = pltpu.get_barrier_semaphore()
+        pl.semaphore_signal(barrier, inc=1, device_id=self.pair, device_id_type=MESH)
+        pl.semaphore_signal(barrier, inc=1, device_id=self.partner, device_id_type=MESH)
+        pl.semaphore_wait(barrier, 2)
+
+
+def remote(src, dst, send, recv, device):
+    copy = pltpu.make_async_remote_copy(
+        src_ref=src,
+        dst_ref=dst,
+        send_sem=send,
+        recv_sem=recv,
+        device_id=device,
+        device_id_type=MESH,
+    )
+    copy.start()
+    return copy
+
+
+class Total:
+    def __init__(self, group, buffers, sems):
+        self.group = group
+        self.pair_out, self.pair_in, self.out, self.into = buffers
+        self.sems = sems
+        self.copies = {}
+
+    def give(self, chunk, part):
+        self.pair_out[chunk] = part.astype(LOW)
+        self.copies["pair", chunk] = remote(
+            self.pair_out.at[chunk],
+            self.pair_in.at[chunk],
+            self.sems.at[0, chunk],
+            self.sems.at[1, chunk],
+            self.group.pair,
+        )
+
+    def pair_sum(self, chunk, part):
+        self.copies["pair", chunk].wait_recv()
+        return part + self.pair_in[chunk].astype(FULL)
+
+    def swap(self, chunk, part):
+        self.out[chunk] = self.pair_sum(chunk, part).astype(LOW)
+        self.copies["far", chunk] = remote(
+            self.out.at[chunk],
+            self.into.at[chunk],
+            self.sems.at[2, chunk],
+            self.sems.at[3, chunk],
+            self.group.partner,
+        )
+
+    def take(self, chunk):
+        self.copies["far", chunk].wait_recv()
+        return self.out[chunk].astype(FULL) + self.into[chunk].astype(FULL)
+
+    def close(self):
+        for copy in self.copies.values():
+            copy.wait_send()
+
+
+def total_scratch(rows, width):
+    return [pltpu.VMEM((2, rows, width), LOW)] * 4 + [pltpu.SemaphoreType.DMA((4, 2))]
+
+
+class Share:
+    def __init__(self, group, full, sems):
+        self.group = group
+        self.full = full
+        self.sems = sems
+        self.copies = {}
+
+    def give(self, chunk, block):
+        mine = self.group.own(chunk)
+        self.full[mine] = block
+        self.copies[chunk] = remote(
+            self.full.at[mine],
+            self.full.at[mine],
+            self.sems.at[0, chunk],
+            self.sems.at[1, chunk],
+            self.group.pair,
+        )
+
+    def await_other(self, chunk):
+        self.copies[chunk].wait_recv()
+
+    def close(self):
+        for copy in self.copies.values():
+            copy.wait_send()
+
+
+def share_scratch(rows, width):
+    return [pltpu.VMEM((4, rows, width), LOW), pltpu.SemaphoreType.DMA((2, 2))]
+
+
+def norm_apply(values, gain):
+    inverse = lax.rsqrt(jnp.mean(values * values, axis=-1, keepdims=True) + EPS)
+    return (values * inverse * gain).astype(LOW)
+
+
+def norm_back(grad, values, gain):
+    inverse = lax.rsqrt(jnp.mean(values * values, axis=-1, keepdims=True) + EPS)
+    scaled = values * inverse
+    d_scaled = grad * gain
+    d_values = inverse * (d_scaled - scaled * jnp.mean(d_scaled * scaled, axis=-1, keepdims=True))
+    return d_values, grad * scaled
+
+
+def gate_forward(gate, up_val):
+    return (gate * up_val / (1.0 + jnp.exp(-gate))).astype(LOW)
+
+
+def gate_backward(d_hidden, gate, up_val):
+    sigma = 1.0 / (1.0 + jnp.exp(-gate))
+    d_gate = (d_hidden * up_val * sigma * (1.0 + gate * (1.0 - sigma))).astype(LOW)
+    d_up = (d_hidden * gate * sigma).astype(LOW)
+    return d_gate, d_up
+
+
+def enter_kernel(
+    inputs, cotangent, gains, w_query, w_key, w_value,
+    start_out, normed_out, grad_out, query_out, key_out, value_out,
+    rows_in, cot_in, full, full_sems, cot_full, cot_sems, sems,
+):
+    group = Group()
+    group.greet()
+    far = remote(inputs, rows_in, sems.at[0], sems.at[1], group.partner)
+    far_cot = remote(cotangent, cot_in, sems.at[2], sems.at[3], group.partner)
+    share = Share(group, full, full_sems)
+    cot_share = Share(group, cot_full, cot_sems)
+
+    def project(block):
+        rows = normed_out[block]
+        query_out[block] = plain(rows, w_query[...]).astype(LOW)
+        key_out[block] = plain(rows, w_key[...]).astype(LOW)
+        value_out[block] = plain(rows, w_value[...]).astype(LOW)
+
+    def hand(step, block, raw):
+        values = raw.astype(FULL)
+        start_out[block // 2] = values
+        normed = norm_apply(values, gains[0:1])
+        normed_out[block] = normed
+        full[block] = normed
+        share.copies[step] = remote(
+            full.at[block], full.at[block], full_sems.at[0, step], full_sems.at[1, step], group.pair
+        )
+
+    def hand_cot(step, block, raw):
+        grad_out[block] = raw
+        cot_full[block] = raw
+        cot_share.copies[step] = remote(
+            cot_full.at[block], cot_full.at[block], cot_sems.at[0, step], cot_sems.at[1, step], group.pair
+        )
+
+    mine = group.index
+    mate = mine + 1 - 2 * group.low
+    theirs = lax.rem(mine + 2, 4)
+    theirs_mate = lax.rem(mate + 2, 4)
+    hand(0, mine, inputs[...])
+    hand_cot(0, mine, cotangent[...])
+    project(mine)
+    share.await_other(0)
+    normed_out[mate] = full[mate]
+    project(mate)
+    far.wait_recv()
+    hand(1, theirs, rows_in[...])
+    project(theirs)
+    share.await_other(1)
+    normed_out[theirs_mate] = full[theirs_mate]
+    project(theirs_mate)
+    far_cot.wait_recv()
+    hand_cot(1, theirs, cot_in[...])
+    cot_share.await_other(0)
+    grad_out[mate] = cot_full[mate]
+    cot_share.await_other(1)
+    grad_out[theirs_mate] = cot_full[theirs_mate]
+    far.wait_send()
+    far_cot.wait_send()
+    share.close()
+    cot_share.close()
+
+
+def forward_kernel(
+    mixed, w_out, start, gains, w_gate, w_up, w_down, w_query, w_key, w_value,
+    middle_out, after_out, normed_mlp_out, normed_out, gate_out, up_out, hidden_out, query_out, key_out, value_out,
+    *scratch,
+):
+    group = Group()
+    group.greet()
+    first = Total(group, scratch[0:4], scratch[4])
+    second = Total(group, scratch[5:9], scratch[9])
+    share_mlp = Share(group, *scratch[10:12])
+    share = Share(group, *scratch[12:14])
+
+    def mlp_rows(block):
+        rows = share_mlp.full[block]
+        normed_mlp_out[block] = rows
+        gate = plain(rows, w_gate[...])
+        up_val = plain(rows, w_up[...])
+        gate_out[block] = gate
+        up_out[block] = up_val
+        hidden = gate_forward(gate, up_val)
+        hidden_out[block] = hidden
+        return plain(hidden, w_down[...])
+
+    def project(block):
+        rows = share.full[block]
+        normed_out[block] = rows
+        query_out[block] = plain(rows, w_query[...]).astype(LOW)
+        key_out[block] = plain(rows, w_key[...]).astype(LOW)
+        value_out[block] = plain(rows, w_value[...]).astype(LOW)
+
+    for chunk in range(2):
+        first.give(chunk, plain(mixed[group.other(chunk)], w_out[...]))
+    for chunk in range(2):
+        first.swap(chunk, plain(mixed[group.own(chunk)], w_out[...]))
+    for chunk in range(2):
+        middle = start[chunk] + first.take(chunk)
+        middle_out[chunk] = middle
+        share_mlp.give(chunk, norm_apply(middle, gains[1:2]))
+        part = mlp_rows(group.own(chunk))
+        share_mlp.await_other(chunk)
+        second.give(chunk, mlp_rows(group.other(chunk)))
+        second.swap(chunk, part)
+    for chunk in range(2):
+        after = middle_out[chunk] + second.take(chunk)
+        after_out[chunk] = after
+        share.give(chunk, norm_apply(after, gains[2:3]))
+        project(group.own(chunk))
+        share.await_other(chunk)
+        project(group.other(chunk))
+    for item in (first, second, share_mlp, share):
+        item.close()
+
+
+def turn_kernel(
+    mixed, w_out, after, gains, w_gate, w_up, w_down, cot,
+    result_out, grad_out, grad_low_out, d_mixed_out, normed_out, hidden_out, d_gate_out, d_up_out, gain_out,
+    *scratch,
+):
+    group = Group()
+    group.greet()
+    first = Total(group, scratch[0:4], scratch[4])
+    second = Total(group, scratch[5:9], scratch[9])
+    last = Total(group, scratch[10:14], scratch[14])
+    share_mlp = Share(group, *scratch[15:17])
+    share = Share(group, *scratch[17:19])
+    middle_keep = scratch[19]
+    gain = gains[3:4]
+
+    def mlp_rows(block):
+        rows = share_mlp.full[block]
+        normed_out[block] = rows
+        gate = plain(rows, w_gate[...])
+        up_val = plain(rows, w_up[...])
+        d_hidden = through(cot[block], w_down[...])
+        hidden_out[block] = gate_forward(gate, up_val)
+        d_gate, d_up = gate_backward(d_hidden, gate, up_val)
+        d_gate_out[block] = d_gate
+        d_up_out[block] = d_up
+        return through(d_gate, w_gate[...]) + through(d_up, w_up[...])
+
+    for chunk in range(2):
+        first.give(chunk, plain(mixed[group.other(chunk)], w_out[...]))
+    for chunk in range(2):
+        first.swap(chunk, plain(mixed[group.own(chunk)], w_out[...]))
+    for chunk in range(2):
+        middle = after[chunk] + first.take(chunk)
+        middle_keep[chunk] = middle
+        share_mlp.give(chunk, norm_apply(middle, gain))
+        part = mlp_rows(group.own(chunk))
+        share_mlp.await_other(chunk)
+        second.give(chunk, mlp_rows(group.other(chunk)))
+        second.swap(chunk, part)
+    for chunk in range(2):
+        last.give(chunk, plain(hidden_out[group.other(chunk)], w_down[...]))
+    for chunk in range(2):
+        last.out[chunk] = last.pair_sum(chunk, plain(hidden_out[group.own(chunk)], w_down[...])).astype(LOW)
+    mine, theirs = group.high, 1 - group.high
+    last.copies["far", 0] = remote(
+        last.out.at[theirs], last.into.at[0], last.sems.at[2, 0], last.sems.at[3, 0], group.partner
+    )
+    gain_out[...] = jnp.zeros_like(gain_out)
+    for chunk in range(2):
+        own = group.own(chunk)
+        d_values, d_gain = norm_back(second.take(chunk), middle_keep[chunk], gain)
+        grad = cot[own].astype(FULL) + d_values
+        grad_out[chunk] = grad
+        gain_out[...] += jnp.where(group.high == chunk, 1.0, 0.0) * jnp.sum(d_gain, axis=0, keepdims=True)
+        share.give(chunk, grad.astype(LOW))
+        grad_low_out[own] = share.full[own]
+        d_mixed_out[own] = through(share.full[own], w_out[...]).astype(LOW)
+        share.await_other(chunk)
+        other = group.other(chunk)
+        grad_low_out[other] = share.full[other]
+        d_mixed_out[other] = through(share.full[other], w_out[...]).astype(LOW)
+    last.copies["far", 0].wait_recv()
+    result_out[...] = (
+        middle_keep[mine] + last.out[mine].astype(FULL) + last.into[0].astype(FULL)
+    ).astype(LOW)
+    for item in (first, second, last, share_mlp, share):
+        item.close()
+
+
+def backward_kernel(
+    d_query, d_key, d_value, w_query, w_key, w_value, after, middle, grad_in, gains,
+    gate_in, up_in, w_gate, w_up, w_down, w_out,
+    grad_out, mlp_grad_out, grad_low_out, d_gate_out, d_up_out, d_mixed_out, gain_out,
+    *scratch,
+):
+    group = Group()
+    group.greet()
+    first = Total(group, scratch[0:4], scratch[4])
+    second = Total(group, scratch[5:9], scratch[9])
+    share_mlp = Share(group, *scratch[10:12])
+    share = Share(group, *scratch[12:14])
+
+    def normed_rows(block):
+        return (
+            through(d_query[block], w_query[...])
+            + through(d_key[block], w_key[...])
+            + through(d_value[block], w_value[...])
+        )
+
+    def mlp_rows(block):
+        rows = share_mlp.full[block]
+        mlp_grad_out[block] = rows
+        d_hidden = through(rows, w_down[...])
+        d_gate, d_up = gate_backward(d_hidden, gate_in[block], up_in[block])
+        d_gate_out[block] = d_gate
+        d_up_out[block] = d_up
+        return through(d_gate, w_gate[...]) + through(d_up, w_up[...])
+
+    def back(total, chunk, values, gain, row):
+        d_values, d_gain = norm_back(total.take(chunk), values, gain)
+        kept = jnp.where(group.high == chunk, 1.0, 0.0) * jnp.sum(d_gain, axis=0, keepdims=True)
+        gain_out[row : row + 1] = kept if chunk == 0 else gain_out[row : row + 1] + kept
+        return d_values
+
+    for chunk in range(2):
+        first.give(chunk, normed_rows(group.other(chunk)))
+    for chunk in range(2):
+        first.swap(chunk, normed_rows(group.own(chunk)))
+    for chunk in range(2):
+        grad = grad_in[chunk] + back(first, chunk, after[chunk], gains[2:3], 1)
+        grad_out[chunk] = grad
+        share_mlp.give(chunk, grad.astype(LOW))
+        part = mlp_rows(group.own(chunk))
+        share_mlp.await_other(chunk)
+        second.give(chunk, mlp_rows(group.other(chunk)))
+        second.swap(chunk, part)
+    for chunk in range(2):
+        own = group.own(chunk)
+        grad = grad_out[chunk] + back(second, chunk, middle[chunk], gains[1:2], 0)
+        grad_out[chunk] = grad
+        share.give(chunk, grad.astype(LOW))
+        grad_low_out[own] = share.full[own]
+        d_mixed_out[own] = through(share.full[own], w_out[...]).astype(LOW)
+        share.await_other(chunk)
+        other = group.other(chunk)
+        grad_low_out[other] = share.full[other]
+        d_mixed_out[other] = through(share.full[other], w_out[...]).astype(LOW)
+    for item in (first, second, share_mlp, share):
+        item.close()
+
+
+def leave_kernel(
+    d_query, d_key, d_value, w_query, w_key, w_value, start, grad_in, gains,
+    grad_out, gain_out, *scratch,
+):
+    group = Group()
+    group.greet()
+    last = Total(group, scratch[0:4], scratch[4])
+
+    def normed_rows(block):
+        return (
+            through(d_query[block], w_query[...])
+            + through(d_key[block], w_key[...])
+            + through(d_value[block], w_value[...])
+        )
+
+    mine, theirs = group.high, 1 - group.high
+    for chunk, place in ((0, theirs), (1, mine)):
+        last.give(chunk, normed_rows(group.other(place)))
+        part = normed_rows(group.own(place))
+        if chunk == 0:
+            last.swap(0, part)
+        else:
+            kept = last.pair_sum(1, part)
+    last.copies["far", 0].wait_recv()
+    d_values, d_gain = norm_back(kept + last.into[0].astype(FULL), start[mine], gains[0:1])
+    grad_out[...] = grad_in[mine] + d_values
+    gain_out[...] = jnp.sum(d_gain, axis=0, keepdims=True)
+    last.close()
+
+
+def run_kernel(kernel, ident, outs, scratch, args, flops):
+    shapes = tuple(jax.ShapeDtypeStruct(shape, dtype) for shape, dtype in outs)
+    moved = sum(a.size * a.dtype.itemsize for a in args) + sum(
+        math.prod(a.shape) * a.dtype.itemsize for a in shapes
+    )
+    return pl.pallas_call(
+        kernel,
+        out_shape=shapes,
+        in_specs=[VMEM] * len(args),
+        out_specs=tuple([VMEM] * len(outs)),
+        scratch_shapes=scratch,
+        cost_estimate=pl.CostEstimate(flops=flops, bytes_accessed=moved, transcendentals=0),
+        compiler_params=pltpu.CompilerParams(
+            collective_id=ident, has_side_effects=True, vmem_limit_bytes=VMEM_BYTES
+        ),
+    )(*args)
+
+
+def blocks(array):
+    return array.reshape((4, array.shape[0] // 4) + array.shape[1:])
+
+
+def flat(array):
+    return array.reshape((array.shape[0] * array.shape[1],) + array.shape[2:])
+
+
+def halve(array, axis):
+    size = lax.axis_size(axis)
+    index = lax.axis_index(axis)
+    pieces = array.reshape((size, array.shape[0] // size) + array.shape[1:])
+    distance = 1
+    while distance < size:
+        bit = (index // distance) % 2
+        pairs = pieces.reshape((pieces.shape[0] // 2, 2) + pieces.shape[1:])
+        keep = lax.dynamic_index_in_dim(pairs, bit, axis=1, keepdims=False)
+        give = lax.dynamic_index_in_dim(pairs, 1 - bit, axis=1, keepdims=False)
+        got = lax.ppermute(give, axis, [(i, i ^ distance) for i in range(size)])
+        pieces = (keep.astype(FULL) + got.astype(FULL)).astype(array.dtype)
+        distance *= 2
+    return pieces[0]
+
+
+def scatter_sums(parts):
+    whole = jnp.concatenate([part.astype(LOW) for part in parts], axis=1)
+    mine = halve(whole, "seq").astype(FULL)
+    out = []
+    first = 0
+    for part in parts:
+        out.append(mine[:, first : first + part.shape[1]])
+        first += part.shape[1]
+    return out
+
+
+def scatter_gains(gains):
+    count = lax.axis_size("tensor")
+    n_seq = lax.axis_size("seq")
+    shaped = gains.reshape(4, n_seq, -1).transpose(1, 0, 2)
+    mine = halve(shaped, "seq")
+    distance = 1
+    while distance < count:
+        mine = mine + lax.ppermute(mine, "tensor", [(i, i ^ distance) for i in range(count)])
+        distance *= 2
+    width = mine.shape[-1] // count
+    return lax.dynamic_slice_in_dim(mine[0] if mine.ndim == 3 else mine, lax.axis_index("tensor") * width, width, 1)
 
 
 def on_device(
@@ -396,72 +812,120 @@
     stretch_start = position * stretch
     flags = start_flags(seq_lengths, stretch, n_seq)
     place = (seq_lengths, stretch_start, stretch, position, n_seq, flags)
-    first_attn = (query_one, key_one, value_one, out_one)
-    second_attn = (query_two, key_two, value_two, out_two)
-    start = inputs.astype(jnp.float32)
-    middle_one, kept_one = attention_forward(
-        start, norm_gains[0], first_attn, taylor_forward, place, rows
-    )
-    layer_out, kept_two = mlp_forward(middle_one, norm_gains[1], gate_one, up_one, down_one, rows)
-    middle_two, kept_three = attention_forward(
-        layer_out, norm_gains[2], second_attn, window_forward, place, rows
-    )
-    result, kept_four = mlp_forward(middle_two, norm_gains[3], gate_two, up_two, down_two, rows)
-    grad = cotangent.astype(jnp.float32)
-    grad, gain_four, feed_two = mlp_backward(
-        grad, kept_four, norm_gains[3], gate_two, up_two, down_two, rows
-    )
-    grad, gain_three, attn_two = attention_backward(
-        grad, kept_three, norm_gains[2], second_attn, window_backward, place, rows
-    )
-    grad, gain_two, feed_one = mlp_backward(
-        grad, kept_two, norm_gains[1], gate_one, up_one, down_one, rows
-    )
-    grad, gain_one, attn_one = attention_backward(
-        grad, kept_one, norm_gains[0], first_attn, taylor_backward, place, rows
-    )
-    summed = (
-        lax.psum_scatter(attn_one[0], "seq", scatter_dimension=0, tiled=True),
-        lax.psum_scatter(attn_one[1], "seq", scatter_dimension=0, tiled=True),
-        lax.psum_scatter(attn_one[2], "seq", scatter_dimension=0, tiled=True),
-        lax.psum_scatter(attn_one[3], "seq", scatter_dimension=1, tiled=True),
-        lax.psum_scatter(feed_one[0], "seq", scatter_dimension=0, tiled=True),
-        lax.psum_scatter(feed_one[1], "seq", scatter_dimension=0, tiled=True),
-        lax.psum_scatter(feed_one[2], "seq", scatter_dimension=1, tiled=True),
-        lax.psum_scatter(attn_two[0], "seq", scatter_dimension=0, tiled=True),
-        lax.psum_scatter(attn_two[1], "seq", scatter_dimension=0, tiled=True),
-        lax.psum_scatter(attn_two[2], "seq", scatter_dimension=0, tiled=True),
-        lax.psum_scatter(attn_two[3], "seq", scatter_dimension=1, tiled=True),
-        lax.psum_scatter(feed_two[0], "seq", scatter_dimension=0, tiled=True),
-        lax.psum_scatter(feed_two[1], "seq", scatter_dimension=0, tiled=True),
-        lax.psum_scatter(feed_two[2], "seq", scatter_dimension=1, tiled=True),
-    )
-    sums_one = summed[:7]
-    sums_two = summed[7:]
-    gains = lax.psum_scatter(
-        jnp.stack([gain_one, gain_two, gain_three, gain_four]),
-        ("seq", "tensor"),
-        scatter_dimension=1,
-        tiled=True,
-    )
+    width = inputs.shape[1]
+    units = gate_one.shape[1]
+    cols = value_one.shape[1]
+    small = query_one.shape[1]
+    wide = (4, rows, width)
+    own = (2, rows, width)
+    total = total_scratch(rows, width)
+    share = share_scratch(rows, width)
+    one_flops = 2 * stretch * width
+
+    start, normed_one, cot, query1, key1, value1 = run_kernel(
+        enter_kernel,
+        0,
+        [(own, FULL), (wide, LOW), (wide, LOW)] + [((4, rows, n), LOW) for n in (small, small, cols)],
+        [pltpu.VMEM((rows, width), LOW)] * 2 + share + share + [pltpu.SemaphoreType.DMA((4,))],
+        (inputs, cotangent, norm_gains, query_one, key_one, value_one),
+        one_flops * (2 * small + cols),
+    )
+    query1, key1, value1 = flat(query1), flat(key1), flat(value1)
+    mixed, saved_one = taylor_forward(query1, key1, value1, place)
+    mixed_one = mixed.astype(LOW)
+    middle_one, after_one, normed_two, normed_three, gate1, up1, hidden_one, query2, key2, value2 = run_kernel(
+        forward_kernel,
+        1,
+        [(own, FULL), (own, FULL), (wide, LOW), (wide, LOW)]
+        + [((4, rows, units), kind) for kind in (FULL, FULL, LOW)]
+        + [((4, rows, cols), LOW)] * 3,
+        total + total + share + share,
+        (blocks(mixed_one), out_one, start, norm_gains, gate_one, up_one, down_one, query_two, key_two, value_two),
+        one_flops * (4 * cols + 3 * units),
+    )
+    query2, key2, value2 = flat(query2), flat(key2), flat(value2)
+    mixed, saved_two = window_forward(query2, key2, value2, place)
+    mixed_two = mixed.astype(LOW)
+    result, grad, grad_three, d_mixed_two, normed_four, hidden_two, d_gate2, d_up2, gain_four = run_kernel(
+        turn_kernel,
+        2,
+        [((rows, width), LOW), (own, FULL), (wide, LOW), ((4, rows, cols), LOW), (wide, LOW)]
+        + [((4, rows, units), LOW)] * 3
+        + [((1, width), FULL)],
+        total + total + total + share + share + [pltpu.VMEM(own, FULL)],
+        (blocks(mixed_two), out_two, after_one, norm_gains, gate_two, up_two, down_two, cot),
+        one_flops * (2 * cols + 6 * units),
+    )
+    feed_two = scatter_sums(
+        (
+            inner(flat(normed_four), flat(d_gate2)),
+            inner(flat(normed_four), flat(d_up2)),
+            inner(flat(cot), flat(hidden_two)),
+        )
+    )
+    d_query2, d_key2, d_value2 = window_backward(flat(d_mixed_two), query2, key2, value2, saved_two, place)
+    attn_two = scatter_sums(
+        (
+            inner(flat(normed_three), d_query2),
+            inner(flat(normed_three), d_key2),
+            inner(flat(normed_three), d_value2),
+            inner(flat(grad_three), mixed_two),
+        )
+    )
+    grad, grad_two, grad_one, d_gate1, d_up1, d_mixed_one, gains_mid = run_kernel(
+        backward_kernel,
+        3,
+        [(own, FULL), (wide, LOW), (wide, LOW)]
+        + [((4, rows, units), LOW)] * 2
+        + [((4, rows, cols), LOW), ((2, width), FULL)],
+        total + total + share + share,
+        (blocks(d_query2), blocks(d_key2), blocks(d_value2), query_two, key_two, value_two)
+        + (after_one, middle_one, grad, norm_gains, gate1, up1, gate_one, up_one, down_one, out_one),
+        one_flops * (4 * cols + 3 * units),
+    )
+    feed_one = scatter_sums(
+        (
+            inner(flat(normed_two), flat(d_gate1)),
+            inner(flat(normed_two), flat(d_up1)),
+            inner(flat(grad_two), flat(hidden_one)),
+        )
+    )
+    d_query1, d_key1, d_value1 = taylor_backward(flat(d_mixed_one), query1, key1, value1, saved_one, place)
+    attn_one = scatter_sums(
+        (
+            inner(flat(normed_one), d_query1),
+            inner(flat(normed_one), d_key1),
+            inner(flat(normed_one), d_value1),
+            inner(flat(grad_one), mixed_one),
+        )
+    )
+    grad, gain_one = run_kernel(
+        leave_kernel,
+        4,
+        [((rows, width), FULL), ((1, width), FULL)],
+        total,
+        (blocks(d_query1), blocks(d_key1), blocks(d_value1), query_one, key_one, value_one, start, grad, norm_gains),
+        one_flops * (2 * small + cols),
+    )
+    gains = scatter_gains(jnp.concatenate([gain_one, gains_mid, gain_four]))
     return (
-        result.astype(jnp.bfloat16),
+        result,
         grad,
         gains,
-        sums_one[0],
-        sums_one[1],
-        sums_one[2],
-        sums_one[3],
-        sums_one[4],
-        sums_one[5],
-        sums_one[6],
-        sums_two[0],
-        sums_two[1],
-        sums_two[2],
-        sums_two[3],
-        sums_two[4],
-        sums_two[5],
-        sums_two[6],
+        attn_one[0],
+        attn_one[1],
+        attn_one[2],
+        attn_one[3].T,
+        feed_one[0],
+        feed_one[1],
+        feed_one[2].T,
+        attn_two[0],
+        attn_two[1],
+        attn_two[2],
+        attn_two[3].T,
+        feed_two[0],
+        feed_two[1],
+        feed_two[2].T,
     )
 
 

time: 1770 us -> 694 us (0.39)
  waiting for transfers between devices: 1430 us -> 124 us
  Pallas kernels: 0 us -> 150 us
  local copies, waits for them, and re-layouts: 39.3 us -> 154 us
  matrix products: 159 us -> 93.6 us
  blocking collectives: 61.4 us -> 92.1 us
    reduce_scatter x22 -> x0, waiting for transfers between devices: 1180 us -> none  [the longest x8 196 us: collect(): lax.psum_scatter(product(jnp.int32(0), rows * lax.axis_size('tensor')).as...]
    pallas_call x0 -> x5, Pallas kernels: none -> 150 us  [run_kernel(): pl.pallas_call(kernel, out_shape=shapes, in_specs=[VMEM] * len(args), out...]
    all_gather x8 -> x0, waiting for transfers between devices: 123 us -> none  [spread(): return lax.all_gather(part, 'tensor', axis=0, tiled=True)]
    ppermute x0 -> x17, waiting for transfers between devices: none -> 95.2 us  [the longest x15 95.2 us: halve(): got = lax.ppermute(give, axis, [(i, i ^ distance) for i in range(size)])]
    unnamed x34 -> x2, waiting for transfers between devices: 92.7 us -> 0.03 us
    dot_general x28 -> x0, matrix products: 58 us -> none  [the longest x14 30.8 us: through(): lax.dot_general(left, right, BACK_DIMS, preferred_element_type=jnp.float32)]
    dynamic_slice x0 -> x6, local copies, waits for them, and re-layouts: none -> 33.2 us  [the longest x5 32.6 us: halve(): keep = lax.dynamic_index_in_dim(pairs, bit, axis=1, keepdims=False)]
    all_gather x1, blocking collectives: 31 us -> 61 us  [pass_states(): lax.all_gather(shortened(norm_sum), 'seq', axis=0, tiled=True)]
  transfers between devices with their start and end apart: 37 -> 23, of which waited for: 33 -> 10; matrix products, arithmetic and copies ran while one was open for 6% -> 33% of each run, Pallas kernels for 0% -> 8%
where the time goes in v1:
time: 694 us; the launch traced here: 687 us
  local copies, waits for them, and re-layouts  154 us (22%)
  Pallas kernels  150 us (22%)
  waiting for transfers between devices  124 us (18%)
  matrix products  93.6 us (13%)
  blocking collectives  92.1 us (13%)
  other arithmetic  34.6 us (5%)
  starting transfers between devices  22.7 us (3%)
  between operations  16.1 us (2%)
    pallas_call x5, Pallas kernels, run_kernel(): pl.pallas_call(kernel, out_shape=shapes, in_specs=[VMEM] * len(args), out...  150 us
    ppermute x15, waiting for transfers between devices, halve(): got = lax.ppermute(give, axis, [(i, i ^ distance) for i in range(size)])  95.2 us
    all_gather x1, blocking collectives, pass_states(): lax.all_gather(shortened(norm_sum), 'seq', axis=0, tiled=True)  61 us
    unnamed x182, local copies, waits for them, and re-layouts  46.4 us
    dynamic_slice x5, local copies, waits for them, and re-layouts, halve(): keep = lax.dynamic_index_in_dim(pairs, bit, axis=1, keepdims=False)  32.6 us
    all_gather x1, blocking collectives, pass_states(): lax.all_gather(norm_sum.astype(jnp.bfloat16), 'seq', axis=0, tiled=True)  31.1 us
    another operation x4, local copies, waits for them, and re-layouts, halve(): pairs = pieces.reshape((pieces.shape[0] // 2, 2) + pieces.shape[1:])  28.6 us
    ppermute x4, waiting for transfers between devices, from_behind(): return lax.ppermute(block, axis, route)  28.5 us
  transfers between devices with their start and end apart: 23, of which 10 were waited for; matrix products, arithmetic and copies ran while one was open for 33% of the time, Pallas kernels for 8%

profile of v1, /device:TPU:0, one launch (start us, length us, event | category | flops | bytes accessed | tf_op | source)
XLA Modules:
  0.0 687.1 jit_solution(4528454299646806529)
XLA Ops:
  12.9 20.2 %shard_map.315 = (f32[2,128,1024]{2,1,0:T(8,128)}, bf16[4,128,1024]{2,1,0:T(8,128)(2,1)}, bf16[4,128,1024]{2,1,0:T(8,128)(2,1)}, bf16[4,128,64]{2,1,0:T(8,128)(2...) custom-call(bf16[128,1024]{1,0:T(8,128)(2,1)} %inputs.1, bf16[128,1024]{1,0:T(8,128)(2,1)} %cotangent.1, ...), custom_call_target="tpu_custom_call" | custom-call | flops 402653184 | bytes 4866048 | tf_op jit(solution)/shard_map/pallas_call | solution.py:727
  41.5 31.1 %all-gather.1 = bf16[8,273,4]{1,2,0:T(4,128)(2,1)S(1)} all-gather(bf16[1,273,4]{1,2,0:T(4,128)(2,1)S(1)} %bitcast.411), channel_id=1, replica_groups=mesh['seq'=8,'tensor'=4] {'seq'}, dimensions={0}, use_global_device_ids=true | all-gather | bytes 19656 | tf_op jit(solution)/shard_map/all_gather | solution.py:120
  82.2 4.3 fusion.22
  88.5 3.3 fusion.23
  91.8 3.2 copy.264
  95.1 2.6 fusion.100
  97.7 4.7 fusion.124
  103.4 36.4 %shard_map.316 = (f32[2,128,1024]{2,1,0:T(8,128)}, f32[2,128,1024]{2,1,0:T(8,128)}, bf16[4,128,1024]{2,1,0:T(8,128)(2,1)}, bf16[4,128,1024]{2,1,0:T(8,128)(2,1)}...) custom-call(bf16[4,128,256]{2,1,0:T(8,128)(2,1)} %copy.265.mixed, ...), custom_call_target="tpu_custom_call" | custom-call | flops 3238002688 | bytes 16154624 | tf_op jit(solution)/shard_map/pallas_call | solution.py:727
  140.6 3.4 collective-permute-start.1
  147.8 2.6 copy.275.w_up
  159.3 3.3 fusion.37
  163.6 41.2 %shard_map.317 = (bf16[128,1024]{1,0:T(8,128)(2,1)}, f32[2,128,1024]{2,1,0:T(8,128)}, bf16[4,128,1024]{2,1,0:T(8,128)(2,1)}, bf16[4,128,256]{2,1,0:T(8,128)(2,1)...) custom-call(bf16[4,128,256]{2,1,0:T(8,128)(2,1)} %copy.273.mixed, ...), custom_call_target="tpu_custom_call" | custom-call | flops 4865392640 | bytes 12914688 | tf_op jit(solution)/shard_map/pallas_call | solution.py:727
  206.0 3.3 fusion.28
  209.4 3.9 multiply_reduce_fusion
  213.3 3.7 convolution_convert_fusion.6
  217.0 4.2 convolution_bitcast_fusion
  227.9 11.2 %reshape_reshape.28 = bf16[4,2,128,2064]{2,1,0,3:T(2,128)(2,1)} reshape(bf16[1024,2064]{0,1:T(8,128)(2,1)} %pad_maximum_fusion.1) | data formatting | bytes 8454144 | tf_op jit(solution)/shard_map/reshape;reshape | solution.py:755
  239.1 11.3 %constant_dynamic-slice_fusion.2 = (bf16[4,1,128,2064]{2,1,0,3:T(2,128)(2,1)}, bf16[4,1,128,2064]{2,1,0,3:T(2,128)(2,1)S(1)}) fusion(bf16[4,2,128,2064]{2,1,0,3:T(2,128)(2,1)} %reshape_reshape.28, s32[]{:T(128)S(6)} %select_n.148, s32[]{:T(128)S(6)} %select_n.149), kind=kLoop, calls=%fused_computation.172 | loop fusion | bytes 8454152 | tf_op jit(solution)/shard_map/jit(dynamic_index_in_dim)/dynamic_slice | solution.py:756
  252.1 2.6 collective-permute-start.18
  273.5 28.5 %collective-permute-done.2 = bf16[63,4,64]{0,2,1:T(8,128)(2,1)} collective-permute-done((bf16[63,4,64]{0,2,1:T(8,128)(2,1)S(1)}, bf16[63,4,64]{0,2,1:T(8,128)(2,1)}, u32[]{:S(2)}, u32[]{:S(2)}) %collective-permute-start.2) | collective-permute-done | bytes 32288 | tf_op jit(solution)/shard_map/ppermute | solution.py:30
  308.4 38.7 %shard_map.318 = (f32[2,128,1024]{2,1,0:T(8,128)}, bf16[4,128,1024]{2,1,0:T(8,128)(2,1)}, bf16[4,128,1024]{2,1,0:T(8,128)(2,1)}, bf16[4,128,688]{2,1,0:T(8,128)(...) custom-call(bf16[4,128,256]{2,1,0:T(8,128)(2,1)} %copy.277.d_query, ...), custom_call_target="tpu_custom_call" | custom-call | flops 3238002688 | bytes 17915904 | tf_op jit(solution)/shard_map/pallas_call | solution.py:727
  351.1 5.0 fusion.41
  359.4 2.8 pad_maximum_fusion.4
  362.2 4.9 reshape_reshape.27
  374.3 11.3 %reshape_reshape.26 = bf16[4,2,128,2064]{2,1,0,3:T(2,128)(2,1)} reshape(bf16[1024,2064]{0,1:T(8,128)(2,1)} %pad_maximum_fusion) | data formatting | bytes 8454144 | tf_op jit(solution)/shard_map/reshape;reshape | solution.py:755
  390.3 6.3 constant_dynamic-slice_fusion.5
  396.6 5.8 copy.345
  402.4 11.2 %constant_dynamic-slice_fusion.8 = (bf16[4,1,128,2064]{2,1,0,3:T(2,128)(2,1)}, bf16[4,1,128,2064]{2,1,0,3:T(2,128)(2,1)S(1)}) fusion(bf16[4,2,128,2064]{2,1,0,3:T(2,128)(2,1)} %reshape_reshape.26, s32[]{:T(128)S(6)} %select_n.148, s32[]{:T(128)S(6)} %select_n.149), kind=kLoop, calls=%fused_computation.178 | loop fusion | bytes 8454152 | tf_op jit(solution)/shard_map/jit(dynamic_index_in_dim)/dynamic_slice | solution.py:756
  418.5 6.0 copy.344
  424.6 4.8 select_multiply_fusion
  429.4 3.4 fusion.57
  438.3 61.0 %all-gather.3 = bf16[8,273,4]{1,2,0:T(4,128)(2,1)S(1)} all-gather(bf16[1,273,4]{1,2,0:T(4,128)(2,1)S(1)} %bitcast.412), channel_id=1, replica_groups=mesh['seq'=8,'tensor'=4] {'seq'}, dimensions={0}, use_global_device_ids=true | all-gather | bytes 19656 | tf_op jit(solution)/shard_map/all_gather | solution.py:111
  499.3 5.4 fusion.20
  511.4 3.8 collective-permute-done.17
  517.1 3.0 copy.287
  520.2 2.7 fusion.98
  522.9 2.8 fusion.36
  532.3 3.6 fusion.58
  536.7 13.7 %shard_map.319 = (f32[128,1024]{1,0:T(8,128)}, f32[1,1024]{1,0:T(1,128)}) custom-call(bf16[4,128,64]{2,1,0:T(8,128)(2,1)} %copy.289.d_query, bf16[4,128,64]{2,1,0:T(8,128)(2,1)} %copy.290.d_key, bf16[4,128,256]{2,1,0:T(8,128)(2,1)} %copy.291.d_value, bf16[1024,64]{1,0:T(8,128)(2,1)} %copy.257.w_query, bf16[1024,64]{1,0:T(8,128)(2,1)} %copy.258.w_key, ...), custom_call_target="tpu_custom_call" | custom-call | flops 402653184 | bytes 3821568 | tf_op jit(solution)/shard_map/pallas_call | solution.py:727
  555.5 3.1 collective-permute-done.5
  559.6 3.5 collective-permute-done.6
  565.3 3.7 constant_dynamic-slice_fusion.11
  576.0 3.4 fusion
  579.6 10.9 %collective-permute-done.9 = bf16[4,128,640]{2,1,0:T(8,128)(2,1)S(1)} collective-permute-done((bf16[4,128,640]{2,1,0:T(8,128)(2,1)S(1)}, bf16[4,128,640]{2,1,0:T(8,128)(2,1)S(1)}, u32[]{:S(2)}, u32[]{:S(2)}) %collective-permute-start.9) | collective-permute-done | bytes 655392 | tf_op jit(solution)/shard_map/ppermute | solution.py:758
  592.8 19.0 %collective-permute-done.10 = bf16[2,128,640]{2,1,0:T(8,128)(2,1)S(1)} collective-permute-done((bf16[2,128,640]{2,1,0:T(8,128)(2,1)S(1)}, bf16[2,128,640]{2,1,0:T(8,128)(2,1)S(1)}, u32[]{:S(2)}, u32[]{:S(2)}) %collective-permute-start.10) | collective-permute-done | bytes 327712 | tf_op jit(solution)/shard_map/ppermute | solution.py:758
  614.0 7.7 %collective-permute-done.11 = bf16[1,128,640]{2,1,0:T(8,128)(2,1)S(1)} collective-permute-done((bf16[1,128,640]{2,1,0:T(8,128)(2,1)S(1)}, bf16[1,128,640]{2,1,0:T(8,128)(2,1)S(1)}, u32[]{:S(2)}, u32[]{:S(2)}) %collective-permute-start.11) | collective-permute-done | bytes 163872 | tf_op jit(solution)/shard_map/ppermute | solution.py:758
  626.6 24.4 %collective-permute-done.13 = bf16[2,128,2064]{1,2,0:T(8,128)(2,1)} collective-permute-done((bf16[2,128,2064]{1,2,0:T(8,128)(2,1)S(1)}, bf16[2,128,2064]{1,2,0:T(8,128)(2,1)}, u32[]{:S(2)}, u32[]{:S(2)}) %collective-permute-start.13) | collective-permute-done | bytes 1056800 | tf_op jit(solution)/shard_map/ppermute | solution.py:758
  654.5 22.7 %collective-permute-done.14 = bf16[1,128,2064]{1,2,0:T(8,128)(2,1)S(1)} collective-permute-done((bf16[1,128,2064]{1,2,0:T(8,128)(2,1)S(1)}, bf16[1,128,2064]{1,2,0:T(8,128)(2,1)S(1)}, u32[]{:S(2)}, u32[]{:S(2)}) %collective-permute-start.14) | collective-permute-done | bytes 528416 | tf_op jit(solution)/shard_map/ppermute | solution.py:758
  (360 shorter events, 151.3 us)
Async XLA Ops:
  7.2 84.6 %all-gather.7.cloned.1.call-start = ((), (), s32[]{:S(2)}) async-start(), calls=%async_computation | async-start | bytes 1290240 | tf_op jit(solution)/shard_map/all_gather | solution.py:117
  34.3 52.3 %copy-start.17 = (bf16[512,4,64]{0,2,1:T(8,128)(2,1)}, bf16[512,4,64]{0,2,1:T(8,128)(2,1)S(1)}, u32[]{:S(2)}) copy-start(bf16[512,4,64]{0,2,1:T(8,128)(2,1)S(1)} %reshape.648) | copy-start | bytes 786436
  35.9 61.8 %copy-start.53 = (f32[273]{0:T(512)}, f32[273]{0:T(512)S(1)}, u32[]{:S(2)}) copy-start(f32[273]{0:T(512)S(1)} %pad.34.clone) | copy-start | bytes 3280
  37.3 60.4 %copy-start.57 = (f32[512]{0:T(512)}, f32[512]{0:T(512)S(1)}, u32[]{:S(2)}) copy-start(f32[512]{0:T(512)S(1)} %get-tuple-element.264) | copy-start | bytes 6148
  39.7 477.4 %all-gather.9.cloned.1.call-start = ((), (), s32[]{:S(2)}) async-start(), calls=%async_computation.1 | async-start | bytes 1290240 | tf_op jit(solution)/shard_map/all_gather | solution.py:110
  102.5 37.4 %copy-start.30 = (bf16[512,4,64]{0,2,1:T(8,128)(2,1)}, bf16[512,4,64]{0,2,1:T(8,128)(2,1)S(1)}, u32[]{:S(2)}) copy-start(bf16[512,4,64]{0,2,1:T(8,128)(2,1)S(1)} %get-tuple-element.269) | copy-start | bytes 786436
  140.6 13.8 %collective-permute-start.1 = (bf16[63,256]{1,0:T(8,128)(2,1)S(1)}, bf16[63,256]{1,0:T(8,128)(2,1)S(1)}, u32[]{:S(2)}, u32[]{:S(2)}) collective-permute-start(bf16[63,256]{1,0:T(8,128)(2,1)S(1)} %slice.188), channel_id=1, source_target_pairs={{0,4},{4,8},{8,12},{12,16},{16,20},{20,24},{24,28},{1,5},{5,9},{9,... | collective-permute-start | bytes 96776 | tf_op jit(solution)/shard_map/ppermute | solution.py:30
  152.1 7.0 %collective-permute-start = (bf16[63,256]{1,0:T(8,128)(2,1)S(1)}, bf16[63,256]{1,0:T(8,128)(2,1)S(1)}, u32[]{:S(2)}, u32[]{:S(2)}) collective-permute-start(bf16[63,256]{1,0:T(8,128)(2,1)S(1)} %slice.187), channel_id=1, source_target_pairs={{0,4},{4,8},{8,12},{12,16},{16,20},{20,24},{24,28},{1,5},{5,9},{9,... | collective-permute-start | bytes 96776 | tf_op jit(solution)/shard_map/ppermute | solution.py:30
  162.6 42.1 %copy-start.32 = (bf16[4,64,512]{2,1,0:T(8,128)(2,1)}, bf16[4,64,512]{2,1,0:T(8,128)(2,1)S(1)}, u32[]{:S(2)}) copy-start(bf16[4,64,512]{2,1,0:T(8,128)(2,1)S(1)} %fusion.37) | copy-start | bytes 786436
  209.3 12.8 %copy-start.25 = (f32[575,4,64]{0,2,1:T(8,128)}, f32[575,4,64]{0,2,1:T(8,128)S(1)}, u32[]{:S(2)}) copy-start(f32[575,4,64]{0,2,1:T(8,128)S(1)} %fusion.28) | copy-start | bytes 1766404
  222.2 42.7 %collective-permute-start.3 = (bf16[63,4,64]{0,2,1:T(8,128)(2,1)S(1)}, bf16[63,4,64]{0,2,1:T(8,128)(2,1)}, u32[]{:S(2)}, u32[]{:S(2)}) collective-permute-start(bf16[63,4,64]{0,2,1:T(8,128)(2,1)S(1)} %slice.224), channel_id=1, source_target_pairs={{4,0},{8,4},{12,8},{16,12},{20,16},{24,20},{28,24},{5,1},{9,5},{13... | collective-permute-start | bytes 96776 | tf_op jit(solution)/shard_map/ppermute | solution.py:30
  252.1 323.9 %collective-permute-start.18 = (bf16[4,128,2064]{1,2,0:T(8,128)(2,1)}, bf16[4,128,2064]{1,2,0:T(8,128)(2,1)}, u32[]{:S(2)}, u32[]{:S(2)}) collective-permute-start(bf16[4,128,2064]{1,2,0:T(8,128)(2,1)} %bitcast.345), channel_id=1, source_target_pairs={{0,4},{4,0},{8,12},{12,8},{16,20},{20,16},{24,28},{28,24},{1,5},{5... | collective-permute-start | bytes 6340616 | tf_op jit(solution)/shard_map/ppermute | solution.py:758
  260.1 41.9 %collective-permute-start.2 = (bf16[63,4,64]{0,2,1:T(8,128)(2,1)S(1)}, bf16[63,4,64]{0,2,1:T(8,128)(2,1)}, u32[]{:S(2)}, u32[]{:S(2)}) collective-permute-start(bf16[63,4,64]{0,2,1:T(8,128)(2,1)S(1)} %slice.225), channel_id=1, source_target_pairs={{4,0},{8,4},{12,8},{16,12},{20,16},{24,20},{28,24},{5,1},{9,5},{13... | collective-permute-start | bytes 96776 | tf_op jit(solution)/shard_map/ppermute | solution.py:30
  308.4 42.7 %copy-start.54 = (f32[273]{0:T(512)S(1)}, f32[273]{0:T(512)}, u32[]{:S(2)}) copy-start(f32[273]{0:T(512)} %copy-done.53) | copy-start | bytes 3280
  308.4 42.7 %copy-start.58 = (f32[512]{0:T(512)S(1)}, f32[512]{0:T(512)}, u32[]{:S(2)}) copy-start(f32[512]{0:T(512)} %copy-done.57) | copy-start | bytes 6148
  374.3 11.3 %copy-start.12 = (f32[512,4,64]{0,2,1:T(8,128)S(1)}, f32[512,4,64]{0,2,1:T(8,128)}, u32[]{:S(2)}) copy-start(f32[512,4,64]{0,2,1:T(8,128)} %reshape.670) | copy-start | bytes 1572868
  374.3 11.3 %copy-start.47 = (f32[1,273,4,64]{1,0,3,2:T(1,128)S(1)}, f32[1,273,4,64]{1,0,3,2:T(1,128)}, u32[]{:S(2)}) copy-start(f32[1,273,4,64]{1,0,3,2:T(1,128)} %copy-done.46) | copy-start | bytes 838660
  374.3 11.3 %copy-start.56 = (f32[1,273,4]{1,2,0:T(4,128)S(1)}, f32[1,273,4]{1,2,0:T(4,128)}, u32[]{:S(2)}) copy-start(f32[1,273,4]{1,2,0:T(4,128)} %copy-done.55) | copy-start | bytes 13108
  402.4 30.4 %collective-permute-start.15 = (bf16[4,128,1024]{2,1,0:T(8,128)(2,1)}, bf16[4,128,1024]{2,1,0:T(8,128)(2,1)}, u32[]{:S(2)}, u32[]{:S(2)}) collective-permute-start(bf16[4,128,1024]{2,1,0:T(8,128)(2,1)} %bitcast.388), channel_id=1, source_target_pairs={{0,4},{4,0},{8,12},{12,8},{16,20},{20,16},{24,28},{28,24},{1,5},{5... | collective-permute-start | bytes 3145736 | tf_op jit(solution)/shard_map/ppermute | solution.py:758
  415.2 175.5 %collective-permute-start.12 = (bf16[4,128,2064]{1,2,0:T(8,128)(2,1)}, bf16[4,128,2064]{1,2,0:T(8,128)(2,1)}, u32[]{:S(2)}, u32[]{:S(2)}) collective-permute-start(bf16[4,128,2064]{1,2,0:T(8,128)(2,1)} %bitcast.346), channel_id=1, source_target_pairs={{0,4},{4,0},{8,12},{12,8},{16,20},{20,16},{24,28},{28,24},{1,5},{5... | collective-permute-start | bytes 6340616 | tf_op jit(solution)/shard_map/ppermute | solution.py:758
  417.3 7.3 %copy-start.29 = (pred[512,512]{0,1:T(8,128)(4,1)S(1)}, pred[512,512]{0,1:T(8,128)(4,1)}, u32[]{:S(2)}) copy-start(pred[512,512]{0,1:T(8,128)(4,1)} %copy-done.28) | copy-start | bytes 786436
  432.8 66.5 %copy-start.15 = (f32[4,512,512]{1,2,0:T(8,128)S(1)}, f32[4,512,512]{1,2,0:T(8,128)}, u32[]{:S(2)}) copy-start(f32[4,512,512]{1,2,0:T(8,128)} %copy-done.14) | copy-start | bytes 12582916
  434.7 70.1 %collective-permute-start.16 = (bf16[2,128,1024]{2,1,0:T(8,128)(2,1)S(1)}, bf16[2,128,1024]{2,1,0:T(8,128)(2,1)S(1)}, u32[]{:S(2)}, u32[]{:S(2)}) collective-permute-start(bf16[2,128,1024]{2,1,0:T(8,128)(2,1)S(1)} %dynamic-slice_bitcast_fusion.2), channel_id=1, source_target_pairs={{0,8},{4,12},{8,0},{12,4},{16,24},{20,28},{24,16},{28,20},{1,9},{5... | collective-permute-start | bytes 1572872 | tf_op jit(solution)/shard_map/ppermute | solution.py:758
  506.5 8.7 %collective-permute-start.17 = (bf16[1,128,1024]{2,1,0:T(8,128)(2,1)}, bf16[1,128,1024]{2,1,0:T(8,128)(2,1)}, u32[]{:S(2)}, u32[]{:S(2)}) collective-permute-start(bf16[1,128,1024]{2,1,0:T(8,128)(2,1)} %constant_dynamic-slice_fusion.3), channel_id=1, source_target_pairs={{0,16},{4,20},{8,24},{12,28},{16,0},{20,4},{24,8},{28,12},{1,17},{... | collective-permute-start | bytes 786440 | tf_op jit(solution)/shard_map/ppermute | solution.py:758
  535.9 14.6 %copy-start.61 = (f32[2,1024]{1,0:T(2,128)S(1)}, f32[2,1024]{1,0:T(2,128)}, u32[]{:S(2)}) copy-start(f32[2,1024]{1,0:T(2,128)} %get-tuple-element.134) | copy-start | bytes 24580
  535.9 14.6 %copy-start.64 = (f32[1,1024]{1,0:T(1,128)S(1)}, f32[1,1024]{1,0:T(1,128)}, u32[]{:S(2)}) copy-start(f32[1,1024]{1,0:T(1,128)} %get-tuple-element.135) | copy-start | bytes 12292
  535.9 17.5 %copy-start.22 = (f32[128,1024]{1,0:T(8,128)S(1)}, f32[128,1024]{1,0:T(8,128)}, u32[]{:S(2)}) copy-start(f32[128,1024]{1,0:T(8,128)} %fusion.75) | copy-start | bytes 1572868
  536.7 18.3 %copy-start.20 = (bf16[4,64,512]{2,1,0:T(8,128)(2,1)S(1)}, bf16[4,64,512]{2,1,0:T(8,128)(2,1)}, u32[]{:S(2)}) copy-start(bf16[4,64,512]{2,1,0:T(8,128)(2,1)} %fusion.36) | copy-start | bytes 786436
  550.4 12.7 %copy-start.21 = (bf16[1024,256]{0,1:T(8,128)(2,1)S(1)}, bf16[1024,256]{0,1:T(8,128)(2,1)}, u32[]{:S(2)}) copy-start(bf16[1024,256]{0,1:T(8,128)(2,1)} %convolution_convert_fusion.4) | copy-start | bytes 1572868
  550.5 12.7 %copy-start.40 = (bf16[1024,64]{0,1:T(8,128)(2,1)S(1)}, bf16[1024,64]{0,1:T(8,128)(2,1)}, u32[]{:S(2)}) copy-start(bf16[1024,64]{0,1:T(8,128)(2,1)} %convolution_convert_fusion.8) | copy-start | bytes 393220
  551.3 3.7 collective-permute-start.4
  555.0 3.6 collective-permute-start.5
  558.7 4.5 collective-permute-start.6
  563.2 1.3 collective-permute-start.7
  564.5 10.8 %collective-permute-start.8 = (f32[1,4,128]{2,1,0:T(4,128)S(1)}, f32[1,4,128]{2,1,0:T(4,128)S(1)}, u32[]{:S(2)}, u32[]{:S(2)}) collective-permute-start(f32[1,4,128]{2,1,0:T(4,128)S(1)} %add.325), channel_id=1, source_target_pairs={{0,2},{1,3},{2,0},{3,1},{4,6},{5,7},{6,4},{7,5},{8,10},{9,11},{10,... | collective-permute-start | bytes 6152 | tf_op jit(solution)/shard_map/ppermute | solution.py:782
  573.3 17.2 %collective-permute-start.9 = (bf16[4,128,640]{2,1,0:T(8,128)(2,1)S(1)}, bf16[4,128,640]{2,1,0:T(8,128)(2,1)S(1)}, u32[]{:S(2)}, u32[]{:S(2)}) collective-permute-start(bf16[4,128,640]{2,1,0:T(8,128)(2,1)S(1)} %bitcast.394), channel_id=1, source_target_pairs={{0,4},{4,0},{8,12},{12,8},{16,20},{20,16},{24,28},{28,24},{1,5},{5... | collective-permute-start | bytes 1966088 | tf_op jit(solution)/shard_map/ppermute | solution.py:758
  576.0 14.8 %slice-start.2 = ((s8[4227072]{0:T(1024)(128)(4,1)}), s8[4194304]{0:T(1024)(128)(4,1)S(1)}, s32[]{:S(2)}) async-start(s8[4227072]{0:T(1024)(128)(4,1)} %bitcast.358), calls=%async_computation.4 | async-start | bytes 8388608
  576.0 14.8 %slice-start.3 = ((s8[4227072]{0:T(1024)(128)(4,1)}), s8[32768]{0:T(1024)(128)(4,1)S(1)}, s32[]{:S(2)}) async-start(s8[4227072]{0:T(1024)(128)(4,1)} %bitcast.358), calls=%async_computation.5 | async-start | bytes 65536
  579.4 11.3 %copy-start.6 = (bf16[4,128,2064]{1,2,0:T(8,128)(2,1)}, bf16[4,128,2064]{1,2,0:T(8,128)(2,1)S(1)}, u32[]{:S(2)}) copy-start(bf16[4,128,2064]{1,2,0:T(8,128)(2,1)S(1)} %fusion) | copy-start | bytes 6340612
  579.5 45.1 %collective-permute-start.19 = (bf16[2,128,2064]{1,2,0:T(8,128)(2,1)S(1)}, bf16[2,128,2064]{1,2,0:T(8,128)(2,1)}, u32[]{:S(2)}, u32[]{:S(2)}) collective-permute-start(bf16[2,128,2064]{1,2,0:T(8,128)(2,1)S(1)} %dynamic-slice_bitcast_fusion), channel_id=1, source_target_pairs={{0,8},{4,12},{8,0},{12,4},{16,24},{20,28},{24,16},{28,20},{1,9},{5... | collective-permute-start | bytes 3170312 | tf_op jit(solution)/shard_map/ppermute | solution.py:758
  590.7 21.1 %collective-permute-start.10 = (bf16[2,128,640]{2,1,0:T(8,128)(2,1)S(1)}, bf16[2,128,640]{2,1,0:T(8,128)(2,1)S(1)}, u32[]{:S(2)}, u32[]{:S(2)}) collective-permute-start(bf16[2,128,640]{2,1,0:T(8,128)(2,1)S(1)} %dynamic-slice_bitcast_fusion.3), channel_id=1, source_target_pairs={{0,8},{4,12},{8,0},{12,4},{16,24},{20,28},{24,16},{28,20},{1,9},{5... | collective-permute-start | bytes 983048 | tf_op jit(solution)/shard_map/ppermute | solution.py:758
  592.8 29.6 %copy-start.7 = (bf16[4,128,2064]{1,2,0:T(8,128)(2,1)}, bf16[4,128,2064]{1,2,0:T(8,128)(2,1)S(1)}, u32[]{:S(2)}) copy-start(bf16[4,128,2064]{1,2,0:T(8,128)(2,1)S(1)} %fusion.1) | copy-start | bytes 6340612
  611.9 9.8 %collective-permute-start.11 = (bf16[1,128,640]{2,1,0:T(8,128)(2,1)S(1)}, bf16[1,128,640]{2,1,0:T(8,128)(2,1)S(1)}, u32[]{:S(2)}, u32[]{:S(2)}) collective-permute-start(bf16[1,128,640]{2,1,0:T(8,128)(2,1)S(1)} %constant_dynamic-slice_fusion.9), channel_id=1, source_target_pairs={{0,16},{4,20},{8,24},{12,28},{16,0},{20,4},{24,8},{28,12},{1,17},{... | collective-permute-start | bytes 491528 | tf_op jit(solution)/shard_map/ppermute | solution.py:758
  612.2 38.8 %collective-permute-start.13 = (bf16[2,128,2064]{1,2,0:T(8,128)(2,1)S(1)}, bf16[2,128,2064]{1,2,0:T(8,128)(2,1)}, u32[]{:S(2)}, u32[]{:S(2)}) collective-permute-start(bf16[2,128,2064]{1,2,0:T(8,128)(2,1)S(1)} %dynamic-slice_bitcast_fusion.1), channel_id=1, source_target_pairs={{0,8},{4,12},{8,0},{12,4},{16,24},{20,28},{24,16},{28,20},{1,9},{5... | collective-permute-start | bytes 3170312 | tf_op jit(solution)/shard_map/ppermute | solution.py:758
  626.5 26.9 %collective-permute-start.20 = (bf16[1,128,2064]{1,2,0:T(8,128)(2,1)S(1)}, bf16[1,128,2064]{1,2,0:T(8,128)(2,1)S(1)}, u32[]{:S(2)}, u32[]{:S(2)}) collective-permute-start(bf16[1,128,2064]{1,2,0:T(8,128)(2,1)S(1)} %constant_dynamic-slice_fusion), channel_id=1, source_target_pairs={{0,16},{4,20},{8,24},{12,28},{16,0},{20,4},{24,8},{28,12},{1,17},{... | collective-permute-start | bytes 1585160 | tf_op jit(solution)/shard_map/ppermute | solution.py:758
  652.8 24.4 %collective-permute-start.14 = (bf16[1,128,2064]{1,2,0:T(8,128)(2,1)S(1)}, bf16[1,128,2064]{1,2,0:T(8,128)(2,1)S(1)}, u32[]{:S(2)}, u32[]{:S(2)}) collective-permute-start(bf16[1,128,2064]{1,2,0:T(8,128)(2,1)S(1)} %constant_dynamic-slice_fusion.6), channel_id=1, source_target_pairs={{0,16},{4,20},{8,24},{12,28},{16,0},{20,4},{24,8},{28,12},{1,17},{... | collective-permute-start | bytes 1585160 | tf_op jit(solution)/shard_map/ppermute | solution.py:758
  654.5 23.8 %copy-start.50 = (bf16[128,1024]{1,0:T(8,128)(2,1)S(1)}, bf16[128,1024]{1,0:T(8,128)(2,1)}, u32[]{:S(2)}) copy-start(bf16[128,1024]{1,0:T(8,128)(2,1)} %get-tuple-element.296) | copy-start | bytes 786436
  654.5 24.5 %copy-start.44 = (f32[128,1024]{1,0:T(8,128)S(1)}, f32[128,1024]{1,0:T(8,128)}, u32[]{:S(2)}) copy-start(f32[128,1024]{1,0:T(8,128)} %get-tuple-element.297) | copy-start | bytes 1572868
  (55 other events, 214.2 us)
Sparse Core Ops, SparseCore 0:
  39.8 41.7 all-gather.6
  358.1 42.8 all-gather.8

commit v2 on v0

v2 whole, which is shorter than its diff:
```python
import functools
import math
import types

import jax
import jax.numpy as jnp
import numpy as np
from jax import lax
from jax.experimental import pallas as pl
from jax.experimental.pallas import tpu as pltpu
from jax.sharding import PartitionSpec as P

FEAT = 16
HEAD = 64
WINDOW = 64
BLOCK = 128
EPS = 1e-05
FLOOR_SCORE = -1e30
MESH = pl.DeviceIdType.MESH
LOW = jnp.bfloat16
FULL = jnp.float32
VMEM_BYTES = 60 * 1024 * 1024
HALF = BLOCK // 2
CHUNKS = 4
PAIRS = [(a, b) for a in range(FEAT + 1) for b in range(a, FEAT + 1)]
FEATS = -(-len(PAIRS) // 16) * 16
NORM_ROWS = 16


def plain(left, right):
    return jnp.dot(left, right, preferred_element_type=FULL)


def inner(left, right):
    return lax.dot_general(left, right, (((0,), (0,)), ((), ())), preferred_element_type=FULL)


def through(left, right):
    return lax.dot_general(left, right, (((1,), (1,)), ((), ())), preferred_element_type=FULL)


def flat(array):
    return array.reshape((math.prod(array.shape[:-1]), array.shape[-1]))


class Group:
    def __init__(self):
        index = lax.axis_index("tensor")
        self.index = index
        self.low = lax.rem(index, 2)
        self.high = index // 2
        self.pair = dict(tensor=index + 1 - 2 * self.low)
        self.partner = dict(tensor=lax.rem(index + 2, 4))

    def mine(self, chunk):
        return jnp.where(self.high == chunk // 2, 1.0, 0.0)

    def split(self, part, count, by_rows=False):
        if by_rows:
            zero, one = part.reshape(2, count, HALF, -1)
        else:
            whole = part.reshape(count, 2, HALF, -1)
            zero, one = whole[:, 0], whole[:, 1]
        even = self.low == 0
        return jnp.where(even, zero, one), jnp.where(even, one, zero)

    def own_rows(self, ref, chunk, count):
        return ref.at[self.low + 2 * (chunk // 2), pl.ds(chunk % 2, count)]

    def own_chunks(self, ref, chunk, count):
        return ref.at[pl.ds(chunk, count), self.low]


def chunk_rows(ref, chunk, count=1):
    first, half = 2 * (chunk // 2), chunk % 2
    if len(ref.shape) == 4:
        return flat(ref[first : first + 2, half : half + count])
    starts = [block * BLOCK + half * HALF for block in (first, first + 1)]
    return jnp.concatenate([ref[start : start + count * HALF] for start in starts], axis=0)


def put_rows(ref, chunk, value, ahead=0):
    for side in range(2):
        start = ahead + (2 * (chunk // 2) + side) * BLOCK + chunk % 2 * HALF
        ref[start : start + HALF] = value[side * HALF : (side + 1) * HALF]


class Line:
    def __init__(self, size):
        self.size = size
        self.index = lax.axis_index("seq")
        self.after = dict(seq=lax.rem(self.index + 1, size))
        self.before = dict(seq=lax.rem(self.index + size - 1, size))

    def flip(self, relative):
        found = 0
        bit = 1
        while bit < self.size:
            found = found + bit * lax.rem(self.index // bit + relative // bit, 2)
            bit *= 2
        return found


def greet(peers, everyone=None):
    barrier = pltpu.get_barrier_semaphore()
    for peer in peers:
        pl.semaphore_signal(barrier, inc=1, device_id=peer, device_id_type=MESH)
    count = len(peers)
    if everyone is not None:

        def call(step, carry):
            peer = dict(seq=lax.rem(everyone.index + step, everyone.size))
            pl.semaphore_signal(barrier, inc=1, device_id=peer, device_id_type=MESH)
            return carry

        lax.fori_loop(1, everyone.size, call, 0)
        count += everyone.size - 1
    pl.semaphore_wait(barrier, count)


def remote(src, dst, send, recv, device):
    return pltpu.make_async_remote_copy(
        src_ref=src, dst_ref=dst, send_sem=send, recv_sem=recv, device_id=device, device_id_type=MESH
    )


def send(src, dst, send_sem, recv_sem, device):
    copy = remote(src, dst, send_sem, recv_sem, device)
    copy.start()
    return copy


class Total:
    def __init__(self, group, keep, buffers):
        self.group = group
        self.keep = keep
        self.pair_out, self.pair_in, self.out, self.into, self.sems = buffers
        self.pairs = {}
        self.fars = {}
        self.arriving = {}
        self.arrived = set()

    @staticmethod
    def scratch(width):
        return [pltpu.VMEM((CHUNKS, HALF, width), LOW)] * 4 + [pltpu.SemaphoreType.DMA((4, CHUNKS))]

    def give(self, chunk, part, count=1, by_rows=False):
        own, other = self.group.split(part, count, by_rows)
        place = pl.ds(chunk, count)
        self.keep[place] = own
        self.pair_out[place] = other.astype(LOW)
        self.pairs[chunk] = send(
            self.pair_out.at[place],
            self.pair_in.at[place],
            self.sems.at[0, chunk],
            self.sems.at[1, chunk],
            self.group.pair,
        )
        self.arriving.update({chunk + step: chunk for step in range(count)})

    def pair_sum(self, chunk, count=1):
        given = self.arriving[chunk]
        if given not in self.arrived:
            self.arrived.add(given)
            self.pairs[given].wait_recv()
        place = pl.ds(chunk, count)
        return self.keep[place] + self.pair_in[place].astype(FULL)

    def swap(self, chunk, count=1):
        place = pl.ds(chunk, count)
        self.out[place] = self.pair_sum(chunk, count).astype(LOW)
        self.fars[chunk] = send(
            self.out.at[place],
            self.into.at[place],
            self.sems.at[2, chunk],
            self.sems.at[3, chunk],
            self.group.partner,
        )

    def swap_half(self):
        for chunk in range(0, CHUNKS, 2):
            self.out[chunk : chunk + 2] = self.pair_sum(chunk, 2).astype(LOW)
        self.fars[0] = send(
            self.out.at[pl.ds(2 - 2 * self.group.high, 2)],
            self.into.at[pl.ds(0, 2)],
            self.sems.at[2, 0],
            self.sems.at[3, 0],
            self.group.partner,
        )

    def take(self, chunk, count=1):
        self.fars[chunk].wait_recv()
        place = pl.ds(chunk, count)
        return self.out[place].astype(FULL) + self.into[place].astype(FULL)

    def take_half(self):
        self.fars[0].wait_recv()
        return self.out[pl.ds(2 * self.group.high, 2)].astype(FULL) + self.into[0:2].astype(FULL)

    def close(self):
        for copy in list(self.pairs.values()) + list(self.fars.values()):
            copy.wait_send()


class Share:
    def __init__(self, group, full, sems, place):
        self.group = group
        self.full = full
        self.sems = sems
        self.place = place
        self.copies = {}

    def give(self, chunk, value, count=1):
        rows = self.place(self.full, chunk, count)
        rows[...] = value
        self.copies[chunk] = send(
            rows, rows, self.sems.at[0, chunk], self.sems.at[1, chunk], self.group.pair
        )

    def await_other(self, chunk):
        self.copies[chunk].wait_recv()

    def close(self):
        for copy in self.copies.values():
            copy.wait_send()


def share_sems():
    return pltpu.SemaphoreType.DMA((2, CHUNKS))


def relay(first, second, share, enter, work, count=1, order=None, between=lambda: None):
    starts = order or list(range(0, CHUNKS, count))
    for step in range(len(starts) + 1):
        if step < len(starts):
            share.give(starts[step], enter(starts[step], first.take(starts[step], count)), count)
        if step > 1:
            second.swap(starts[step - 2], count)
        if step > 0:
            chunk = starts[step - 1]
            share.await_other(chunk)
            second.give(chunk, work(chunk), count)
        between()
    second.swap(starts[-1], count)


class Later:
    def __init__(self, source, target, sem):
        self.copy = pltpu.make_async_copy(source, target, sem)
        self.copy.start()
        self.target = target
        self.waiting = True

    def __call__(self):
        if self.waiting:
            self.copy.wait()
            self.waiting = False
        return self.target


class Saved:
    def __init__(self, ref, target, sem):
        self.ref = ref
        self.target = target
        self.sem = sem
        self.copy = None

    def store(self):
        self.copy = pltpu.make_async_copy(self.ref, self.target, self.sem)
        self.copy.start()


class Scatter:
    def __init__(self, line, base, give, got, sems, first=0):
        self.line = line
        self.ready, self.base = base
        self.give = give
        self.got = got
        self.sems = sems
        self.first = first

    @staticmethod
    def blocks(size, width):
        return [pltpu.VMEM((size >> (at + 1), width, BLOCK), LOW) for at in range(int(math.log2(size)))]

    @staticmethod
    def signals(size):
        return [pltpu.SemaphoreType.DMA((2, size >> (at + 1))) for at in range(int(math.log2(size)))]

    def part(self, relative, upto):
        total = self.base(self.line.flip(relative))
        for at in range(upto):
            total = total + self.got[at][relative // 2 ** (at + 1)].astype(FULL)
        return total

    def copy(self, at, index):
        return remote(
            self.give[at].at[index],
            self.got[at].at[index],
            self.sems[at].at[0, index],
            self.sems[at].at[1, index],
            dict(seq=self.line.flip(2**at)),
        )

    def each(self, at, body):
        def step(index, carry):
            body(index)
            return carry

        lax.fori_loop(0, self.line.size >> (at + 1), step, 0)

    def start(self, at):
        self.ready()
        if at > self.first:
            self.arrive(at - 1)

        def body(index):
            self.give[at][index] = self.part(2**at * (2 * index + 1), at).astype(self.give[at].dtype)
            self.copy(at, index).start()

        self.each(at, body)

    def arrive(self, at):
        self.each(at, lambda index: self.copy(at, index).wait_recv())

    def finish(self, out=None):
        self.arrive(len(self.got) - 1)
        found = self.part(0, len(self.got))
        if out is None:
            return found
        out[...] = found

    def sent(self, upto=None):
        for at in range(self.first, len(self.sems) if upto is None else upto):
            self.each(at, lambda index, at=at: self.copy(at, index).wait_send())


def product(left, right):
    def base(block):
        columns = pl.ds(pl.multiple_of(block * BLOCK, BLOCK), BLOCK)
        return plain(right()[...], flat(left()[:, :, :, columns]))

    def ready():
        left()
        right()

    return ready, base


def norm_apply(values, gain):
    inverse = lax.rsqrt(jnp.mean(values * values, axis=-1, keepdims=True) + EPS)
    return (values * inverse * gain).astype(LOW)


def norm_back(grad, values, gain):
    inverse = lax.rsqrt(jnp.mean(values * values, axis=-1, keepdims=True) + EPS)
    scaled = values * inverse
    d_scaled = grad * gain
    d_values = inverse * (d_scaled - scaled * jnp.mean(d_scaled * scaled, axis=-1, keepdims=True))
    return d_values, jnp.sum(grad * scaled, axis=0, keepdims=True)


def gate_forward(gate, up_val):
    return gate * up_val / (1.0 + jnp.exp(-gate))


def gate_backward(d_hidden, gate, up_val):
    sigma = 1.0 / (1.0 + jnp.exp(-gate))
    return d_hidden * up_val * sigma * (1.0 + gate * (1.0 - sigma)), d_hidden * gate * sigma


def segment_of(lengths, positions):
    end = 0
    found = jnp.zeros_like(positions)
    for index in range(lengths.shape[0]):
        end = end + lengths[index]
        found = found + jnp.where(positions >= end, 1, 0)
    return found


def ramp(shape, axis, first):
    return lax.broadcasted_iota(jnp.int32, shape, axis) + first


def same(left, right):
    return jnp.where(left == right, 1.0, 0.0)


def feature_tables():
    choice = np.zeros((2, FEAT, FEATS), np.float32)
    rows = np.zeros((8, FEATS), np.float32)
    for index, pair in enumerate(PAIRS):
        for side, entry in enumerate(pair):
            if entry < FEAT:
                choice[side, entry, index] = 1.0
            else:
                rows[side, index] = 1.0
        rows[2, index] = 0.5**0.5 if pair[0] == pair[1] and pair[0] < FEAT else 1.0
    return jnp.asarray(choice, LOW), jnp.asarray(rows, FULL)


class Taylor:
    def __init__(self, line, k, query, key, value):
        self.line = line
        self.k = k
        self.query = query
        self.key = key
        self.value = value
        self.rows = query.shape[0]
        self.count = self.rows // BLOCK
        self.heads = value.shape[1] // HEAD
        start = line.index * self.rows
        self.start = start
        column = segment_of(k.lengths, ramp((self.rows, 1), 0, start))
        last = segment_of(k.lengths, ramp((1, 1), 0, start + self.rows - 1))
        before = segment_of(k.lengths, ramp((1, 1), 0, start - 1))
        self.last = last
        self.before = before
        self.segments = column
        self.across = segment_of(k.lengths, ramp((1, self.rows), 1, start))
        self.tail = same(column, last)
        self.carried = same(column, before)
        self.lane = ramp((1, self.heads * HEAD), 1, 0) // HEAD

    def half(self, array, head, upto=None, only=None):
        first, last = (0, upto or self.count) if only is None else (only, only + 1)
        return array[first * BLOCK : last * BLOCK, head * FEAT : (head + 1) * FEAT] * jnp.asarray(0.5, LOW)

    def factors(self, half):
        rows = self.k.feature_rows
        left = plain(half, self.k.feature_choice[0]) + rows[0:1]
        right = plain(half, self.k.feature_choice[1]) + rows[1:2]
        return left, right

    def features(self, array, head):
        left, right = self.factors(self.half(array, head))
        return left * right * self.k.feature_rows[2:3]

    def features_back(self, grad, array, head):
        left, right = self.factors(self.half(array, head))
        weighted = grad * self.k.feature_rows[2:3]
        return through((weighted * right).astype(LOW), self.k.feature_choice[0]) + through(
            (weighted * left).astype(LOW), self.k.feature_choice[1]
        )

    def of_head(self, head, array):
        return jnp.where(self.lane == head, array, jnp.zeros_like(array))

    def mask(self, block):
        upto = (block + 1) * BLOCK
        rows = ramp((BLOCK, 1), 0, block * BLOCK)
        allowed = (ramp((1, upto), 1, 0) <= rows) & (
            self.across[:, :upto] == self.segments[block * BLOCK : upto]
        )
        return jnp.where(allowed, 1.0, 0.0)

    def send_state(self, forward):
        k, line = self.k, self.line

        def step(other, carry):
            @pl.when((other > line.index) if forward else (other < line.index))
            def _():
                self.state_copy(other).start()

            return carry

        lax.fori_loop(0, line.size, step, 0)

    def state_copy(self, other):
        k = self.k
        return remote(
            k.state_own,
            k.state_slots.at[self.line.index],
            k.state_sems.at[0, other],
            k.state_sems.at[1, self.line.index],
            dict(seq=other),
        )

    def state_arrival(self, other):
        k = self.k
        return remote(
            k.state_own,
            k.state_slots.at[other],
            k.state_sems.at[0, other],
            k.state_sems.at[1, other],
            dict(seq=other),
        )

    def take_state(self, total, forward):
        k, line = self.k, self.line
        total[...] = jnp.zeros_like(total)

        def step(other, carry):
            @pl.when((other < line.index) if forward else (other > line.index))
            def _():
                self.state_arrival(other).wait_recv()
                if forward:
                    edge = segment_of(k.lengths, ramp((1, 1), 0, (other + 1) * self.rows - 1))
                    weight = same(edge, self.before)
                else:
                    edge = segment_of(k.lengths, ramp((1, 1), 0, other * self.rows - 1))
                    weight = same(edge, self.last)
                total[...] += weight * k.state_slots[other].astype(FULL)

            return carry

        lax.fori_loop(0, line.size, step, 0)

    def close(self, forward):
        line = self.line

        def step(other, carry):
            @pl.when((other > line.index) if forward else (other < line.index))
            def _():
                self.state_copy(other).wait_send()

            return carry

        lax.fori_loop(0, line.size, step, 0)

    @staticmethod
    def scratch(size, cols):
        shape = (FEATS + NORM_ROWS, cols)
        return dict(
            state_own=pltpu.VMEM(shape, LOW),
            state_build=pltpu.VMEM(shape, FULL),
            state_slots=pltpu.VMEM((size,) + shape, LOW),
            state_sems=pltpu.SemaphoreType.DMA((2, size)),
        )

    def forward(self):
        k = self.k
        value = self.value[...]
        build = k.state_build
        build[...] = jnp.zeros_like(build)
        state = jnp.zeros((FEATS, value.shape[1]), FULL)
        for head in range(self.heads):
            feats = self.features(self.key, head) * self.tail
            state = state + self.of_head(head, inner(feats.astype(LOW), value))
            build[FEATS + head : FEATS + head + 1, :FEATS] = jnp.sum(feats, axis=0, keepdims=True)
        build[:FEATS] = state
        k.state_own[...] = build[...].astype(LOW)
        self.send_state(True)
        for block in range(self.count):
            allowed = self.mask(block)
            rows = slice(block * BLOCK, (block + 1) * BLOCK)
            for head in range(self.heads):
                places = slice(head * HEAD, (head + 1) * HEAD)
                score = through(self.half(self.query, head, only=block), self.half(self.key, head, block + 1))
                score = allowed * (1.0 + score + 0.5 * score * score)
                k.mixed[rows, places] = plain(score.astype(LOW), value[: (block + 1) * BLOCK, places])
                k.inverse[rows, places] = jnp.broadcast_to(jnp.sum(score, axis=1, keepdims=True), (BLOCK, HEAD))
        self.take_state(k.carry, True)
        state = k.carry[:FEATS].astype(LOW)
        numerator = jnp.zeros((self.rows, value.shape[1]), FULL)
        totals = jnp.zeros((self.rows, value.shape[1]), FULL)
        for head in range(self.heads):
            feats = self.features(self.query, head)
            numerator = numerator + self.of_head(head, plain(feats.astype(LOW), state))
            norm = k.carry[FEATS + head : FEATS + head + 1, :FEATS]
            totals = totals + self.of_head(head, jnp.sum(feats * norm, axis=1, keepdims=True) + jnp.zeros_like(totals))
        inverse = 1.0 / (k.inverse[...] + self.carried * totals)
        mixed = (k.mixed[...] + self.carried * numerator) * inverse
        k.inverse[...] = inverse
        k.mixed[...] = mixed
        k.mixed_low[...] = mixed.astype(LOW)
        k.mixed_turned[...] = mixed.T.astype(LOW)

    def backward(self, d_mixed):
        k = self.k
        value = self.value[...]
        d_out = d_mixed[...].astype(FULL)
        d_numer = d_out * k.inverse[...]
        d_low = d_numer.astype(LOW)
        product = d_numer * k.mixed[...]
        d_totals = [
            -jnp.sum(product[:, head * HEAD : (head + 1) * HEAD], axis=1, keepdims=True) for head in range(self.heads)
        ]
        build = k.state_build
        build[...] = jnp.zeros_like(build)
        state = jnp.zeros((FEATS, value.shape[1]), FULL)
        for head in range(self.heads):
            feats = self.features(self.query, head) * self.carried
            state = state + self.of_head(head, inner(feats.astype(LOW), d_low))
            build[FEATS + head : FEATS + head + 1, :FEATS] = jnp.sum(feats * d_totals[head], axis=0, keepdims=True)
        build[:FEATS] = state
        k.state_own[...] = build[...].astype(LOW)
        self.send_state(False)
        yield
        carry = k.carry[:FEATS].astype(LOW)
        k.d_key_acc[...] = jnp.zeros_like(k.d_key_acc)
        k.d_value_acc[...] = jnp.zeros_like(k.d_value_acc)
        for head in range(self.heads):
            norm = k.carry[FEATS + head : FEATS + head + 1, :FEATS]
            d_feats = self.carried * (through(self.of_head(head, d_low), carry) + d_totals[head] * norm)
            k.d_query_acc[:, head * FEAT : (head + 1) * FEAT] = self.features_back(d_feats, self.query, head)
        for block in range(self.count):
            allowed = self.mask(block)
            upto = (block + 1) * BLOCK
            rows = slice(block * BLOCK, upto)
            for head in range(self.heads):
                places = slice(head * HEAD, (head + 1) * HEAD)
                narrow = slice(head * FEAT, (head + 1) * FEAT)
                query = self.half(self.query, head, only=block)
                key = self.half(self.key, head, block + 1)
                score = through(query, key)
                d_rows = d_low[rows, places]
                d_score = through(d_rows, value[:upto, places]) + d_totals[head][rows]
                d_score = (allowed * d_score * (1.0 + score)).astype(LOW)
                score = (allowed * (1.0 + score + 0.5 * score * score)).astype(LOW)
                k.d_query_acc[rows, narrow] += plain(d_score, key)
                k.d_key_acc[:upto, narrow] += inner(d_score, query)
                k.d_value_acc[:upto, places] += inner(score, d_rows)
            yield
        self.take_state(k.grad_carry, False)
        carry = k.grad_carry[:FEATS].astype(LOW)
        for head in range(self.heads):
            norm = k.grad_carry[FEATS + head : FEATS + head + 1, :FEATS]
            d_feats = self.tail * (through(self.of_head(head, value), carry) + norm)
            k.d_key_acc[:, head * FEAT : (head + 1) * FEAT] += self.features_back(d_feats, self.key, head)
            feats = self.features(self.key, head).astype(LOW)
            k.d_value_acc[...] += self.of_head(head, self.tail * plain(feats, carry))


def window_mask(k, line, block, rows):
    span = BLOCK + WINDOW
    first = line.index * rows + block * BLOCK
    query = ramp((BLOCK, 1), 0, first)
    key = ramp((1, span), 1, first - WINDOW)
    return (
        (key <= query)
        & (key > query - WINDOW)
        & (key >= 0)
        & (segment_of(k.lengths, key) == segment_of(k.lengths, query))
    )


def window_weights(query, key, allowed):
    score = jnp.where(allowed, through(query, key) * HEAD**-0.5, FLOOR_SCORE)
    weight = jnp.exp(score - jnp.max(score, axis=1, keepdims=True))
    return weight / jnp.sum(weight, axis=1, keepdims=True)


def window_forward(k, line, block):
    own = slice(block * BLOCK, (block + 1) * BLOCK)
    allowed = window_mask(k, line, block, k.query2.shape[0])
    span = slice(block * BLOCK, (block + 1) * BLOCK + WINDOW)
    outs = []
    for head in range(k.keys.shape[1] // HEAD):
        places = slice(head * HEAD, (head + 1) * HEAD)
        weight = window_weights(k.query2[own, places], k.keys[span, places], allowed)
        outs.append(plain(weight.astype(LOW), k.values[span, places]))
    whole = jnp.concatenate(outs, axis=1)
    k.window_low[own] = whole.astype(LOW)
    k.window_turned[:, own] = whole.T.astype(LOW)


def window_backward(k, line, block):
    own = slice(block * BLOCK, (block + 1) * BLOCK)
    allowed = window_mask(k, line, block, k.query2.shape[0])
    span = slice(block * BLOCK, (block + 1) * BLOCK + WINDOW)
    grads = []
    for head in range(k.keys.shape[1] // HEAD):
        places = slice(head * HEAD, (head + 1) * HEAD)
        query = k.query2[own, places]
        key = k.keys[span, places]
        d_out = k.d_window[own, places]
        weight = window_weights(query, key, allowed)
        d_weight = through(d_out, k.values[span, places])
        d_score = weight * (d_weight - jnp.sum(weight * d_weight, axis=1, keepdims=True)) * HEAD**-0.5
        d_score = d_score.astype(LOW)
        grads.append(plain(d_score, key))
        k.d_keys[span, places] += inner(d_score, query)
        k.d_values[span, places] += inner(weight.astype(LOW), d_out)
    whole = jnp.concatenate(grads, axis=1)
    k.d_query2[own] = whole.astype(LOW)
    k.d_turned2[: whole.shape[1], own] = whole.T.astype(LOW)


def first_kernel(k, size):
    group, line = Group(), Line(size)
    greet([group.pair, group.partner], line)
    width = k.inputs.shape[1]
    rows = k.query.shape[0]
    cols = k.value.shape[1]
    total_a, total_b, total_c = (Total(group, k.keep, k.totals[i]) for i in range(3))
    closing = [total_a, total_b]

    def offer(step, block, raw):
        values = raw.astype(FULL)
        k.start[pl.ds(2 * (block // 2), 2)] = values.reshape(2, HALF, width)
        k.normed_one[block] = norm_apply(values, k.gains[0:1]).reshape(2, HALF, width)
        place = k.normed_one.at[block]
        copy = send(place, place, k.near_sems.at[0, step], k.near_sems.at[1, step], group.pair)
        copy.wait_recv()
        return copy

    def project_one(pair):
        normed = flat(k.normed_one[pl.ds(2 * pair, 2)])
        place = pl.ds(pl.multiple_of(pair * 2 * BLOCK, 2 * BLOCK), 2 * BLOCK)
        k.key[place] = through(normed, k.w_key_one[...]).astype(LOW)
        k.value[place] = plain(normed, k.w_value_one[...]).astype(LOW)
        k.query[place] = through(normed, k.w_query_one[...]).astype(LOW)

    def offer_cot(step, half, raw):
        place = k.cot.at[pl.ds(2 * half, 2), group.low]
        place[...] = raw.reshape(2, HALF, width)
        return send(place, place, k.near_sems.at[0, 2 + step], k.near_sems.at[1, 2 + step], group.pair)

    far = send(k.inputs, k.rows_in, k.far_sems.at[0, 0], k.far_sems.at[1, 0], group.partner)
    copies = [offer(0, group.index, k.inputs[...])]
    project_one(group.high)
    far.wait_recv()
    far_cot = send(k.cotangent, k.cot_in, k.far_sems.at[0, 1], k.far_sems.at[1, 1], group.partner)
    copies.append(offer(1, lax.rem(group.index + 2, 4), k.rows_in[...]))
    project_one(1 - group.high)
    copies.append(offer_cot(0, group.high, k.cotangent[...]))
    taylor = Taylor(line, k, k.query, k.key, k.value)
    taylor.forward()
    for item in (k.start, k.normed_one, k.query, k.key, k.value, k.mixed, k.inverse, k.mixed_turned, k.carry):
        k.store(item)
    far_cot.wait_recv()
    copies.append(offer_cot(1, 1 - group.high, k.cot_in[...]))

    share = Share(group, k.normed_two, k.share_sems.at[0], group.own_chunks)
    closing.append(share)

    def enter_mlp(chunk, total):
        middle = k.start[chunk : chunk + 1] + total
        k.middle[chunk : chunk + 1] = middle
        return norm_apply(middle, k.gains[1:2])

    def mlp_one(chunk):
        normed = flat(k.normed_two[chunk])
        gate = through(normed, k.w_gate_one()[...])
        up_val = through(normed, k.w_up_one()[...])
        k.gate[chunk] = gate.astype(LOW).reshape(k.gate.shape[1:])
        k.up[chunk] = up_val.astype(LOW).reshape(k.up.shape[1:])
        hidden = gate_forward(gate, up_val)
        k.hidden_one[:, chunk * BLOCK : (chunk + 1) * BLOCK] = hidden.T.astype(LOW)
        return plain(hidden.astype(LOW), k.w_down_one()[...])

    for chunk in range(0, CHUNKS, 2):
        part = plain(chunk_rows(k.mixed_low, chunk, 2), k.w_out_one()[...])
        total_a.give(chunk, part, 2, by_rows=True)
    for chunk in range(CHUNKS):
        total_a.swap(chunk)
    relay(total_a, total_b, share, enter_mlp, mlp_one)
    for item in (k.middle, k.normed_two, k.gate, k.up, k.hidden_one):
        k.store(item)

    share = Share(group, k.normed_three, k.share_sems.at[1], group.own_rows)
    closing.append(share)

    def project_two(chunk):
        normed = chunk_rows(k.normed_three, chunk)
        put_rows(k.keys, chunk, plain(normed, k.w_key_two()[...]).astype(LOW), WINDOW)
        put_rows(k.values, chunk, plain(normed, k.w_value_two()[...]).astype(LOW), WINDOW)
        put_rows(k.query2, chunk, plain(normed, k.w_query_two()[...]).astype(LOW))

    for step in range(CHUNKS + 1):
        if step < CHUNKS:
            after = k.middle[step : step + 1] + total_b.take(step)
            k.after[step : step + 1] = after
            share.give(step, norm_apply(after, k.gains[2:3]))
        if step > 0:
            share.await_other(step - 1)
            project_two(step - 1)
        if step == 2:
            window_forward(k, line, 1)
    k.store(k.after)
    k.store(k.normed_three)
    halo = Halo(k, 0, (k.keys, k.values), slice(rows, rows + WINDOW), line.after)
    for item in closing:
        item.close()
    closing = [halo]
    total_a, total_b = (Total(group, k.keep, k.totals[i]) for i in range(2))
    closing += [total_a, total_b, total_c]
    order = [2, 3, 0, 1]
    for chunk in (2, 0):
        if chunk == 2:
            window_forward(k, line, 2)
            window_forward(k, line, 3)
        else:
            for index, target in enumerate((k.keys, k.values)):
                target[:WINDOW] = halo.take(index)
            window_forward(k, line, 0)
        part = plain(chunk_rows(k.window_low, chunk, 2), k.w_out_two()[...])
        total_a.give(chunk, part, 2, by_rows=True)
        total_a.swap(chunk)
        total_a.swap(chunk + 1)
    k.store(k.window_turned)

    gain = k.gains[3:4]
    share = Share(group, k.normed_four, k.share_sems.at[2], group.own_chunks)
    closing.append(share)
    for copy in copies[2:]:
        copy.wait_recv()
    k.store(k.cot)

    def enter_turn(chunk, total):
        middle = k.after[chunk : chunk + 1] + total
        k.middle_two[chunk : chunk + 1] = middle
        return norm_apply(middle, gain)

    def mlp_two(chunk):
        normed = flat(k.normed_four[chunk])
        gate = through(normed, k.w_gate_two()[...])
        up_val = through(normed, k.w_up_two()[...])
        d_hidden = through(flat(k.cot[chunk]), k.w_down_two()[...])
        d_gate, d_up = gate_backward(d_hidden, gate, up_val)
        back = plain(d_gate.astype(LOW), k.w_gate_two()[...]) + plain(d_up.astype(LOW), k.w_up_two()[...])
        hidden = gate_forward(gate, up_val)
        k.hidden[chunk] = hidden.astype(LOW).reshape(k.hidden.shape[1:])
        columns = slice(chunk * BLOCK, (chunk + 1) * BLOCK)
        k.hidden_two[:, columns] = hidden.T.astype(LOW)
        k.d_gate_two[:, columns] = d_gate.T.astype(LOW)
        k.d_up_two[:, columns] = d_up.T.astype(LOW)
        return back

    relay(total_a, total_b, share, enter_turn, mlp_two, order=order)
    for item in (k.normed_four, k.hidden_two, k.d_gate_two, k.d_up_two):
        k.store(item)
    if k.scatter:
        gate_sum = Scatter(
            line, product(lambda: k.normed_four, lambda: k.d_gate_two), k.give, [k.gate_two_got], [k.give_sems]
        )
        gate_sum.start(0)
    for chunk in range(0, CHUNKS, 2):
        total_c.give(chunk, plain(flat(k.hidden[chunk : chunk + 2]), k.w_down_two()[...]), 2)
    total_c.swap_half()

    share = Share(group, k.grad_three, k.share_sems.at[3], group.own_rows)
    closing.append(share)
    k.gain_grad[...] = jnp.zeros_like(k.gain_grad)
    k.d_keys[...] = jnp.zeros_like(k.d_keys)
    k.d_values[...] = jnp.zeros_like(k.d_values)
    for step in range(CHUNKS + 1):
        if step < CHUNKS:
            chunk = order[step]
            d_values, d_gain = norm_back(total_b.take(chunk)[0], k.middle_two[chunk], gain)
            grad = k.cot[chunk, pl.ds(group.low, 1)].astype(FULL) + d_values[None]
            k.grad[chunk : chunk + 1] = grad
            k.gain_grad[...] += group.mine(chunk) * d_gain
            share.give(chunk, grad.astype(LOW))
        if step > 0:
            chunk = order[step - 1]
            share.await_other(chunk)
            put_rows(k.d_window, chunk, through(chunk_rows(k.grad_three, chunk), k.w_out_two()[...]).astype(LOW))
        if step == 2:
            window_backward(k, line, 2)
            window_backward(k, line, 3)
    k.store(k.grad)
    k.store(k.grad_three)
    window_backward(k, line, 0)
    halo = Halo(k, 1, (k.d_keys, k.d_values), slice(0, WINDOW), line.before)
    closing.append(halo)
    window_backward(k, line, 1)
    k.store(k.d_query2)
    k.result[...] = (flat(k.middle_two[pl.ds(2 * group.high, 2)]) + flat(total_c.take_half())).astype(LOW)
    for index, (target, out) in enumerate(((k.d_keys, k.d_key2), (k.d_values, k.d_value2))):
        target[rows : rows + WINDOW] += halo.take(index).astype(FULL)
        whole = target[WINDOW:]
        out[...] = whole.astype(LOW)
        k.store(out)
        k.d_turned2[(index + 1) * cols : (index + 2) * cols] = whole.T.astype(LOW)
    k.store(k.d_turned2)
    if k.scatter:
        gate_sum.arrive(0)
        gate_sum.sent()
    for item in closing:
        item.close()
    for copy in [far, far_cot] + copies:
        copy.wait_send()
    taylor.close(True)


class Halo:
    def __init__(self, k, turn, sources, rows, peer):
        self.into = k.halo_in.at[turn]
        self.copies = []
        for index, source in enumerate(sources):
            k.halo_out[turn, index] = source[rows].astype(LOW)
            self.copies.append(
                send(
                    k.halo_out.at[turn, index],
                    k.halo_in.at[turn, index],
                    k.halo_sems.at[0, turn, index],
                    k.halo_sems.at[1, turn, index],
                    peer,
                )
            )

    def take(self, index):
        self.copies[index].wait_recv()
        return self.into[index]

    def close(self):
        for copy in self.copies:
            copy.wait_send()


def second_kernel(k, size):
    group, line = Group(), Line(size)
    greet([group.pair, group.partner], line)
    width = k.gains.shape[1]
    total_a, total_b = (Total(group, k.keep, k.totals[i]) for i in range(2))
    share_mlp = Share(group, k.grad_two, k.share_sems.at[0], group.own_chunks)
    share = Share(group, k.grad_one, k.share_sems.at[1], group.own_rows)
    taylor = Taylor(line, k, k.query(), k.key(), k.value())
    background = []
    sums = {}

    def tick(count=1):
        for _ in range(count):
            if background:
                background.pop(0)()

    def normed_rows(chunk):
        return (
            through(chunk_rows(k.d_query2(), chunk, 2), k.w_query_two()[...])
            + through(chunk_rows(k.d_key2(), chunk, 2), k.w_key_two()[...])
            + through(chunk_rows(k.d_value2(), chunk, 2), k.w_value_two()[...])
        )

    def back(chunk, total, values, gain, row):
        d_values, d_gain = norm_back(flat(total), flat(values[chunk : chunk + 2]), gain)
        k.gain_rows[row : row + 1] += group.mine(chunk) * d_gain
        return d_values.reshape(2, HALF, width)

    def enter_mlp(chunk, total):
        grad = k.grad()[chunk : chunk + 2] + back(chunk, total, k.after(), k.gains[2:3], 2)
        k.grad()[chunk : chunk + 2] = grad
        return grad.astype(LOW)

    def mlp(chunk):
        d_hidden = through(flat(k.grad_two[chunk : chunk + 2]), k.w_down_one()[...])
        gate = flat(k.gate()[chunk : chunk + 2]).astype(FULL)
        up_val = flat(k.up()[chunk : chunk + 2]).astype(FULL)
        d_gate, d_up = gate_backward(d_hidden, gate, up_val)
        columns = slice(chunk * BLOCK, (chunk + 2) * BLOCK)
        k.d_gate_one[:, columns] = d_gate.T.astype(LOW)
        k.d_up_one[:, columns] = d_up.T.astype(LOW)
        return plain(d_gate.astype(LOW), k.w_gate_one()[...]) + plain(d_up.astype(LOW), k.w_up_one()[...])

    if k.scatter:
        levels = len(k.sems)

        def add(name, left, right, give, got, sems, first=0):
            sums[name] = Scatter(line, product(left, right), give, got, sems, first)

        at = lambda index: [sem.at[index] for sem in k.sems]
        add(1, k.normed_four, k.d_up_two, k.unit_gives[1], k.unit_gots[1], at(1))
        add(2, k.cot, k.hidden_two, k.unit_gives[2], k.unit_gots[2], at(2))
        add(3, k.grad_three, k.window_turned, k.out_gives[0], k.out_gots[0], at(3))
        add(4, k.normed_three, k.d_turned2, k.three_two_gives, k.three_two_gots, at(4))
        add(5, k.normed_two, lambda: k.d_gate_one, k.unit_gives[0], k.unit_gots[3], at(5))
        add(6, k.normed_two, lambda: k.d_up_one, k.unit_gives[1], k.unit_gots[4], at(6))
        add(7, lambda: k.grad_two, k.hidden_one, k.unit_gives[2], k.unit_gots[5], at(7))
        add(8, k.normed_one, lambda: k.d_turned, k.three_one_gives, k.three_one_gots, at(8))
        add(9, lambda: k.grad_one, k.mixed_turned, k.out_gives[1], k.out_gots[1], at(9))
        sums[10] = Scatter(line, (lambda: None, lambda block: k.gain_rows[:, columns_of(block)]), k.gain_gives, k.gain_gots, at(10))
        before = {5: 0, 6: 1, 7: 2}

        def start(name, level):
            def step():
                if level == 0 and name in before:
                    sums[before[name]].sent()
                sums[name].start(level)

            return step

        def finish(name):
            def step():
                sums[name].finish(k.sums[name])
                k.store(k.sums[name])

            return step

        background += [
            start(0, 2),
            start(2, 0),
            start(1, 1),
            finish(0),
            start(1, 2),
            start(3, 0),
            start(4, 0),
            start(2, 1),
            finish(1),
            start(2, 2),
            start(5, 0),
            start(3, 1),
            start(4, 1),
        ]

    k.gain_rows[...] = jnp.zeros_like(k.gain_rows)
    k.gain_rows[3:4] = k.gain_in[...]
    for chunk in range(0, CHUNKS, 2):
        total_a.give(chunk, normed_rows(chunk), 2, by_rows=True)
    for chunk in range(0, CHUNKS, 2):
        total_a.swap(chunk, 2)
    if k.scatter:
        sums[1].start(0)
        add(0, k.normed_four, k.d_gate_two, k.unit_gives[0], [k.gate_two_got()] + k.unit_gots[0][1:], at(0), 1)
        sums[0].start(1)
    relay(total_a, total_b, share_mlp, enter_mlp, mlp, 2, between=tick)
    for step in range(3):
        if step < 2:
            chunk = 2 * step
            grad = k.grad()[chunk : chunk + 2] + back(chunk, total_b.take(chunk, 2), k.middle(), k.gains[1:2], 1)
            k.grad()[chunk : chunk + 2] = grad
            share.give(chunk, grad.astype(LOW), 2)
        if step > 0:
            chunk = 2 * step - 2
            share.await_other(chunk)
            rows = through(chunk_rows(k.grad_one, chunk, 2), k.w_out_one()[...])
            k.d_mixed[chunk * BLOCK : (chunk + 2) * BLOCK] = rows.astype(LOW)
        tick()

    total_a.close()
    total_c = Total(group, k.keep, k.totals[0])
    k.mixed, k.inverse, k.carry = k.mixed(), k.inverse(), k.carry()
    for _ in taylor.backward(k.d_mixed):
        tick()
    d_query = 0.5 * k.d_query_acc[...]
    d_key = 0.5 * k.d_key_acc[...]
    d_value = k.d_value_acc[...]
    small, cols = d_query.shape[1], d_value.shape[1]
    k.d_query_low[...] = d_query.astype(LOW)
    k.d_key_low[...] = d_key.astype(LOW)
    k.d_value_low[...] = d_value.astype(LOW)
    k.d_turned[:small] = d_query.T.astype(LOW)
    k.d_turned[small : 2 * small] = d_key.T.astype(LOW)
    k.d_turned[2 * small : 2 * small + cols] = d_value.T.astype(LOW)
    for chunk in range(0, CHUNKS, 2):
        part = (
            plain(chunk_rows(k.d_query_low, chunk, 2), k.w_query_one()[...])
            + plain(chunk_rows(k.d_key_low, chunk, 2), k.w_key_one()[...])
            + through(chunk_rows(k.d_value_low, chunk, 2), k.w_value_one()[...])
        )
        total_c.give(chunk, part, 2, by_rows=True)
    total_c.swap_half()
    tick()
    half = pl.ds(2 * group.high, 2)
    d_values, d_gain = norm_back(flat(total_c.take_half()), flat(k.start()[half]), k.gains[0:1])
    k.input_grad[...] = flat(k.grad()[half]) + d_values
    k.gain_rows[0:1] = d_gain

    if k.scatter:
        background += [
            start(6, 0),
            start(10, 0),
            finish(2),
            start(3, 2),
            start(10, 1),
            start(4, 2),
            start(5, 1),
            start(7, 0),
            start(10, 2),
            finish(3),
            finish(4),
            start(5, 2),
            start(6, 1),
            start(8, 0),
            start(9, 0),
            finish(5),
            start(6, 2),
            start(7, 1),
            finish(6),
            start(7, 2),
            start(8, 1),
            start(9, 1),
            finish(7),
            start(8, 2),
            start(9, 2),
        ]
        tick(13)
        copies = []
        k.gain_sum[0] = sums[10].finish()
        for index, peer in enumerate((group.pair, group.partner)):
            copy = send(
                k.gain_sum.at[index], k.gain_in_sum.at[index], k.gain_sems.at[0, index], k.gain_sems.at[1, index], peer
            )
            tick(4)
            copy.wait_recv()
            k.gain_sum[index + 1] = k.gain_sum[index] + k.gain_in_sum[index]
            copies.append(copy)
        total = k.gain_sum[2]
        share_of = BLOCK // 4
        found = jnp.zeros((8, share_of), FULL)
        for index in range(4):
            found = found + jnp.where(group.index == index, 1.0, 0.0) * total[:, index * share_of : (index + 1) * share_of]
        k.gain_out[...] = found
        while background:
            tick()
        finish(8)()
        finish(9)()
        for name in (3, 4, 5, 6, 7, 8, 9, 10):
            sums[name].sent()
        for copy in copies:
            copy.wait_send()
    else:
        for item in (k.d_gate_one, k.d_up_one, k.d_turned, k.grad_one, k.grad_two):
            k.store(item)
        k.gain_out[...] = k.gain_rows[...]
    for item in (total_b, total_c, share_mlp, share):
        item.close()
    taylor.close(False)


def columns_of(block):
    return pl.ds(pl.multiple_of(block * BLOCK, BLOCK), BLOCK)


def finish_kernel(k, small, cols):
    k.result[...] = k.result_in[...]
    k.input_grad[...] = k.input_grad_in[...]
    k.gains[...] = k.gains_in[0:4]
    for source, target in zip(k.sums, k.same):
        target[...] = source[...]
    for source, targets in zip(k.threes, k.turned):
        first = 0
        for target in targets:
            if target.shape[1] == BLOCK:
                target[...] = source[first : first + target.shape[0]]
                first += target.shape[0]
            else:
                target[...] = source[first : first + target.shape[1]].T
                first += target.shape[1]


def run_kernel(kernel, ident, ins, outs, scratch, flops, later=None, saved=None, apart=None, scalars=None, extra=None):
    later, saved, apart, scalars = (found or {} for found in (later, saved, apart, scalars))
    is_shape = lambda leaf: isinstance(leaf, tuple) and isinstance(leaf[0], tuple)

    def buffer(array):
        return pltpu.VMEM(array.shape, array.dtype)

    def held(tree):
        return jax.tree.map(lambda leaf: pltpu.VMEM(*leaf), tree, is_leaf=is_shape)

    def sems(tree):
        return jax.tree.map(lambda leaf: pltpu.SemaphoreType.DMA(()), tree, is_leaf=is_shape)

    arguments = (ins, later, scalars)
    results = (outs, saved, apart)
    own = (
        scratch,
        jax.tree.map(buffer, later),
        jax.tree.map(lambda leaf: pltpu.SemaphoreType.DMA(()), later),
        held(saved),
        sems(saved),
    )
    flat_in, tree_in = jax.tree.flatten(arguments)
    flat_out, tree_out = jax.tree.flatten(results, is_leaf=is_shape)
    flat_own, tree_own = jax.tree.flatten(own)

    def body(*refs):
        in_refs = jax.tree.unflatten(tree_in, refs[: len(flat_in)])
        out_refs = jax.tree.unflatten(tree_out, refs[len(flat_in) : len(flat_in) + len(flat_out)])
        own_refs = jax.tree.unflatten(tree_own, refs[len(flat_in) + len(flat_out) :])
        k = types.SimpleNamespace(**(extra or {}))
        for tree in (in_refs[0], in_refs[2], out_refs[0], out_refs[2], own_refs[0], own_refs[3]):
            k.__dict__.update(tree)
        waited = []
        for name, source in in_refs[1].items():
            waited.append(Later(source, own_refs[1][name], own_refs[2][name]))
            setattr(k, name, waited[-1])
        saves = []
        for name in saved:
            parts = zip(*(jax.tree.leaves(tree[name]) for tree in (own_refs[3], out_refs[1], own_refs[4])))
            saves += [Saved(*part) for part in parts]

        def store(ref):
            for item in saves:
                if item.ref is ref:
                    item.store()

        k.store = store
        kernel(k)
        for item in waited:
            item()
        for item in saves:
            if item.copy is None:
                item.store()
            item.copy.wait()

    shapes = [jax.ShapeDtypeStruct(*leaf) for leaf in flat_out]
    moved = sum(a.size * a.dtype.itemsize for a in flat_in) + sum(
        math.prod(a.shape) * a.dtype.itemsize for a in shapes
    )
    there = pl.BlockSpec(memory_space=pl.ANY)
    here = pl.BlockSpec(memory_space=pltpu.VMEM)
    scalar = pl.BlockSpec(memory_space=pltpu.SMEM)

    def places(trees, kinds):
        return [kind for tree, kind in zip(trees, kinds) for _ in jax.tree.leaves(tree, is_leaf=is_shape)]

    found = pl.pallas_call(
        body,
        out_shape=shapes,
        in_specs=places(arguments, (here, there, scalar)),
        out_specs=places(results, (here, there, there)),
        scratch_shapes=flat_own,
        cost_estimate=pl.CostEstimate(flops=flops, bytes_accessed=moved, transcendentals=0),
        compiler_params=pltpu.CompilerParams(
            collective_id=ident, has_side_effects=ident is not None, vmem_limit_bytes=VMEM_BYTES
        ),
    )(*flat_in)
    found = jax.tree.unflatten(tree_out, found)
    return types.SimpleNamespace(**found[0], **found[1], **found[2])


def halve(array, axis):
    size = lax.axis_size(axis)
    index = lax.axis_index(axis)
    pieces = array.reshape((size, array.shape[0] // size) + array.shape[1:])
    distance = 1
    while distance < size:
        bit = (index // distance) % 2
        pairs = pieces.reshape((pieces.shape[0] // 2, 2) + pieces.shape[1:])
        keep = lax.dynamic_index_in_dim(pairs, bit, axis=1, keepdims=False)
        give = lax.dynamic_index_in_dim(pairs, 1 - bit, axis=1, keepdims=False)
        got = lax.ppermute(give, axis, [(i, i ^ distance) for i in range(size)])
        pieces = (keep.astype(FULL) + got.astype(FULL)).astype(array.dtype)
        distance *= 2
    return pieces[0]


def scatter_plain(left, right):
    return halve(inner(flat(left), right.T).astype(LOW), "seq").astype(FULL).T


def scatter_gains(gains):
    count = lax.axis_size("tensor")
    n_seq = lax.axis_size("seq")
    shaped = gains.reshape(4, n_seq, -1).transpose(1, 0, 2)
    mine = halve(shaped, "seq")[0]
    distance = 1
    while distance < count:
        mine = mine + lax.ppermute(mine, "tensor", [(i, i ^ distance) for i in range(count)])
        distance *= 2
    width = mine.shape[-1] // count
    return lax.dynamic_slice_in_dim(mine, lax.axis_index("tensor") * width, width, 1)


def on_device(
    inputs,
    cotangent,
    seq_lengths,
    norm_gains,
    query_one,
    key_one,
    value_one,
    out_one,
    gate_one,
    up_one,
    down_one,
    query_two,
    key_two,
    value_two,
    out_two,
    gate_two,
    up_two,
    down_two,
):
    rows, width = inputs.shape
    size = lax.axis_size("seq")
    stretch = 4 * rows
    units = gate_one.shape[1]
    cols = value_one.shape[1]
    small = query_one.shape[1]
    scatter = width // size == BLOCK
    count = int(math.log2(size))
    wide = ((4, 2, HALF, width), LOW)
    own = ((CHUNKS, HALF, width), FULL)
    heads = ((stretch, cols), LOW)
    heads_full = ((stretch, cols), FULL)
    narrow = ((stretch, small), LOW)
    unit_rows = ((CHUNKS, 2, HALF, units), LOW)
    turned_units = ((units, stretch), LOW)
    turned_cols = ((cols, stretch), LOW)
    state = ((FEATS + NORM_ROWS, cols), FULL)
    padded = ((stretch + WINDOW, cols), LOW)
    one_flops = 2 * stretch * width
    blocks = functools.partial(Scatter.blocks, size)
    choice, feature_rows = feature_tables()
    tables = dict(feature_choice=choice, feature_rows=feature_rows)
    tensor_sums = dict(
        keep=pltpu.VMEM(*own),
        share_sems=pltpu.SemaphoreType.DMA((4, 2, CHUNKS)),
    )
    got = ((size // 2, units, BLOCK), LOW)
    ahead = run_kernel(
        functools.partial(first_kernel, size=size),
        0,
        dict(
            gains=norm_gains,
            inputs=inputs,
            cotangent=cotangent,
            w_query_one=query_one.T,
            w_key_one=key_one.T,
            w_value_one=value_one,
            **tables,
        ),
        dict(result=((rows, width), LOW), gain_grad=((1, width), FULL)),
        dict(
            **tensor_sums,
            **Taylor.scratch(size, cols),
            totals=[Total.scratch(width) for _ in range(3)],
            rows_in=pltpu.VMEM((rows, width), LOW),
            cot_in=pltpu.VMEM((rows, width), LOW),
            near_sems=pltpu.SemaphoreType.DMA((2, 4)),
            far_sems=pltpu.SemaphoreType.DMA((2, 2)),
            mixed_low=pltpu.VMEM(*heads),
            query2=pltpu.VMEM(*heads),
            keys=pltpu.VMEM(*padded),
            values=pltpu.VMEM(*padded),
            window_low=pltpu.VMEM(*heads),
            d_window=pltpu.VMEM(*heads),
            d_keys=pltpu.VMEM(padded[0], FULL),
            d_values=pltpu.VMEM(padded[0], FULL),
            middle_two=pltpu.VMEM(*own),
            hidden=pltpu.VMEM(*unit_rows),
            halo_out=pltpu.VMEM((2, 2, WINDOW, cols), LOW),
            halo_in=pltpu.VMEM((2, 2, WINDOW, cols), LOW),
            halo_sems=pltpu.SemaphoreType.DMA((2, 2, 2)),
            give=[pltpu.VMEM(*got)],
            give_sems=pltpu.SemaphoreType.DMA((2, size // 2)),
        ),
        one_flops * (8 * cols + 9 * units),
        later=dict(
            w_out_one=out_one,
            w_gate_one=gate_one.T,
            w_up_one=up_one.T,
            w_down_one=down_one,
            w_key_two=key_two,
            w_value_two=value_two,
            w_query_two=query_two,
            w_out_two=out_two,
            w_gate_two=gate_two.T,
            w_up_two=up_two.T,
            w_down_two=down_two,
        ),
        saved=dict(
            start=own,
            middle=own,
            after=own,
            grad=own,
            normed_one=wide,
            normed_two=wide,
            normed_three=wide,
            normed_four=wide,
            cot=wide,
            grad_three=wide,
            query=narrow,
            key=narrow,
            value=heads,
            mixed=heads_full,
            inverse=heads_full,
            mixed_turned=turned_cols,
            carry=state,
            gate=unit_rows,
            up=unit_rows,
            hidden_one=turned_units,
            hidden_two=turned_units,
            d_gate_two=turned_units,
            d_up_two=turned_units,
            window_turned=turned_cols,
            d_query2=heads,
            d_key2=heads,
            d_value2=heads,
            d_turned2=((3 * cols, stretch), LOW),
        ),
        apart=dict(gate_two_got=got) if scatter else None,
        scalars=dict(lengths=seq_lengths),
        extra=dict(scatter=scatter),
    )
    widths = [units, units, units, cols, 3 * cols, units, units, units, 2 * small + cols, cols]
    carried = dict(
        d_query2=ahead.d_query2,
        d_key2=ahead.d_key2,
        d_value2=ahead.d_value2,
        w_query_two=query_two,
        w_key_two=key_two,
        w_value_two=value_two,
    )
    summed = dict(
        normed_four=ahead.normed_four,
        d_up_two=ahead.d_up_two,
        d_gate_two=ahead.d_gate_two,
        cot=ahead.cot,
        hidden_two=ahead.hidden_two,
        grad_three=ahead.grad_three,
        window_turned=ahead.window_turned,
        normed_three=ahead.normed_three,
        d_turned2=ahead.d_turned2,
        normed_two=ahead.normed_two,
        hidden_one=ahead.hidden_one,
        normed_one=ahead.normed_one,
        mixed_turned=ahead.mixed_turned,
    )
    chain = dict(
        after=ahead.after,
        grad=ahead.grad,
        w_down_one=down_one,
        gate=ahead.gate,
        up=ahead.up,
        w_gate_one=gate_one.T,
        w_up_one=up_one.T,
        middle=ahead.middle,
        w_out_one=out_one,
        query=ahead.query,
        key=ahead.key,
        value=ahead.value,
        mixed=ahead.mixed,
        inverse=ahead.inverse,
        carry=ahead.carry,
        w_query_one=query_one.T,
        w_key_one=key_one.T,
        w_value_one=value_one,
        start=ahead.start,
    )
    early = ("normed_four", "d_up_two", "d_gate_two")
    made = dict(
        d_gate_one=turned_units,
        d_up_one=turned_units,
        d_turned=((2 * small + cols, stretch), LOW),
        grad_two=wide,
        grad_one=wide,
    )
    if scatter:
        gain_blocks = [pltpu.VMEM((size >> (at + 1), 8, BLOCK), FULL) for at in range(count)]
        buffers = dict(
            unit_gives=[blocks(units) for _ in range(3)],
            unit_gots=[blocks(units) for _ in range(6)],
            out_gives=[blocks(cols) for _ in range(2)],
            out_gots=[blocks(cols) for _ in range(2)],
            three_two_gives=blocks(3 * cols),
            three_two_gots=blocks(3 * cols),
            three_one_gives=blocks(2 * small + cols),
            three_one_gots=blocks(2 * small + cols),
            gain_gives=gain_blocks,
            gain_gots=gain_blocks,
            sems=[pltpu.SemaphoreType.DMA((11, 2, size >> (at + 1))) for at in range(count)],
            gain_sum=pltpu.VMEM((3, 8, BLOCK), FULL),
            gain_in_sum=pltpu.VMEM((2, 8, BLOCK), FULL),
            gain_sems=pltpu.SemaphoreType.DMA((2, 2)),
            **{name: pltpu.VMEM(*leaf) for name, leaf in made.items()},
        )
        buffers["unit_gots"][0][0] = None
        inputs_later = dict(
            **carried,
            **{name: summed[name] for name in early},
            gate_two_got=ahead.gate_two_got,
            **chain,
            **{name: array for name, array in summed.items() if name not in early},
        )
        kept = dict(sums=[((wide_, BLOCK), FULL) for wide_ in widths])
    else:
        buffers = {}
        inputs_later = dict(**carried, **chain)
        kept = made
    behind = run_kernel(
        functools.partial(second_kernel, size=size),
        1,
        dict(gains=norm_gains, gain_in=ahead.gain_grad, **tables),
        dict(input_grad=((rows, width), FULL), gain_out=((8, BLOCK // 4 if scatter else width), FULL)),
        dict(
            **tensor_sums,
            **Taylor.scratch(size, cols),
            totals=[Total.scratch(width) for _ in range(2)],
            d_mixed=pltpu.VMEM(*heads),
            gain_rows=pltpu.VMEM((8, width), FULL),
            grad_carry=pltpu.VMEM(*state),
            d_query_acc=pltpu.VMEM((stretch, small), FULL),
            d_key_acc=pltpu.VMEM((stretch, small), FULL),
            d_value_acc=pltpu.VMEM((stretch, cols), FULL),
            d_query_low=pltpu.VMEM(*narrow),
            d_key_low=pltpu.VMEM(*narrow),
            d_value_low=pltpu.VMEM(*heads),
            **buffers,
        ),
        one_flops * (6 * cols + 9 * units),
        later=inputs_later,
        saved=kept,
        scalars=dict(lengths=seq_lengths),
        extra=dict(scatter=scatter),
    )
    if not scatter:
        sums = [
            scatter_plain(left, right)
            for left, right in (
                (ahead.normed_four, ahead.d_gate_two),
                (ahead.normed_four, ahead.d_up_two),
                (ahead.cot, ahead.hidden_two),
                (ahead.grad_three, ahead.window_turned),
                (ahead.normed_three, ahead.d_turned2),
                (ahead.normed_two, behind.d_gate_one),
                (ahead.normed_two, behind.d_up_one),
                (behind.grad_two, ahead.hidden_one),
                (ahead.normed_one, behind.d_turned),
                (behind.grad_one, ahead.mixed_turned),
            )
        ]
        gains = scatter_gains(behind.gain_out[:4])
        three_one, three_two = sums[8], sums[4]
        return (
            (ahead.result, behind.input_grad, gains)
            + (three_one[:small].T, three_one[small : 2 * small].T, three_one[2 * small :].T)
            + (sums[9], sums[5].T, sums[6].T, sums[7])
            + tuple(three_two[first : first + cols].T for first in range(0, 3 * cols, cols))
            + (sums[3], sums[0].T, sums[1].T, sums[2])
        )
    block = ((BLOCK, cols), FULL)
    unit = ((units, BLOCK), FULL)
    done = run_kernel(
        functools.partial(finish_kernel, small=small, cols=cols),
        None,
        dict(
            result_in=ahead.result,
            input_grad_in=behind.input_grad,
            gains_in=behind.gain_out,
            sums=[behind.sums[name] for name in (0, 1, 2, 3, 5, 6, 7, 9)],
            threes=[behind.sums[8], behind.sums[4]],
        ),
        dict(
            result=((rows, width), LOW),
            input_grad=((rows, width), FULL),
            gains=((4, BLOCK // 4), FULL),
            same=[unit, unit, unit, ((cols, BLOCK), FULL), unit, unit, unit, ((cols, BLOCK), FULL)],
            turned=[[((small, BLOCK), FULL), ((small, BLOCK), FULL), block], [block, block, block]],
        ),
        {},
        stretch,
    )
    same, turned = done.same, done.turned
    return (
        (done.result, done.input_grad, done.gains)
        + (turned[0][0].T, turned[0][1].T, turned[0][2])
        + (same[7], same[4].T, same[5].T, same[6])
        + tuple(turned[1])
        + (same[3], same[0].T, same[1].T, same[2])
    )


def solution(mesh):
    both = P(("seq", "tensor"), None)
    split = P(None, "tensor")
    stacked = P("tensor", None)
    columns_out = P("seq", "tensor")
    rows_out = P("tensor", "seq")
    layer_in = (split, split, split, stacked, split, split, stacked)
    layer_out = (columns_out, columns_out, columns_out, rows_out, columns_out, columns_out, rows_out)
    return jax.shard_map(
        on_device,
        mesh=mesh,
        in_specs=(both, both, P(), P()) + layer_in + layer_in,
        out_specs=(both, both, P(None, ("seq", "tensor"))) + layer_out + layer_out,
        check_vma=False,
    )
```

time: 1770 us -> 289 us (0.16)
  waiting for transfers between devices: 1430 us -> 0 us
  Pallas kernels: 0 us -> 284 us
  matrix products: 159 us -> 0 us
  blocking collectives: 61.4 us -> 0 us
  other arithmetic: 45.4 us -> 0 us
  local copies, waits for them, and re-layouts: 39.3 us -> 0 us
    reduce_scatter x22 -> x0, waiting for transfers between devices: 1180 us -> none  [the longest x8 196 us: collect(): lax.psum_scatter(product(jnp.int32(0), rows * lax.axis_size('tensor')).as...]
    pallas_call x0 -> x3, Pallas kernels: none -> 284 us  [run_kernel(): pl.pallas_call(body, out_shape=shapes, in_specs=places(arguments, (here,...]
    dot_general x67 -> x0, matrix products: 159 us -> none  [the longest x14 34.7 us: inner(): lax.dot_general(left, right, SAME_DIMS, preferred_element_type=jnp.float32)]
    all_gather x10 -> x0, waiting for transfers between devices: 150 us -> none  [the longest x8 123 us: spread(): return lax.all_gather(part, 'tensor', axis=0, tiled=True)]
    unnamed x34 -> x0, waiting for transfers between devices: 92.7 us -> none
    all_gather x2 -> x0, blocking collectives: 61.4 us -> none  [the longest x1 31 us: pass_states(): lax.all_gather(shortened(norm_sum), 'seq', axis=0, tiled=True)]
    unnamed x232 -> x0, local copies, waits for them, and re-layouts: 19.1 us -> none
  transfers between devices with their start and end apart: 37 -> 0, of which waited for: 33 -> 0; matrix products, arithmetic and copies ran while one was open for 6% -> 0% of each run, Pallas kernels for 0% -> 0%
where the time goes in v2:
time: 289 us; the launch traced here: 285 us
  Pallas kernels  284 us (98%)
    pallas_call x3, Pallas kernels, run_kernel(): pl.pallas_call(body, out_shape=shapes, in_specs=places(arguments, (here,...  284 us

profile of v2, /device:TPU:0, one launch (start us, length us, event | category | flops | bytes accessed | tf_op | source)
XLA Modules:
  0.0 285.3 jit_solution(11813607242873906277)
XLA Ops:
  0.7 108.1 %shard_map.323 = (f32[1,1024]{1,0:T(1,128)}, bf16[128,1024]{1,0:T(8,128)(2,1)}, f32[4,64,1024]{2,1,0:T(8,128)}, f32[176,256]{1,0:T(8,128)}, bf16[4,2,64,1024]{3,...) custom-call(bf16[128,1024]{1,0:T(8,128)(2,1)} %refs_0_.2, ...), custom_call_target="tpu_custom_call" | custom-call | flops 8640266240 | bytes 31820832 | tf_op jit(solution)/shard_map/pallas_call | solution.py:1199
  108.7 172.3 %shard_map.324 = (f32[8,32]{1,0:T(8,128)}, f32[128,1024]{1,0:T(8,128)}, f32[688,128]{1,0:T(8,128)}, f32[688,128]{1,0:T(8,128)}, f32[688,128]{1,0:T(8,128)}, /*in...) custom-call(bf16[2,16,160]{2,1,0:T(8,128)(2,1)} %constant.4.clone.re, ...), custom_call_target="tpu_custom_call" | custom-call | flops 8103395328 | bytes 29773856 | tf_op jit(solution)/shard_map/pallas_call | solution.py:1199
  281.0 4.0 %shard_map.325 = (f32[4,32]{1,0:T(4,128)}, f32[128,1024]{1,0:T(8,128)}, bf16[128,1024]{1,0:T(8,128)(2,1)}, f32[688,128]{1,0:T(8,128)}, f32[688,128]{1,0:T(8,128)...) custom-call(f32[8,32]{1,0:T(8,128)} %get-tuple-element.107.refs_0_, ...), custom_call_target="tpu_custom_call" | custom-call | flops 512 | bytes 7505408 | tf_op jit(solution)/shard_map/pallas_call | solution.py:1199

commit v3 on v2

--- a/solution.py
+++ b/solution.py
@@ -271,27 +271,18 @@
 
 
 class Scatter:
-    def __init__(self, line, base, give, got, sems, first=0):
+    def __init__(self, line, source, order, give, got, sems, begun=0):
         self.line = line
-        self.ready, self.base = base
+        self.ready, self.base = source
+        self.order = order
         self.give = give
         self.got = got
         self.sems = sems
-        self.first = first
+        self.begun = begun
 
     @staticmethod
     def blocks(size, width):
         return [pltpu.VMEM((size >> (at + 1), width, BLOCK), LOW) for at in range(int(math.log2(size)))]
-
-    @staticmethod
-    def signals(size):
-        return [pltpu.SemaphoreType.DMA((2, size >> (at + 1))) for at in range(int(math.log2(size)))]
-
-    def part(self, relative, upto):
-        total = self.base(self.line.flip(relative))
-        for at in range(upto):
-            total = total + self.got[at][relative // 2 ** (at + 1)].astype(FULL)
-        return total
 
     def copy(self, at, index):
         return remote(
@@ -299,52 +290,58 @@
             self.got[at].at[index],
             self.sems[at].at[0, index],
             self.sems[at].at[1, index],
-            dict(seq=self.line.flip(2**at)),
+            dict(seq=self.line.flip(self.order[at])),
         )
 
-    def each(self, at, body):
-        def step(index, carry):
-            body(index)
-            return carry
-
-        lax.fori_loop(0, self.line.size >> (at + 1), step, 0)
+    def part(self, place, upto):
+        relative = sum(bit for at, bit in enumerate(self.order) if place >> at & 1)
+        total = self.base(self.line.flip(relative))
+        for at in range(upto):
+            index = place >> (at + 1)
+            if at >= self.begun:
+                self.copy(at, index).wait_recv()
+            total = total + self.got[at][index].astype(FULL)
+        return total
+
+    def places(self, at):
+        return sorted(range(self.line.size >> (at + 1)), key=lambda index: (index & -index) or self.line.size)
 
     def start(self, at):
         self.ready()
-        if at > self.first:
-            self.arrive(at - 1)
-
-        def body(index):
+        for index in self.places(at):
             self.give[at][index] = self.part(2**at * (2 * index + 1), at).astype(self.give[at].dtype)
             self.copy(at, index).start()
 
-        self.each(at, body)
+    def finish(self):
+        return self.part(0, len(self.order))
 
     def arrive(self, at):
-        self.each(at, lambda index: self.copy(at, index).wait_recv())
-
-    def finish(self, out=None):
-        self.arrive(len(self.got) - 1)
-        found = self.part(0, len(self.got))
-        if out is None:
-            return found
-        out[...] = found
-
-    def sent(self, upto=None):
-        for at in range(self.first, len(self.sems) if upto is None else upto):
-            self.each(at, lambda index, at=at: self.copy(at, index).wait_send())
+        for index in self.places(at):
+            self.copy(at, index).wait_recv()
+
+    def sent(self):
+        for at in range(self.begun, len(self.sems)):
+            for index in self.places(at):
+                self.copy(at, index).wait_send()
+
+
+def columns_of(block):
+    return pl.ds(pl.multiple_of(block * BLOCK, BLOCK), BLOCK)
 
 
 def product(left, right):
     def base(block):
-        columns = pl.ds(pl.multiple_of(block * BLOCK, BLOCK), BLOCK)
-        return plain(right()[...], flat(left()[:, :, :, columns]))
+        return plain(held(right)[...], flat(held(left)[:, :, :, columns_of(block)]))
 
     def ready():
-        left()
-        right()
+        held(left)
+        held(right)
 
     return ready, base
+
+
+def held(item):
+    return item() if isinstance(item, Later) else item
 
 
 def norm_apply(values, gain):
@@ -528,7 +525,7 @@
             state_sems=pltpu.SemaphoreType.DMA((2, size)),
         )
 
-    def forward(self):
+    def forward(self, meanwhile):
         k = self.k
         value = self.value[...]
         build = k.state_build
@@ -550,6 +547,7 @@
                 score = allowed * (1.0 + score + 0.5 * score * score)
                 k.mixed[rows, places] = plain(score.astype(LOW), value[: (block + 1) * BLOCK, places])
                 k.inverse[rows, places] = jnp.broadcast_to(jnp.sum(score, axis=1, keepdims=True), (BLOCK, HEAD))
+        meanwhile()
         self.take_state(k.carry, True)
         state = k.carry[:FEATS].astype(LOW)
         numerator = jnp.zeros((self.rows, value.shape[1]), FULL)
@@ -677,6 +675,11 @@
     k.d_turned2[: whole.shape[1], own] = whole.T.astype(LOW)
 
 
+X_FIRST, Z_FIRST = (1, 2, 4), (2, 4, 1)
+ORDERS = [X_FIRST, X_FIRST, Z_FIRST, Z_FIRST, X_FIRST, X_FIRST, X_FIRST, X_FIRST, X_FIRST, X_FIRST, X_FIRST]
+PLAN = [[(2, 1), (4, 0), (0, 1), (1, 0), (4, 1)], [(0, 2), (3, 0)], [], [(4, 2)], [(5, 0), (1, 1)], [], [(2, 2)], [], [(3, 1), (5, 1)], [(1, 2)], [(7, 0), (5, 2), (7, 1), (6, 0)], [], [(7, 2), (1, 3), (6, 1)], [(10, 0)], [(8, 0), (7, 3), (9, 0), (6, 2), (4, 3), (5, 3), (3, 2), (10, 1), (8, 1), (10, 2), (9, 1), (8, 2), (11, 0), (11, 1), (2, 3), (3, 3), (11, 2), (9, 2), (0, 3), (6, 3), (8, 3), (9, 3)]]
+
+
 def first_kernel(k, size):
     group, line = Group(), Line(size)
     greet([group.pair, group.partner], line)
@@ -716,11 +719,20 @@
     project_one(1 - group.high)
     copies.append(offer_cot(0, group.high, k.cotangent[...]))
     taylor = Taylor(line, k, k.query, k.key, k.value)
-    taylor.forward()
+
+    def turn_ahead():
+        far_cot.wait_recv()
+        copies.append(offer_cot(1, 1 - group.high, k.cot_in[...]))
+        for copy in copies[2:]:
+            copy.wait_recv()
+        k.store(k.cot)
+        for chunk in range(0, CHUNKS, 2):
+            found = through(flat(k.cot[chunk : chunk + 2]), k.w_down_two()[...])
+            k.d_hidden[chunk : chunk + 2] = found.reshape(2, 2 * HALF, -1)
+
+    taylor.forward(turn_ahead)
     for item in (k.start, k.normed_one, k.query, k.key, k.value, k.mixed, k.inverse, k.mixed_turned, k.carry):
         k.store(item)
-    far_cot.wait_recv()
-    copies.append(offer_cot(1, 1 - group.high, k.cot_in[...]))
 
     share = Share(group, k.normed_two, k.share_sems.at[0], group.own_chunks)
     closing.append(share)
@@ -740,12 +752,13 @@
         k.hidden_one[:, chunk * BLOCK : (chunk + 1) * BLOCK] = hidden.T.astype(LOW)
         return plain(hidden.astype(LOW), k.w_down_one()[...])
 
-    for chunk in range(0, CHUNKS, 2):
+    order = [2, 3, 0, 1]
+    for chunk in (2, 0):
         part = plain(chunk_rows(k.mixed_low, chunk, 2), k.w_out_one()[...])
         total_a.give(chunk, part, 2, by_rows=True)
-    for chunk in range(CHUNKS):
+    for chunk in order:
         total_a.swap(chunk)
-    relay(total_a, total_b, share, enter_mlp, mlp_one)
+    relay(total_a, total_b, share, enter_mlp, mlp_one, order=order)
     for item in (k.middle, k.normed_two, k.gate, k.up, k.hidden_one):
         k.store(item)
 
@@ -760,43 +773,37 @@
 
     for step in range(CHUNKS + 1):
         if step < CHUNKS:
-            after = k.middle[step : step + 1] + total_b.take(step)
-            k.after[step : step + 1] = after
-            share.give(step, norm_apply(after, k.gains[2:3]))
+            chunk = order[step]
+            after = k.middle[chunk : chunk + 1] + total_b.take(chunk)
+            k.after[chunk : chunk + 1] = after
+            share.give(chunk, norm_apply(after, k.gains[2:3]))
         if step > 0:
-            share.await_other(step - 1)
-            project_two(step - 1)
+            chunk = order[step - 1]
+            share.await_other(chunk)
+            project_two(chunk)
         if step == 2:
-            window_forward(k, line, 1)
-    k.store(k.after)
-    k.store(k.normed_three)
-    halo = Halo(k, 0, (k.keys, k.values), slice(rows, rows + WINDOW), line.after)
+            halo = Halo(k, 0, (k.keys, k.values), slice(rows, rows + WINDOW), line.after)
     for item in closing:
         item.close()
     closing = [halo]
     total_a, total_b = (Total(group, k.keep, k.totals[i]) for i in range(2))
     closing += [total_a, total_b, total_c]
-    order = [2, 3, 0, 1]
-    for chunk in (2, 0):
-        if chunk == 2:
-            window_forward(k, line, 2)
-            window_forward(k, line, 3)
-        else:
-            for index, target in enumerate((k.keys, k.values)):
-                target[:WINDOW] = halo.take(index)
-            window_forward(k, line, 0)
+    for index, target in enumerate((k.keys, k.values)):
+        target[:WINDOW] = halo.take(index)
+    for chunk in (0, 2):
+        window_forward(k, line, chunk)
+        window_forward(k, line, chunk + 1)
         part = plain(chunk_rows(k.window_low, chunk, 2), k.w_out_two()[...])
         total_a.give(chunk, part, 2, by_rows=True)
         total_a.swap(chunk)
         total_a.swap(chunk + 1)
+    k.store(k.after)
+    k.store(k.normed_three)
     k.store(k.window_turned)
 
     gain = k.gains[3:4]
     share = Share(group, k.normed_four, k.share_sems.at[2], group.own_chunks)
     closing.append(share)
-    for copy in copies[2:]:
-        copy.wait_recv()
-    k.store(k.cot)
 
     def enter_turn(chunk, total):
         middle = k.after[chunk : chunk + 1] + total
@@ -807,25 +814,35 @@
         normed = flat(k.normed_four[chunk])
         gate = through(normed, k.w_gate_two()[...])
         up_val = through(normed, k.w_up_two()[...])
-        d_hidden = through(flat(k.cot[chunk]), k.w_down_two()[...])
-        d_gate, d_up = gate_backward(d_hidden, gate, up_val)
-        back = plain(d_gate.astype(LOW), k.w_gate_two()[...]) + plain(d_up.astype(LOW), k.w_up_two()[...])
-        hidden = gate_forward(gate, up_val)
-        k.hidden[chunk] = hidden.astype(LOW).reshape(k.hidden.shape[1:])
+        d_gate, d_up = gate_backward(k.d_hidden[chunk], gate, up_val)
+        d_gate, d_up = d_gate.astype(LOW), d_up.astype(LOW)
+        back = plain(d_gate, k.w_gate_two()[...]) + plain(d_up, k.w_up_two()[...])
+        k.gate_two[chunk] = gate
+        k.up_two[chunk] = up_val
+        k.d_gate_low[chunk] = d_gate
+        k.d_up_low[chunk] = d_up
+        return back
+
+    relay(total_a, total_b, share, enter_turn, mlp_two)
+    for chunk in range(CHUNKS):
         columns = slice(chunk * BLOCK, (chunk + 1) * BLOCK)
+        k.d_gate_two[:, columns] = k.d_gate_low[chunk].T
+        k.d_up_two[:, columns] = k.d_up_low[chunk].T
+        hidden = gate_forward(k.gate_two[chunk], k.up_two[chunk])
+        k.hidden[chunk] = hidden.astype(LOW)
         k.hidden_two[:, columns] = hidden.T.astype(LOW)
-        k.d_gate_two[:, columns] = d_gate.T.astype(LOW)
-        k.d_up_two[:, columns] = d_up.T.astype(LOW)
-        return back
-
-    relay(total_a, total_b, share, enter_turn, mlp_two, order=order)
     for item in (k.normed_four, k.hidden_two, k.d_gate_two, k.d_up_two):
         k.store(item)
+    begun = []
     if k.scatter:
-        gate_sum = Scatter(
-            line, product(lambda: k.normed_four, lambda: k.d_gate_two), k.give, [k.gate_two_got], [k.give_sems]
-        )
-        gate_sum.start(0)
+        begun = [
+            Scatter(line, product(left, right), order, [k.gives[i]], [k.begun[i]], [k.give_sems.at[i]])
+            for i, (left, right, order) in enumerate(
+                ((k.normed_four, k.d_gate_two, X_FIRST), (k.cot, k.hidden_two, Z_FIRST))
+            )
+        ]
+    for item in begun:
+        item.start(0)
     for chunk in range(0, CHUNKS, 2):
         total_c.give(chunk, plain(flat(k.hidden[chunk : chunk + 2]), k.w_down_two()[...]), 2)
     total_c.swap_half()
@@ -837,25 +854,25 @@
     k.d_values[...] = jnp.zeros_like(k.d_values)
     for step in range(CHUNKS + 1):
         if step < CHUNKS:
-            chunk = order[step]
+            chunk = step
             d_values, d_gain = norm_back(total_b.take(chunk)[0], k.middle_two[chunk], gain)
             grad = k.cot[chunk, pl.ds(group.low, 1)].astype(FULL) + d_values[None]
             k.grad[chunk : chunk + 1] = grad
             k.gain_grad[...] += group.mine(chunk) * d_gain
             share.give(chunk, grad.astype(LOW))
         if step > 0:
-            chunk = order[step - 1]
+            chunk = step - 1
             share.await_other(chunk)
             put_rows(k.d_window, chunk, through(chunk_rows(k.grad_three, chunk), k.w_out_two()[...]).astype(LOW))
         if step == 2:
-            window_backward(k, line, 2)
-            window_backward(k, line, 3)
+            window_backward(k, line, 0)
+            halo = Halo(k, 1, (k.d_keys, k.d_values), slice(0, WINDOW), line.before)
+            closing.append(halo)
+            window_backward(k, line, 1)
     k.store(k.grad)
     k.store(k.grad_three)
-    window_backward(k, line, 0)
-    halo = Halo(k, 1, (k.d_keys, k.d_values), slice(0, WINDOW), line.before)
-    closing.append(halo)
-    window_backward(k, line, 1)
+    window_backward(k, line, 2)
+    window_backward(k, line, 3)
     k.store(k.d_query2)
     k.result[...] = (flat(k.middle_two[pl.ds(2 * group.high, 2)]) + flat(total_c.take_half())).astype(LOW)
     for index, (target, out) in enumerate(((k.d_keys, k.d_key2), (k.d_values, k.d_value2))):
@@ -865,9 +882,9 @@
         k.store(out)
         k.d_turned2[(index + 1) * cols : (index + 2) * cols] = whole.T.astype(LOW)
     k.store(k.d_turned2)
-    if k.scatter:
-        gate_sum.arrive(0)
-        gate_sum.sent()
+    for item in begun:
+        item.arrive(0)
+        item.sent()
     for item in closing:
         item.close()
     for copy in [far, far_cot] + copies:
@@ -908,13 +925,13 @@
     share_mlp = Share(group, k.grad_two, k.share_sems.at[0], group.own_chunks)
     share = Share(group, k.grad_one, k.share_sems.at[1], group.own_rows)
     taylor = Taylor(line, k, k.query(), k.key(), k.value())
-    background = []
+    background = list(PLAN)
     sums = {}
 
-    def tick(count=1):
-        for _ in range(count):
-            if background:
-                background.pop(0)()
+    def tick():
+        if k.scatter:
+            for name, level in background.pop(0):
+                act(name, level)
 
     def normed_rows(chunk):
         return (
@@ -944,54 +961,61 @@
         return plain(d_gate.astype(LOW), k.w_gate_one()[...]) + plain(d_up.astype(LOW), k.w_up_one()[...])
 
     if k.scatter:
-        levels = len(k.sems)
-
-        def add(name, left, right, give, got, sems, first=0):
-            sums[name] = Scatter(line, product(left, right), give, got, sems, first)
-
-        at = lambda index: [sem.at[index] for sem in k.sems]
-        add(1, k.normed_four, k.d_up_two, k.unit_gives[1], k.unit_gots[1], at(1))
-        add(2, k.cot, k.hidden_two, k.unit_gives[2], k.unit_gots[2], at(2))
-        add(3, k.grad_three, k.window_turned, k.out_gives[0], k.out_gots[0], at(3))
-        add(4, k.normed_three, k.d_turned2, k.three_two_gives, k.three_two_gots, at(4))
-        add(5, k.normed_two, lambda: k.d_gate_one, k.unit_gives[0], k.unit_gots[3], at(5))
-        add(6, k.normed_two, lambda: k.d_up_one, k.unit_gives[1], k.unit_gots[4], at(6))
-        add(7, lambda: k.grad_two, k.hidden_one, k.unit_gives[2], k.unit_gots[5], at(7))
-        add(8, k.normed_one, lambda: k.d_turned, k.three_one_gives, k.three_one_gots, at(8))
-        add(9, lambda: k.grad_one, k.mixed_turned, k.out_gives[1], k.out_gots[1], at(9))
-        sums[10] = Scatter(line, (lambda: None, lambda block: k.gain_rows[:, columns_of(block)]), k.gain_gives, k.gain_gots, at(10))
+        pieces = [
+            (k.normed_four, k.d_gate_two),
+            (k.normed_four, k.d_up_two),
+            (k.cot, k.hidden_two),
+            (k.grad_three, k.window_turned),
+            (k.normed_three, k.d_turned2),
+            (k.normed_two, k.d_gate_one),
+            (k.normed_two, k.d_up_one),
+            (k.grad_two, k.hidden_one),
+            (k.normed_one, k.d_turned),
+            (k.grad_one, k.mixed_turned),
+        ]
+        sources = [product(left, right) for left, right in pieces]
+        sources.append((lambda: None, lambda block: k.gain_rows[:, columns_of(block)]))
+        begun = {0: 0, 2: 1}
         before = {5: 0, 6: 1, 7: 2}
 
-        def start(name, level):
-            def step():
-                if level == 0 and name in before:
+        gain_copies = []
+
+        def gain_step(step):
+            if step:
+                gain_copies[-1].wait_recv()
+                k.gain_sum[step] = k.gain_sum[step - 1] + k.gain_in_sum[step - 1]
+            else:
+                k.gain_sum[0] = sums[10].finish()
+            if step < 2:
+                signals = k.gain_sems.at[0, step], k.gain_sems.at[1, step]
+                peer = (group.pair, group.partner)[step]
+                gain_copies.append(send(k.gain_sum.at[step], k.gain_in_sum.at[step], *signals, peer))
+                return
+            share_of = BLOCK // 4
+            found = jnp.zeros((8, share_of), FULL)
+            for index in range(4):
+                part = k.gain_sum[2][:, index * share_of : (index + 1) * share_of]
+                found = found + jnp.where(group.index == index, 1.0, 0.0) * part
+            k.gain_out[...] = found
+
+        def act(name, level):
+            if name == 11:
+                return gain_step(level)
+            if name not in sums:
+                got = list(k.gots[name])
+                if name in begun:
+                    got[0] = k.begun[begun[name]]()
+                if name in before:
                     sums[before[name]].sent()
+                sems = [sem.at[name] for sem in k.sems]
+                give = k.gives[before.get(name, name)]
+                order = ORDERS[name]
+                sums[name] = Scatter(line, sources[name], order, give, got, sems, 1 if name in begun else 0)
+            if level < len(ORDERS[name]):
                 sums[name].start(level)
-
-            return step
-
-        def finish(name):
-            def step():
-                sums[name].finish(k.sums[name])
+            else:
+                k.sums[name][...] = sums[name].finish()
                 k.store(k.sums[name])
-
-            return step
-
-        background += [
-            start(0, 2),
-            start(2, 0),
-            start(1, 1),
-            finish(0),
-            start(1, 2),
-            start(3, 0),
-            start(4, 0),
-            start(2, 1),
-            finish(1),
-            start(2, 2),
-            start(5, 0),
-            start(3, 1),
-            start(4, 1),
-        ]
 
     k.gain_rows[...] = jnp.zeros_like(k.gain_rows)
     k.gain_rows[3:4] = k.gain_in[...]
@@ -999,10 +1023,7 @@
         total_a.give(chunk, normed_rows(chunk), 2, by_rows=True)
     for chunk in range(0, CHUNKS, 2):
         total_a.swap(chunk, 2)
-    if k.scatter:
-        sums[1].start(0)
-        add(0, k.normed_four, k.d_gate_two, k.unit_gives[0], [k.gate_two_got()] + k.unit_gots[0][1:], at(0), 1)
-        sums[0].start(1)
+    tick()
     relay(total_a, total_b, share_mlp, enter_mlp, mlp, 2, between=tick)
     for step in range(3):
         if step < 2:
@@ -1046,58 +1067,13 @@
     k.input_grad[...] = flat(k.grad()[half]) + d_values
     k.gain_rows[0:1] = d_gain
 
+    tick()
     if k.scatter:
-        background += [
-            start(6, 0),
-            start(10, 0),
-            finish(2),
-            start(3, 2),
-            start(10, 1),
-            start(4, 2),
-            start(5, 1),
-            start(7, 0),
-            start(10, 2),
-            finish(3),
-            finish(4),
-            start(5, 2),
-            start(6, 1),
-            start(8, 0),
-            start(9, 0),
-            finish(5),
-            start(6, 2),
-            start(7, 1),
-            finish(6),
-            start(7, 2),
-            start(8, 1),
-            start(9, 1),
-            finish(7),
-            start(8, 2),
-            start(9, 2),
-        ]
-        tick(13)
-        copies = []
-        k.gain_sum[0] = sums[10].finish()
-        for index, peer in enumerate((group.pair, group.partner)):
-            copy = send(
-                k.gain_sum.at[index], k.gain_in_sum.at[index], k.gain_sems.at[0, index], k.gain_sems.at[1, index], peer
-            )
-            tick(4)
-            copy.wait_recv()
-            k.gain_sum[index + 1] = k.gain_sum[index] + k.gain_in_sum[index]
-            copies.append(copy)
-        total = k.gain_sum[2]
-        share_of = BLOCK // 4
-        found = jnp.zeros((8, share_of), FULL)
-        for index in range(4):
-            found = found + jnp.where(group.index == index, 1.0, 0.0) * total[:, index * share_of : (index + 1) * share_of]
-        k.gain_out[...] = found
         while background:
             tick()
-        finish(8)()
-        finish(9)()
-        for name in (3, 4, 5, 6, 7, 8, 9, 10):
+        for name in set(sums) - set(before.values()):
             sums[name].sent()
-        for copy in copies:
+        for copy in gain_copies:
             copy.wait_send()
     else:
         for item in (k.d_gate_one, k.d_up_one, k.d_turned, k.grad_one, k.grad_two):
@@ -1106,10 +1082,6 @@
     for item in (total_b, total_c, share_mlp, share):
         item.close()
     taylor.close(False)
-
-
-def columns_of(block):
-    return pl.ds(pl.multiple_of(block * BLOCK, BLOCK), BLOCK)
 
 
 def finish_kernel(k, small, cols):
@@ -1164,8 +1136,10 @@
             k.__dict__.update(tree)
         waited = []
         for name, source in in_refs[1].items():
-            waited.append(Later(source, own_refs[1][name], own_refs[2][name]))
-            setattr(k, name, waited[-1])
+            parts = zip(*(jax.tree.leaves(tree) for tree in (source, own_refs[1][name], own_refs[2][name])))
+            found = [Later(*part) for part in parts]
+            waited += found
+            setattr(k, name, found if isinstance(source, list) else found[0])
         saves = []
         for name in saved:
             parts = zip(*(jax.tree.leaves(tree[name]) for tree in (own_refs[3], out_refs[1], own_refs[4])))
@@ -1183,6 +1157,7 @@
         for item in saves:
             if item.copy is None:
                 item.store()
+        for item in saves:
             item.copy.wait()
 
     shapes = [jax.ShapeDtypeStruct(*leaf) for leaf in flat_out]
@@ -1321,12 +1296,17 @@
             d_keys=pltpu.VMEM(padded[0], FULL),
             d_values=pltpu.VMEM(padded[0], FULL),
             middle_two=pltpu.VMEM(*own),
-            hidden=pltpu.VMEM(*unit_rows),
+            hidden=pltpu.VMEM((CHUNKS, 2 * HALF, units), LOW),
+            d_hidden=pltpu.VMEM((CHUNKS, 2 * HALF, units), FULL),
+            gate_two=pltpu.VMEM((CHUNKS, 2 * HALF, units), FULL),
+            up_two=pltpu.VMEM((CHUNKS, 2 * HALF, units), FULL),
+            d_gate_low=pltpu.VMEM((CHUNKS, 2 * HALF, units), LOW),
+            d_up_low=pltpu.VMEM((CHUNKS, 2 * HALF, units), LOW),
             halo_out=pltpu.VMEM((2, 2, WINDOW, cols), LOW),
             halo_in=pltpu.VMEM((2, 2, WINDOW, cols), LOW),
             halo_sems=pltpu.SemaphoreType.DMA((2, 2, 2)),
-            give=[pltpu.VMEM(*got)],
-            give_sems=pltpu.SemaphoreType.DMA((2, size // 2)),
+            gives=[pltpu.VMEM(*got), pltpu.VMEM(*got)],
+            give_sems=pltpu.SemaphoreType.DMA((2, 2, size // 2)),
         ),
         one_flops * (8 * cols + 9 * units),
         later=dict(
@@ -1372,7 +1352,7 @@
             d_value2=heads,
             d_turned2=((3 * cols, stretch), LOW),
         ),
-        apart=dict(gate_two_got=got) if scatter else None,
+        apart=dict(begun=[got, got]) if scatter else None,
         scalars=dict(lengths=seq_lengths),
         extra=dict(scatter=scatter),
     )
@@ -1432,27 +1412,20 @@
     if scatter:
         gain_blocks = [pltpu.VMEM((size >> (at + 1), 8, BLOCK), FULL) for at in range(count)]
         buffers = dict(
-            unit_gives=[blocks(units) for _ in range(3)],
-            unit_gots=[blocks(units) for _ in range(6)],
-            out_gives=[blocks(cols) for _ in range(2)],
-            out_gots=[blocks(cols) for _ in range(2)],
-            three_two_gives=blocks(3 * cols),
-            three_two_gots=blocks(3 * cols),
-            three_one_gives=blocks(2 * small + cols),
-            three_one_gots=blocks(2 * small + cols),
-            gain_gives=gain_blocks,
-            gain_gots=gain_blocks,
+            gives=[[] if name in (5, 6, 7) else blocks(wide_) for name, wide_ in enumerate(widths)] + [gain_blocks],
+            gots=[blocks(wide_) for wide_ in widths] + [gain_blocks],
             sems=[pltpu.SemaphoreType.DMA((11, 2, size >> (at + 1))) for at in range(count)],
             gain_sum=pltpu.VMEM((3, 8, BLOCK), FULL),
             gain_in_sum=pltpu.VMEM((2, 8, BLOCK), FULL),
             gain_sems=pltpu.SemaphoreType.DMA((2, 2)),
             **{name: pltpu.VMEM(*leaf) for name, leaf in made.items()},
         )
-        buffers["unit_gots"][0][0] = None
+        for name in (0, 2):
+            buffers["gots"][name][0] = None
         inputs_later = dict(
             **carried,
             **{name: summed[name] for name in early},
-            gate_two_got=ahead.gate_two_got,
+            begun=ahead.begun,
             **chain,
             **{name: array for name, array in summed.items() if name not in early},
         )

time: 289 us -> 253 us (0.88)
  Pallas kernels: 284 us -> 247 us
    pallas_call x3, Pallas kernels: 284 us -> 247 us  [run_kernel(): pl.pallas_call(body, out_shape=shapes, in_specs=places(arguments, (here,...]
where the time goes in v3:
time: 253 us; the launch traced here: 248 us
  Pallas kernels  247 us (98%)
    pallas_call x3, Pallas kernels, run_kernel(): pl.pallas_call(body, out_shape=shapes, in_specs=places(arguments, (here,...  247 us

profile of v3, /device:TPU:0, one launch (start us, length us, event | category | flops | bytes accessed | tf_op | source)
XLA Modules:
  0.0 248.1 jit_solution(17349366513369292971)
XLA Ops:
  0.7 112.8 %shard_map.323 = (f32[1,1024]{1,0:T(1,128)}, bf16[128,1024]{1,0:T(8,128)(2,1)}, f32[4,64,1024]{2,1,0:T(8,128)}, f32[176,256]{1,0:T(8,128)}, bf16[4,2,64,1024]{3,...) custom-call(bf16[128,1024]{1,0:T(8,128)(2,1)} %refs_0_.2, ...), custom_call_target="tpu_custom_call" | custom-call | flops 8640266240 | bytes 32525344 | tf_op jit(solution)/shard_map/pallas_call | solution.py:1174
  113.4 130.5 %shard_map.324 = (f32[8,32]{1,0:T(8,128)}, f32[128,1024]{1,0:T(8,128)}, f32[688,128]{1,0:T(8,128)}, f32[688,128]{1,0:T(8,128)}, f32[688,128]{1,0:T(8,128)}, /*in...) custom-call(bf16[2,16,160]{2,1,0:T(8,128)(2,1)} %constant.4.clone.re, ...), custom_call_target="tpu_custom_call" | custom-call | flops 8103395328 | bytes 30478368 | tf_op jit(solution)/shard_map/pallas_call | solution.py:1174
  243.9 4.0 %shard_map.325 = (f32[4,32]{1,0:T(4,128)}, f32[128,1024]{1,0:T(8,128)}, bf16[128,1024]{1,0:T(8,128)(2,1)}, f32[688,128]{1,0:T(8,128)}, f32[688,128]{1,0:T(8,128)...) custom-call(f32[8,32]{1,0:T(8,128)} %get-tuple-element.109.refs_0_, ...), custom_call_target="tpu_custom_call" | custom-call | flops 512 | bytes 7505408 | tf_op jit(solution)/shard_map/pallas_call | solution.py:1174
